TPU v7x, 32 devices: a whole 2x2x4 slice. The times are simulated.
32 devices in a mesh: dp: 4 (over z), seq: 8 (over y, x, core).
Axes of the slice: x: 2, y: 2, z: 4, core: 2. Of those that a mesh axis runs over, the one named last changes fastest.
Arguments:
- block_input: bfloat16 [8, 1024, 1536], P('dp', 'seq'), may hold values from -6 to 6
- cotangent: bfloat16 [8, 1024, 1536], P('dp', 'seq'), may hold values from -6 to 6
- lengths: int32 [8], P('dp'), may hold values from 256 to 1024, as said below
- in_weight: bfloat16 [1536, 6448], P(('dp', 'seq')), may hold values from -0.15625 to 0.15625
- out_weight: bfloat16 [3072, 1536], P(('dp', 'seq')), may hold values from -0.109375 to 0.109375
- norm_gain: bfloat16 [1536], P(('dp', 'seq')), may hold values from 0.5 to 1.5
- gate_gain: bfloat16 [3072], P(('dp', 'seq')), may hold values from 0.5 to 1.5
- conv_weight: bfloat16 [4, 3328], P(None, ('dp', 'seq')), may hold values from -3 to 3
- conv_bias: bfloat16 [3328], P(('dp', 'seq')), may hold values from -0.5 to 0.5
- dt_bias: float32 [48], replicated, may hold values from -12 to -3
- a_log: float32 [48], replicated, may hold values from -0.7 to 0.7
- d_skip: float32 [48], replicated, may hold values from 0.5 to 1.5
Outputs:
- output: bfloat16 [8, 1024, 1536], P('dp', 'seq')
- input_grad: bfloat16 [8, 1024, 1536], P('dp', 'seq')
- in_weight_grad: float32 [1536, 6448], P(('dp', 'seq'))
- out_weight_grad: float32 [3072, 1536], P(('dp', 'seq'))
- norm_gain_grad: float32 [1536], P(('dp', 'seq'))
- gate_gain_grad: float32 [3072], P(('dp', 'seq'))
- conv_weight_grad: float32 [4, 3328], P(None, ('dp', 'seq'))
- conv_bias_grad: float32 [3328], P(('dp', 'seq'))
- dt_bias_grad: float32 [48], replicated
- a_log_grad: float32 [48], replicated
- d_skip_grad: float32 [48], replicated
Inputs may be any that keep to these rules, and one draw needn't show every extreme that they name: `lengths`: in every aligned block of 2 slots one or more slots have length 1024.
All inputs are finite; a program needn't handle non-finite values.
Results may differ from a plain program's by a relative error of at most 0.007.
Values may be sent and summed in bfloat16 or wider, within the bound.
A program may use at most 448 MiB of HBM per device.

v0:
```python
import jax
import jax.numpy as jnp
from jax import lax
from jax.sharding import PartitionSpec as P

SLOTS_MB = 1


EPS = 1e-05
HIGH = lax.Precision.HIGHEST


def from_behind(value, axis, steps):
    count = lax.axis_size(axis)
    leading, last = (max(0, -steps), min(count, count - steps))
    return lax.ppermute(value, axis, [(source, source + steps) for source in range(leading, last)])


def carried_in(value, axis, join, neutral, backward):
    count = lax.axis_size(axis)
    place = lax.axis_index(axis)
    ahead = count - 1 - place if backward else place
    gathered = jax.tree.map(
        lambda a, kind: lax.all_gather(a.astype(kind), axis),
        value,
        jax.tree.map(lambda a: jnp.bfloat16 if a.dtype == jnp.float32 else a.dtype, value),
    )
    state = jax.tree.map(lambda a, e: jnp.zeros_like(a) + jnp.asarray(e, a.dtype), value, neutral)

    def one(lap, state):
        source = count - 1 - lap if backward else lap
        return join(
            state,
            jax.tree.map(
                lambda a, own: lax.dynamic_index_in_dim(a, source, 0, False).astype(own.dtype),
                gathered,
                value,
            ),
        )

    return lax.fori_loop(0, ahead, one, state)


def as_sent(value):

    def short(part):
        return part.astype(jnp.bfloat16) if part.dtype == jnp.float32 else part

    return jax.tree.map(short, value)


def link_states(earlier, later):
    return (earlier[0] * later[0], later[0][:, :, None, None] * earlier[1] + later[1])


def silu_slope(values):
    sigma = jax.nn.sigmoid(values)
    return sigma * (1.0 + values * (1.0 - sigma))


def rows_product(left, right):
    return lax.dot_general(
        left, right, (((0,), (0,)), ((), ())), preferred_element_type=jnp.float32
    )


def cols_product(left, right):
    return lax.dot_general(
        left, right, (((1,), (1,)), ((), ())), preferred_element_type=jnp.float32
    )


def add_pair(first, second):
    return first + second


def first_total(stacked):
    return jnp.sum(stacked, axis=0)


def owner_sums(grads):
    lifted = tuple((grad[None] for grad in grads))
    by_data = (
        lax.all_to_all(lifted[0], "dp", split_axis=1, concat_axis=0, tiled=True),
        lax.all_to_all(lifted[1], "dp", split_axis=1, concat_axis=0, tiled=True),
        lax.all_to_all(lifted[2], "dp", split_axis=1, concat_axis=0, tiled=True),
        lax.all_to_all(lifted[3], "dp", split_axis=1, concat_axis=0, tiled=True),
        lax.all_to_all(lifted[4], "dp", split_axis=1, concat_axis=0, tiled=True),
        lax.all_to_all(lifted[5], "dp", split_axis=1, concat_axis=0, tiled=True),
    )
    partial_value = tuple((first_total(stacked)[None] for stacked in by_data))
    by_piece = (
        lax.all_to_all(partial_value[0], "seq", split_axis=1, concat_axis=0, tiled=True),
        lax.all_to_all(partial_value[1], "seq", split_axis=1, concat_axis=0, tiled=True),
        lax.all_to_all(partial_value[2], "seq", split_axis=1, concat_axis=0, tiled=True),
        lax.all_to_all(partial_value[3], "seq", split_axis=1, concat_axis=0, tiled=True),
        lax.all_to_all(partial_value[4], "seq", split_axis=1, concat_axis=0, tiled=True),
        lax.all_to_all(partial_value[5], "seq", split_axis=1, concat_axis=0, tiled=True),
    )
    return tuple((first_total(stacked) for stacked in by_piece))


def forward_pass(slot_in, weights, head_params):
    in_full, out_full, norm_full, gate_full, conv_full, bias_full = weights
    dt_shift, log_rate, skip_gain = head_params
    slot_count, piece_len, model_width = slot_in.shape
    inner_width = out_full.shape[0]
    channels = conv_full.shape[1]
    kernel = conv_full.shape[0]
    head_count = dt_shift.shape[0]
    head_size = inner_width // head_count
    state_size = (channels - inner_width) // 2
    input_f = slot_in.astype(jnp.float32)
    inv_rms = lax.rsqrt(jnp.mean(input_f * input_f, axis=-1, keepdims=True) + EPS)
    normed = (input_f * inv_rms * norm_full.astype(jnp.float32)).astype(jnp.bfloat16)
    projected = jnp.dot(
        normed.reshape(-1, model_width), in_full, preferred_element_type=jnp.float32
    ).reshape(slot_count, piece_len, -1)
    gate_part = projected[..., :inner_width]
    conv_in = projected[..., inner_width : inner_width + channels]
    dt_arg = projected[..., inner_width + channels :] + dt_shift
    rim_rows = from_behind(
        conv_in[:, piece_len - kernel + 1 :].astype(jnp.bfloat16), "seq", 1
    ).astype(jnp.float32)
    extended = jnp.concatenate([rim_rows, conv_in], axis=1)
    conv_taps = conv_full.astype(jnp.float32)
    pre_act = bias_full.astype(jnp.float32) + sum(
        (
            conv_taps[tap_index] * extended[:, tap_index : tap_index + piece_len]
            for tap_index in range(kernel)
        )
    )
    activated = jax.nn.silu(pre_act)
    x_heads = activated[..., :inner_width].reshape(slot_count, piece_len, head_count, head_size)
    b_rows = activated[..., inner_width : inner_width + state_size]
    c_rows = activated[..., inner_width + state_size :]
    dt_vals = jax.nn.softplus(dt_arg)
    decay_rates = -jnp.exp(log_rate)
    log_cum = jnp.cumsum(dt_vals * decay_rates, axis=1)
    log_tot = log_cum[:, -1]
    weights_in = jnp.exp(log_tot[:, None] - log_cum) * dt_vals
    local_state = jnp.einsum(
        "sthp,stn->shpn", weights_in[..., None] * x_heads, b_rows, precision=HIGH
    )
    carry_decay = jnp.exp(log_tot)
    neutral = (jnp.ones_like(carry_decay), jnp.zeros_like(local_state))
    _, start_state = carried_in((carry_decay, local_state), "seq", link_states, neutral, False)
    spots = jnp.arange(piece_len)
    causal = spots[:, None] >= spots[None, :]
    cum_heads = jnp.swapaxes(log_cum, 1, 2)
    gap_vals = jnp.where(causal, cum_heads[..., :, None] - cum_heads[..., None, :], 0.0)
    decay_mat = jnp.where(causal, jnp.exp(gap_vals), 0.0)
    cb_mat = jnp.einsum("stn,sun->stu", c_rows, b_rows, precision=HIGH)
    dt_cols = jnp.swapaxes(dt_vals, 1, 2)[:, :, None, :]
    mixing = decay_mat * cb_mat[:, None] * dt_cols
    y_intra = jnp.einsum("shtu,suhp->sthp", mixing, x_heads, precision=HIGH)
    state_read = jnp.einsum("stn,shpn->sthp", c_rows, start_state, precision=HIGH)
    exp_cum = jnp.exp(log_cum)
    y_heads = y_intra + exp_cum[..., None] * state_read + skip_gain[:, None] * x_heads
    y_flat = y_heads.reshape(slot_count, piece_len, inner_width)
    gate_act = jax.nn.silu(gate_part)
    gated_out = y_flat * gate_act
    inv_gate = lax.rsqrt(jnp.mean(gated_out * gated_out, axis=-1, keepdims=True) + EPS)
    gate_normed = (gated_out * inv_gate * gate_full.astype(jnp.float32)).astype(jnp.bfloat16)
    mixed = jnp.dot(
        gate_normed.reshape(-1, inner_width), out_full, preferred_element_type=jnp.float32
    )
    output = (input_f + mixed.reshape(slot_count, piece_len, model_width)).astype(jnp.bfloat16)
    saved = dict(
        input_f=input_f,
        inv_rms=inv_rms,
        normed=normed,
        gate_part=gate_part,
        dt_arg=dt_arg,
        extended=extended,
        pre_act=pre_act,
        x_heads=x_heads,
        b_rows=b_rows,
        c_rows=c_rows,
        dt_vals=dt_vals,
        log_cum=log_cum,
        log_tot=log_tot,
        weights_in=weights_in,
        carry_decay=carry_decay,
        start_state=start_state,
        decay_mat=decay_mat,
        cb_mat=cb_mat,
        dt_cols=dt_cols,
        mixing=mixing,
        state_read=state_read,
        exp_cum=exp_cum,
        y_flat=y_flat,
        gate_act=gate_act,
        gated_out=gated_out,
        inv_gate=inv_gate,
        gate_normed=gate_normed,
    )
    return (output, saved)


def backward_pass(saved, slot_cot, live, weights, head_params):
    in_full, out_full, norm_full, gate_full, conv_full, bias_full = weights
    dt_shift, log_rate, skip_gain = head_params
    slot_count, piece_len, model_width = slot_cot.shape
    inner_width = out_full.shape[0]
    kernel = conv_full.shape[0]
    x_heads = saved["x_heads"]
    b_rows = saved["b_rows"]
    c_rows = saved["c_rows"]
    dt_vals = saved["dt_vals"]
    log_cum = saved["log_cum"]
    weights_in = saved["weights_in"]
    carry_decay = saved["carry_decay"]
    start_state = saved["start_state"]
    decay_mat = saved["decay_mat"]
    cb_mat = saved["cb_mat"]
    dt_cols = saved["dt_cols"]
    decay_rates = -jnp.exp(log_rate)
    masked_cot = slot_cot * live[..., None].astype(jnp.bfloat16)
    cot_rows = masked_cot.reshape(-1, model_width)
    d_gn = cols_product(cot_rows, out_full).reshape(slot_count, piece_len, inner_width)
    gate_hat = saved["gated_out"] * saved["inv_gate"]
    grad_ggain = jnp.sum(d_gn * gate_hat, axis=(0, 1))
    d_hat = d_gn * gate_full.astype(jnp.float32)
    d_gated = saved["inv_gate"] * (
        d_hat - gate_hat * jnp.mean(d_hat * gate_hat, axis=-1, keepdims=True)
    )
    d_gate_part = d_gated * saved["y_flat"] * silu_slope(saved["gate_part"])
    d_heads = (d_gated * saved["gate_act"]).reshape(x_heads.shape)
    grad_skip = jnp.sum(d_heads * x_heads, axis=(0, 1, 3))
    exp_cum = saved["exp_cum"]
    d_read = d_heads * exp_cum[..., None]
    d_cvals = jnp.einsum("sthp,shpn->stn", d_read, start_state, precision=HIGH)
    d_start = jnp.einsum("sthp,stn->shpn", d_read, c_rows, precision=HIGH)
    d_cum = jnp.sum(d_heads * saved["state_read"], axis=-1) * exp_cum
    d_mixing = jnp.einsum("sthp,suhp->shtu", d_heads, x_heads, precision=HIGH)
    d_x = skip_gain[:, None] * d_heads + jnp.einsum(
        "shtu,sthp->suhp", saved["mixing"], d_heads, precision=HIGH
    )
    d_decay = d_mixing * cb_mat[:, None] * dt_cols
    d_cb = jnp.sum(d_mixing * decay_mat * dt_cols, axis=1)
    d_dt = jnp.swapaxes(jnp.sum(d_mixing * decay_mat * cb_mat[:, None], axis=2), 1, 2)
    spread = d_decay * decay_mat
    d_cum = d_cum + jnp.swapaxes(jnp.sum(spread, axis=3) - jnp.sum(spread, axis=2), 1, 2)
    d_cvals = d_cvals + jnp.einsum("stu,sun->stn", d_cb, b_rows, precision=HIGH)
    d_bvals = jnp.einsum("stu,stn->sun", d_cb, c_rows, precision=HIGH)
    neutral = (jnp.ones_like(carry_decay), jnp.zeros_like(d_start))
    _, later_grad = carried_in((carry_decay, d_start), "seq", link_states, neutral, True)
    d_tot = jnp.sum(later_grad * start_state, axis=(2, 3)) * carry_decay
    grad_proj_b = jnp.einsum("shpn,stn->sthp", later_grad, b_rows, precision=HIGH)
    d_x = d_x + weights_in[..., None] * grad_proj_b
    d_weights = jnp.sum(grad_proj_b * x_heads, axis=-1)
    d_bvals = d_bvals + jnp.einsum(
        "sthp,shpn->stn", weights_in[..., None] * x_heads, later_grad, precision=HIGH
    )
    d_dt = d_dt + d_weights * jnp.exp(saved["log_tot"][:, None] - log_cum)
    through = d_weights * weights_in
    d_tot = d_tot + jnp.sum(through, axis=1)
    last_row = (jnp.arange(piece_len) == piece_len - 1).astype(jnp.float32)
    d_cum = d_cum - through + last_row[None, :, None] * d_tot[:, None, :]
    d_log = lax.cumsum(d_cum, axis=1, reverse=True)
    d_dt = d_dt + d_log * decay_rates
    grad_alog = jnp.sum(d_log * dt_vals, axis=(0, 1)) * decay_rates
    d_arg = d_dt * jax.nn.sigmoid(saved["dt_arg"])
    grad_dtb = jnp.sum(d_arg, axis=(0, 1))
    d_act = jnp.concatenate(
        [d_x.reshape(slot_count, piece_len, inner_width), d_bvals, d_cvals], axis=-1
    )
    d_pre = d_act * silu_slope(saved["pre_act"])
    grad_cbias = jnp.sum(d_pre, axis=(0, 1))
    extended = saved["extended"]
    grad_conv = jnp.stack(
        [
            jnp.sum(d_pre * extended[:, tap_index : tap_index + piece_len], axis=(0, 1))
            for tap_index in range(kernel)
        ]
    )
    conv_taps = conv_full.astype(jnp.float32)
    d_ext = sum(
        (
            jnp.pad(
                conv_taps[tap_index] * d_pre, ((0, 0), (tap_index, kernel - 1 - tap_index), (0, 0))
            )
            for tap_index in range(kernel)
        )
    )
    back_rim = from_behind(as_sent(d_ext[:, : kernel - 1]), "seq", -1)
    d_conv_in = d_ext[:, kernel - 1 :] + jnp.pad(
        back_rim, ((0, 0), (piece_len - kernel + 1, 0), (0, 0))
    )
    d_proj = jnp.concatenate([d_gate_part, d_conv_in, d_arg], axis=-1).astype(jnp.bfloat16)
    d_proj = d_proj.reshape(slot_count * piece_len, -1)
    d_normed = cols_product(d_proj, in_full).reshape(slot_count, piece_len, model_width)
    in_hat = saved["input_f"] * saved["inv_rms"]
    grad_ngain = jnp.sum(d_normed * in_hat, axis=(0, 1))
    d_norm_in = d_normed * norm_full.astype(jnp.float32)
    input_grad = saved["inv_rms"] * (
        d_norm_in - in_hat * jnp.mean(d_norm_in * in_hat, axis=-1, keepdims=True)
    )
    input_grad = input_grad + masked_cot.astype(jnp.float32)
    product_rows = (
        saved["normed"].reshape(-1, model_width),
        d_proj,
        saved["gate_normed"].reshape(-1, inner_width),
        cot_rows,
    )
    small_grads = (grad_ngain, grad_ggain, grad_conv, grad_cbias)
    return (
        input_grad.astype(jnp.bfloat16),
        product_rows,
        small_grads,
        (grad_dtb, grad_alog, grad_skip),
    )


def body(
    block_input,
    cotangent,
    lengths,
    in_weight,
    out_weight,
    norm_gain,
    gate_gain,
    conv_weight,
    conv_bias,
    dt_bias,
    a_log,
    d_skip,
):
    shards = (in_weight, out_weight, norm_gain, gate_gain, conv_weight, conv_bias)
    head_params = (dt_bias, a_log, d_skip)
    piece_len = block_input.shape[1]
    batches = block_input.shape[0] // SLOTS_MB
    positions = lax.axis_index("seq") * piece_len + jnp.arange(piece_len, dtype=jnp.int32)
    held = (
        lax.all_gather(shards[0], ("dp", "seq"), axis=0, tiled=True),
        lax.all_gather(shards[1], ("dp", "seq"), axis=0, tiled=True),
        lax.all_gather(shards[2], ("dp", "seq"), axis=0, tiled=True),
        lax.all_gather(shards[3], ("dp", "seq"), axis=0, tiled=True),
        lax.all_gather(shards[4], ("dp", "seq"), axis=1, tiled=True),
        lax.all_gather(shards[5], ("dp", "seq"), axis=0, tiled=True),
    )
    outputs = []
    input_grads = []
    kept_rows = []
    small_totals = None
    head_totals = None
    for batch_index in range(batches):
        first = batch_index * SLOTS_MB
        slot_in = block_input[first : first + SLOTS_MB]
        slot_cot = cotangent[first : first + SLOTS_MB]
        live = (positions[None, :] < lengths[first : first + SLOTS_MB, None]).astype(jnp.float32)
        output, saved = forward_pass(slot_in, held, head_params)
        input_grad, product_rows, small_grads, head_grads = backward_pass(
            saved, slot_cot, live, held, head_params
        )
        outputs.append(output)
        input_grads.append(input_grad)
        kept_rows.append(product_rows)
        small_totals = (
            small_grads
            if small_totals is None
            else jax.tree.map(add_pair, small_totals, small_grads)
        )
        head_totals = (
            head_grads if head_totals is None else jax.tree.map(add_pair, head_totals, head_grads)
        )
    normed_all = jnp.concatenate([rows[0] for rows in kept_rows], axis=0)
    dproj_all = jnp.concatenate([rows[1] for rows in kept_rows], axis=0)
    gnormed_all = jnp.concatenate([rows[2] for rows in kept_rows], axis=0)
    cot_all = jnp.concatenate([rows[3] for rows in kept_rows], axis=0)
    grad_win = rows_product(normed_all, dproj_all)
    grad_wout = rows_product(gnormed_all, cot_all)
    grad_ngain, grad_ggain, grad_conv, grad_cbias = small_totals
    owned = owner_sums((grad_win, grad_wout, grad_ngain, grad_ggain, grad_conv.T, grad_cbias))
    head_sums = lax.psum(head_totals, ("dp", "seq"))
    return (
        jnp.concatenate(outputs, axis=0),
        jnp.concatenate(input_grads, axis=0),
        owned[0],
        owned[1],
        owned[2],
        owned[3],
        owned[4].T,
        owned[5],
        head_sums[0],
        head_sums[1],
        head_sums[2],
    )


def solution(mesh):
    placed = (
        P("dp", "seq", None),
        P("dp", "seq", None),
        P("dp"),
        P(("dp", "seq"), None),
        P(("dp", "seq"), None),
        P(("dp", "seq")),
        P(("dp", "seq")),
        P(None, ("dp", "seq")),
        P(("dp", "seq")),
        P(),
        P(),
        P(),
    )
    return jax.shard_map(
        body,
        mesh=mesh,
        in_specs=placed,
        out_specs=(
            P("dp", "seq", None),
            P("dp", "seq", None),
            P(("dp", "seq"), None),
            P(("dp", "seq"), None),
            P(("dp", "seq")),
            P(("dp", "seq")),
            P(None, ("dp", "seq")),
            P(("dp", "seq")),
            P(),
            P(),
            P(),
        ),
        check_vma=False,
    )
```

profile of v0, /device:TPU:9, one launch (start us, length us, event | category | flops | bytes accessed | tf_op | source)
XLA Modules:
  0.0 2248.7 jit_solution(6814819859999348512)
XLA Ops:
  11.3 42.4 %all-reduce.14 = (bf16[1536]{0:T(1024)(128)(2,1)S(1)}, bf16[3328]{0:T(1024)(128)(2,1)S(1)}, bf16[3072]{0:T(1024)(128)(2,1)}) all-reduce(bf16[1536]{0:T(1024)(128)(2,1)S(1)} %dynamic-update-slice.1, bf16[3328]{0:T(1024)(128)(2,1)S(1)} %dynamic-update-slice, ...), channel_id=1, replica_groups=mesh['dp'=4,'seq'=8] {'dp','seq'}, use_global_device_ids=true, to_apply=%add.11 | all-reduce | flops 7936 | bytes 31744
  54.3 34.3 %all-gather.4 = bf16[32,104,4]{1,2,0:T(4,128)(2,1)S(1)} all-gather(bf16[1,104,4]{1,2,0:T(4,128)(2,1)} %bitcast.527), channel_id=1, replica_groups=mesh['dp'=4,'seq'=8] {'dp','seq'}, dimensions={0}, use_global_device_ids=true | all-gather | bytes 27456 | tf_op jit(solution)/shard_map/all_gather | solution.py:340
  90.9 51.8 %all-gather.12.cloned.1.call-done = bf16[1536,6448]{1,0:T(8,128)(2,1)} async-done(((bf16[48,6448]{1,0:T(8,128)(2,1)}), bf16[1536,6448]{1,0:T(8,128)(2,1)}) %all-gather.12.cloned.1.call-update) | async-done | bytes 19808272 | tf_op jit(solution)/shard_map/all_gather | solution.py:336
  142.7 12.2 convolution_bitcast_fusion.3
  161.8 12.5 convolution_bitcast_fusion.2
  192.4 15.5 fusion.32
  227.3 7.5 fusion.234
  235.6 8.8 all_gather.58
  244.3 7.8 all_gather.63
  254.9 19.1 all-gather.16.cloned.1.call-done
  277.3 6.5 fusion.51
  283.8 3.8 multiply_reduce_fusion.21
  288.1 33.8 %all-gather.18.cloned.1.call-done = bf16[384,64,128]{2,1,0:T(8,128)(2,1)} async-done(((bf16[48,64,128]{2,1,0:T(8,128)(2,1)}), bf16[384,64,128]{2,1,0:T(8,128)(2,1)}) %all-gather.18.cloned.1.call-update) | async-done | bytes 6291472 | tf_op jit(solution)/shard_map/all_gather | solution.py:24
  326.6 6.5 fusion.50
  335.1 6.3 fusion.53
  341.4 6.3 multiply_reduce_fusion.12
  359.7 4.6 all-to-all-start.6
  364.2 4.2 fusion.115
  368.5 5.2 fusion.235
  373.8 10.8 fusion.21
  393.6 13.7 all-gather.22.cloned.1.call-done
  408.8 22.1 while.55
  440.2 15.0 all-gather.20.cloned.1.call-done
  455.4 13.4 while.54
  476.7 3.7 fusion.48
  480.5 6.7 fusion.225
  490.7 3.7 fusion.49
  494.5 7.2 fusion.226
  503.7 4.8 all-to-all-start.10
  521.6 6.7 broadcast_multiply_fusion.6
  535.3 4.9 collective-permute-start.3
  540.2 5.7 pad_add_fusion.1
  557.7 19.4 fusion.39
  586.0 4.7 all-to-all-start.11
  590.8 20.4 fusion.136
  611.9 4.7 all-to-all-start.4
  619.3 14.8 reduce.72
  636.1 4.5 all-to-all-start.8
  644.3 6.2 all-to-all-start.5
  658.5 4.4 all-to-all-start.9
  663.0 3.7 convolution_bitcast_fusion.1
  666.8 22.7 %copy.313 = f32[1,3072,1536]{2,0,1:T(1,128)} copy(f32[1,3072,1536]{2,1,0:T(8,128)S(1)} %convolution_bitcast_fusion.1) | data formatting | bytes 37748736 | tf_op jit(solution)/shard_map/broadcast_in_dim | solution.py:82
  690.1 8.3 all-to-all-start.2
  698.5 20.7 convolution_bitcast_fusion
  719.2 86.7 %copy.310 = f32[1,1536,6448]{2,0,1:T(1,128)} copy(f32[1,1536,6448]{1,2,0:T(8,128)} %convolution_bitcast_fusion) | data formatting | bytes 79233024 | tf_op jit(solution)/shard_map/broadcast_in_dim | solution.py:82
  806.0 297.4 %all-to-all-done.2 = f32[1,3072,1536]{2,0,1:T(1,128)} async-done(((f32[1,3072,1536]{2,0,1:T(1,128)}), f32[1,3072,1536]{2,0,1:T(1,128)}, u32[]{:S(2)}, u32[]{:S(2)}) %all-to-all-start.2) | async-done | bytes 18874400 | tf_op jit(solution)/shard_map/all_to_all | solution.py:85
  1103.4 14.2 all-to-all-start
  1117.6 16.4 copy.340
  1134.0 11.3 reduce_sum.574
  1145.3 6.4 broadcast_in_dim.43
  1151.7 824.9 %all-to-all-done = f32[1,1536,6448]{2,0,1:T(1,128)} async-done(((f32[1,1536,6448]{2,0,1:T(1,128)}), f32[1,1536,6448]{2,0,1:T(1,128)}, u32[]{:S(2)}, u32[]{:S(2)}) %all-to-all-start) | async-done | bytes 39616544 | tf_op jit(solution)/shard_map/all_to_all | solution.py:84
  1976.6 6.2 all-to-all-start.3
  1982.8 31.7 %copy.338 = f32[1,1536,6448]{2,1,0:T(8,128)} copy(f32[1,1536,6448]{2,0,1:T(1,128)} %all-to-all-done) | data formatting | bytes 79233024
  2014.5 18.5 reduce_sum.572
  2033.0 10.7 copy.342
  2043.7 22.3 copy.312
  2066.0 5.3 all-to-all-start.1
  2071.7 5.2 fusion.19
  2077.0 5.2 fusion.20
  2083.8 130.5 %all-reduce.13 = (f32[48]{0:T(128)}, f32[48]{0:T(128)}, f32[48]{0:T(128)}) all-reduce(f32[48]{0:T(128)S(1)} %add.487, f32[48]{0:T(128)S(1)} %add_multiply_fusion, f32[48]{0:T(128)S(1)} %add.489), channel_id=1, replica_groups=mesh['dp'=4,'seq'=8] {'dp','seq'}, use_global_device_ids=true, to_apply=%region_64.65 | all-reduce | flops 144 | bytes 1152 | tf_op jit(solution)/shard_map/psum | solution.py:376
  2219.1 4.8 copy.341
  2223.9 3.6 reduce_sum.575
  2227.5 8.3 copy.339
  2235.8 5.5 reduce_sum.573
  (529 shorter events, 212.7 us)
Async XLA Ops:
  7.2 82.3 %copy-start.31 = (bf16[2,128,1536]{2,1,0:T(8,128)(2,1)S(1)}, bf16[2,128,1536]{2,1,0:T(8,128)(2,1)}, u32[]{:S(2)}) copy-start(bf16[2,128,1536]{2,1,0:T(8,128)(2,1)} %param.20) | copy-start | bytes 2359300
  7.2 82.5 %copy-start.156 = (f32[48]{0:T(128)S(1)}, f32[48]{0:T(128)}, u32[]{:S(2)}) copy-start(f32[48]{0:T(128)} %param.30) | copy-start | bytes 580
  7.2 135.5 %all-gather.12.cloned.1.call-start = ((), (), s32[]{:S(2)}) async-start(), calls=%async_computation.12 | async-start | bytes 20680704 | tf_op jit(solution)/shard_map/all_gather | solution.py:336
  7.9 219.4 %all-gather.14.cloned.1.call-start = ((), (), s32[]{:S(2)}) async-start(), calls=%async_computation.13 | async-start | bytes 9732096 | tf_op jit(solution)/shard_map/all_gather | solution.py:337
  8.7 265.3 %all-gather.16.cloned.1.call-start = ((), (), s32[]{:S(2)}) async-start(), calls=%async_computation.14 | async-start | bytes 7077888 | tf_op jit(solution)/shard_map/all_gather | solution.py:24
  53.7 537.0 %copy-start.84 = (f32[1536]{0:T(1024)}, f32[1536]{0:T(1024)S(1)}, u32[]{:S(2)}) copy-start(f32[1536]{0:T(1024)S(1)} %convert_element_type.300) | copy-start | bytes 18436
  89.7 86.0 %copy-start.147 = (f32[48]{0:T(128)}, f32[48]{0:T(128)S(1)}, u32[]{:S(2)}) copy-start(f32[48]{0:T(128)S(1)} %exponential_negate_fusion) | copy-start | bytes 580
  89.7 53.0 %copy-start.138 = (f32[128]{0:T(128)}, f32[128]{0:T(128)S(1)}, u32[]{:S(2)}) copy-start(f32[128]{0:T(128)S(1)} %get-tuple-element.619) | copy-start | bytes 1540
  89.7 53.0 %copy-start.141 = (f32[128]{0:T(128)}, f32[128]{0:T(128)S(1)}, u32[]{:S(2)}) copy-start(f32[128]{0:T(128)S(1)} %get-tuple-element.620) | copy-start | bytes 1540
  154.9 29.0 %copy-start.1 = (f32[1,128,6448]{1,2,0:T(8,128)}, f32[1,128,6448]{1,2,0:T(8,128)S(1)}, u32[]{:S(2)}) copy-start(f32[1,128,6448]{1,2,0:T(8,128)S(1)} %convolution_bitcast_fusion.3) | copy-start | bytes 9904132
  158.4 29.3 %collective-permute-start = (bf16[1,3,3328]{2,1,0:T(4,128)(2,1)}, bf16[1,3,3328]{2,1,0:T(4,128)(2,1)}, u32[]{:S(2)}, u32[]{:S(2)}) collective-permute-start(bf16[1,3,3328]{2,1,0:T(4,128)(2,1)} %copy.274), channel_id=1, source_target_pairs={{0,1},{1,2},{2,3},{3,4},{4,5},{5,6},{6,7},{8,9},{9,10},{10,11},{11... | collective-permute-start | bytes 59912 | tf_op jit(solution)/shard_map/ppermute | solution.py:16
  179.1 11.0 collective-permute-start.1
  192.4 15.6 copy-start.77
  208.0 67.8 %copy-start.10 = (f32[1,128,3328]{1,2,0:T(8,128)}, f32[1,128,3328]{1,2,0:T(8,128)S(1)}, u32[]{:S(2)}) copy-start(f32[1,128,3328]{1,2,0:T(8,128)S(1)} %get-tuple-element.550) | copy-start | bytes 5111812
  213.0 108.9 %all-gather.18.cloned.1.call-start = ((), (), s32[]{:S(2)}) async-start(), calls=%async_computation.15 | async-start | bytes 7077888 | tf_op jit(solution)/shard_map/all_gather | solution.py:24
  220.2 187.2 %all-gather.22.cloned.1.call-start = ((), (), s32[]{:S(2)}) async-start(), calls=%async_computation.17 | async-start | bytes 7077888 | tf_op jit(solution)/shard_map/all_gather | solution.py:24
  222.4 12.4 copy-start.134
  222.4 12.4 copy-start.136
  223.9 10.9 copy-start.54
  227.3 17.0 copy-start.155
  234.9 42.4 %copy-start.105 = (f32[48,128]{1,0:T(8,128)}, f32[48,128]{1,0:T(8,128)S(1)}, u32[]{:S(2)}) copy-start(f32[48,128]{1,0:T(8,128)S(1)} %copy.277) | copy-start | bytes 73732
  352.5 102.7 %all-gather.20.cloned.1.call-start = ((), (), s32[]{:S(2)}) async-start(), calls=%async_computation.16 | async-start | bytes 7077888 | tf_op jit(solution)/shard_map/all_gather | solution.py:24
  359.7 33.3 %all-to-all-start.6 = ((f32[1,4,768]{2,0,1:T(1,128)}), f32[1,4,768]{2,0,1:T(1,128)S(1)}, u32[]{:S(2)}, u32[]{:S(2)}) async-start(f32[1,4,768]{2,0,1:T(1,128)} %bitcast.138), calls=%async_computation.6 | async-start | bytes 24576 | tf_op jit(solution)/shard_map/all_to_all | solution.py:87
  373.8 12.0 copy-start.45
  480.4 10.2 copy-start.20
  480.4 10.2 copy-start.78
  480.4 10.2 copy-start.89
  480.4 10.2 copy-start.107
  480.5 14.0 copy-start.40
  503.7 74.6 %all-to-all-start.10 = ((f32[1,4,832]{2,0,1:T(1,128)}), f32[1,4,832]{2,0,1:T(1,128)}, u32[]{:S(2)}, u32[]{:S(2)}) async-start(f32[1,4,832]{2,0,1:T(1,128)} %add.486), calls=%async_computation.10 | async-start | bytes 28672 | tf_op jit(solution)/shard_map/all_to_all | solution.py:89
  535.3 19.1 collective-permute-start.3
  550.8 26.2 %collective-permute-start.2 = (bf16[1,3,3328]{2,1,0:T(4,128)(2,1)}, bf16[1,3,3328]{2,1,0:T(4,128)(2,1)}, u32[]{:S(2)}, u32[]{:S(2)}) collective-permute-start(bf16[1,3,3328]{2,1,0:T(4,128)(2,1)} %copy.298), channel_id=1, source_target_pairs={{1,0},{2,1},{3,2},{4,3},{5,4},{6,5},{7,6},{9,8},{10,9},{11,10},{12... | collective-permute-start | bytes 59912 | tf_op jit(solution)/shard_map/ppermute | solution.py:16
  557.6 19.4 copy-start.55
  578.3 7.7 all-to-all-start.7
  584.6 26.7 %copy-start.57 = (bf16[128,3328]{0,1:T(8,128)(2,1)}, bf16[128,3328]{0,1:T(8,128)(2,1)S(1)}, u32[]{:S(2)}) copy-start(bf16[128,3328]{0,1:T(8,128)(2,1)S(1)} %fusion.128) | copy-start | bytes 2555908
  586.0 25.2 %copy-start.119 = (f32[1,8,96]{2,0,1:T(1,128)}, f32[1,8,96]{2,0,1:T(1,128)S(1)}, u32[]{:S(2)}) copy-start(f32[1,8,96]{2,0,1:T(1,128)S(1)} %all-to-all-done.7) | copy-start | bytes 9220
  586.0 25.8 %all-to-all-start.11 = ((f32[1,8,104]{2,0,1:T(1,128)}), f32[1,8,104]{2,0,1:T(1,128)S(1)}, u32[]{:S(2)}, u32[]{:S(2)}) async-start(f32[1,8,104]{2,0,1:T(1,128)} %all_to_all.127), calls=%async_computation.11 | async-start | bytes 8192 | tf_op jit(solution)/shard_map/all_to_all | solution.py:98
  590.8 25.8 %copy-start.95 = (f32[1,3328]{1,0:T(1,128)S(1)}, f32[1,3328]{1,0:T(1,128)}, u32[]{:S(2)}) copy-start(f32[1,3328]{1,0:T(1,128)} %stack.38) | copy-start | bytes 39940
  590.8 25.8 %copy-start.96 = (f32[1,3328]{1,0:T(1,128)S(1)}, f32[1,3328]{1,0:T(1,128)}, u32[]{:S(2)}) copy-start(f32[1,3328]{1,0:T(1,128)} %stack.36) | copy-start | bytes 39940
  590.8 25.8 %copy-start.97 = (f32[1,3328]{1,0:T(1,128)S(1)}, f32[1,3328]{1,0:T(1,128)}, u32[]{:S(2)}) copy-start(f32[1,3328]{1,0:T(1,128)} %stack.37) | copy-start | bytes 39940
  590.8 25.8 %copy-start.98 = (f32[1,3328]{1,0:T(1,128)S(1)}, f32[1,3328]{1,0:T(1,128)}, u32[]{:S(2)}) copy-start(f32[1,3328]{1,0:T(1,128)} %stack.35) | copy-start | bytes 39940
  590.8 25.8 %copy-start.99 = (f32[1,3328]{1,0:T(1,128)S(1)}, f32[1,3328]{1,0:T(1,128)}, u32[]{:S(2)}) copy-start(f32[1,3328]{1,0:T(1,128)} %stack.33) | copy-start | bytes 39940
  590.8 25.8 %copy-start.100 = (f32[1,3328]{1,0:T(1,128)S(1)}, f32[1,3328]{1,0:T(1,128)}, u32[]{:S(2)}) copy-start(f32[1,3328]{1,0:T(1,128)} %stack.31) | copy-start | bytes 39940
  590.8 25.8 %copy-start.101 = (f32[1,3328]{1,0:T(1,128)S(1)}, f32[1,3328]{1,0:T(1,128)}, u32[]{:S(2)}) copy-start(f32[1,3328]{1,0:T(1,128)} %stack.32) | copy-start | bytes 39940
  590.8 25.8 %copy-start.102 = (f32[1,3328]{1,0:T(1,128)S(1)}, f32[1,3328]{1,0:T(1,128)}, u32[]{:S(2)}) copy-start(f32[1,3328]{1,0:T(1,128)} %stack.30) | copy-start | bytes 39940
  611.9 22.3 copy-start.117
  611.9 24.3 %all-to-all-start.4 = ((f32[1,4,384]{2,0,1:T(1,128)}), f32[1,4,384]{2,0,1:T(1,128)S(1)}, u32[]{:S(2)}, u32[]{:S(2)}) async-start(f32[1,4,384]{2,0,1:T(1,128)} %add.481), calls=%async_computation.4 | async-start | bytes 12288 | tf_op jit(solution)/shard_map/all_to_all | solution.py:86
  636.1 8.2 all-to-all-start.8
  644.3 14.2 all-to-all-start.5
  658.5 31.0 %all-to-all-start.9 = ((f32[8,1,416]{2,1,0:T(1,128)}), f32[8,1,416]{2,1,0:T(1,128)S(1)}, u32[]{:S(2)}, u32[]{:S(2)}) async-start(f32[8,1,416]{2,1,0:T(1,128)} %reshape.1305), calls=%async_computation.9 | async-start | bytes 32768 | tf_op jit(solution)/shard_map/all_to_all | solution.py:97
  690.1 413.2 %all-to-all-start.2 = ((f32[1,3072,1536]{2,0,1:T(1,128)}), f32[1,3072,1536]{2,0,1:T(1,128)}, u32[]{:S(2)}, u32[]{:S(2)}) async-start(f32[1,3072,1536]{2,0,1:T(1,128)} %copy.313), calls=%async_computation.2 | async-start | bytes 37748736 | tf_op jit(solution)/shard_map/all_to_all | solution.py:85
  1103.4 873.2 %all-to-all-start = ((f32[1,1536,6448]{2,0,1:T(1,128)}), f32[1,1536,6448]{2,0,1:T(1,128)}, u32[]{:S(2)}, u32[]{:S(2)}) async-start(f32[1,1536,6448]{2,0,1:T(1,128)} %copy.310), calls=%async_computation | async-start | bytes 80216064 | tf_op jit(solution)/shard_map/all_to_all | solution.py:84
  1976.6 89.4 %all-to-all-start.3 = ((f32[1,768,1536]{2,0,1:T(1,128)}), f32[1,768,1536]{2,0,1:T(1,128)}, u32[]{:S(2)}, u32[]{:S(2)}) async-start(f32[1,768,1536]{2,0,1:T(1,128)} %broadcast_in_dim.43), calls=%async_computation.3 | async-start | bytes 9437184 | tf_op jit(solution)/shard_map/all_to_all | solution.py:94
  2066.0 161.5 %all-to-all-start.1 = ((f32[1,384,6448]{2,0,1:T(1,128)}), f32[1,384,6448]{2,0,1:T(1,128)}, u32[]{:S(2)}, u32[]{:S(2)}) async-start(f32[1,384,6448]{2,0,1:T(1,128)} %copy.312), calls=%async_computation.1 | async-start | bytes 20054016 | tf_op jit(solution)/shard_map/all_to_all | solution.py:93
  2076.9 137.4 %copy-start.162 = (f32[128]{0:T(128)S(1)}, f32[128]{0:T(128)}, u32[]{:S(2)}) copy-start(f32[128]{0:T(128)} %get-tuple-element.475) | copy-start | bytes 1540
  2077.0 137.3 %copy-start.161 = (f32[128]{0:T(128)S(1)}, f32[128]{0:T(128)}, u32[]{:S(2)}) copy-start(f32[128]{0:T(128)} %get-tuple-element.476) | copy-start | bytes 1540
  2077.0 137.3 %copy-start.66 = (f32[128,1536]{1,0:T(8,128)S(1)}, f32[128,1536]{1,0:T(8,128)}, u32[]{:S(2)}) copy-start(f32[128,1536]{1,0:T(8,128)} %get-tuple-element.618) | copy-start | bytes 2359300
  2077.0 137.3 %copy-start.85 = (f32[1536]{0:T(1024)S(1)}, f32[1536]{0:T(1024)}, u32[]{:S(2)}) copy-start(f32[1536]{0:T(1024)} %copy-done.84) | copy-start | bytes 18436
  2077.0 137.3 %copy-start.135 = (bf16[128]{0:T(256)(128)(2,1)S(1)}, bf16[128]{0:T(256)(128)(2,1)}, u32[]{:S(2)}) copy-start(bf16[128]{0:T(256)(128)(2,1)} %copy-done.134) | copy-start | bytes 772
  2077.0 137.3 %copy-start.137 = (bf16[128]{0:T(256)(128)(2,1)S(1)}, bf16[128]{0:T(256)(128)(2,1)}, u32[]{:S(2)}) copy-start(bf16[128]{0:T(256)(128)(2,1)} %copy-done.136) | copy-start | bytes 772
  2077.0 137.3 %copy-start.140 = (f32[128]{0:T(128)S(1)}, f32[128]{0:T(128)}, u32[]{:S(2)}) copy-start(f32[128]{0:T(128)} %copy-done.138) | copy-start | bytes 1540
  2077.0 137.3 %copy-start.143 = (f32[128]{0:T(128)S(1)}, f32[128]{0:T(128)}, u32[]{:S(2)}) copy-start(f32[128]{0:T(128)} %copy-done.141) | copy-start | bytes 1540
  2082.2 132.1 %copy-start.63 = (bf16[2,128,1536]{2,1,0:T(8,128)(2,1)S(1)}, bf16[2,128,1536]{2,1,0:T(8,128)(2,1)}, u32[]{:S(2)}) copy-start(bf16[2,128,1536]{2,1,0:T(8,128)(2,1)} %param.21) | copy-start | bytes 2359300
  2082.2 132.1 %copy-start.65 = (f32[128,1536]{1,0:T(8,128)S(1)}, f32[128,1536]{1,0:T(8,128)}, u32[]{:S(2)}) copy-start(f32[128,1536]{1,0:T(8,128)} %fusion.39) | copy-start | bytes 2359300
  (121 other events, 550.5 us)
Sparse Core Ops, SparseCore 0:
  10.9 131.7 all-gather.11
  145.6 81.6 all-gather.13
  229.8 44.1 all-gather.15
  276.3 45.5 all-gather.17
  352.6 54.6 all-gather.21
  409.7 45.5 all-gather.19
where the time goes:
time: 2270 us; the launch traced here: 2250 us
  waiting for transfers between devices  1260 us (56%)
  local copies, waits for them, and re-layouts  276 us (12%)
  blocking collectives  224 us (10%)
  other arithmetic  192 us (8%)
  matrix products  191 us (8%)
  starting transfers between devices  84.3 us (4%)
    all_to_all x1, waiting for transfers between devices, owner_sums(): lax.all_to_all(lifted[0], 'dp', split_axis=1, concat_axis=0, tiled=True)  825 us
    all_to_all x1, waiting for transfers between devices, owner_sums(): lax.all_to_all(lifted[1], 'dp', split_axis=1, concat_axis=0, tiled=True)  297 us
    psum x1, blocking collectives, body(): head_sums = lax.psum(head_totals, ('dp', 'seq'))  131 us
    broadcast_in_dim x3, local copies, waits for them, and re-layouts, owner_sums(): lifted = tuple((grad[None] for grad in grads))  111 us
    unnamed x343, local copies, waits for them, and re-layouts  96.5 us
    all_gather x4, waiting for transfers between devices, carried_in(): lax.all_gather(a.astype(kind), axis)  81.6 us
    dot_general x4, matrix products, cols_product(): lax.dot_general(left, right, (((1,), (1,)), ((), ())), preferred_element_...  53.6 us
    all_gather x1, waiting for transfers between devices, body(): lax.all_gather(shards[0], ('dp', 'seq'), axis=0, tiled=True)  51.8 us
  transfers between devices with their start and end apart: 22, of which 9 were waited for; matrix products, arithmetic and copies ran while one was open for 25% of the time, Pallas kernels for 0%

commit v1 on v0

--- a/solution.py
+++ b/solution.py
@@ -1,6 +1,10 @@
+import functools
+
 import jax
 import jax.numpy as jnp
 from jax import lax
+from jax.experimental import pallas as pl
+from jax.experimental.pallas import tpu as pltpu
 from jax.sharding import PartitionSpec as P
 
 SLOTS_MB = 1
@@ -389,6 +393,1632 @@
     )
 
 
+F32 = jnp.float32
+BF16 = jnp.bfloat16
+MESH_ID = pl.DeviceIdType.MESH
+ANY = pl.BlockSpec(memory_space=pl.ANY)
+INVMEM = pl.BlockSpec(memory_space=pltpu.VMEM)
+VMEM_LIMIT = 60 * 1024 * 1024
+CHUNK = 128
+
+
+def flip(place, bit):
+    return place + bit - 2 * bit * lax.rem(lax.div(place, bit), 2)
+
+
+def flip_all(place, mask):
+    for bit in (1, 2, 4):
+        if mask & bit:
+            place = flip(place, bit)
+    return place
+
+
+class Links:
+    def __init__(self, sends, recvs):
+        self.sends, self.recvs, self.used = sends, recvs, 0
+
+    def copy(self, source, target, device):
+        slot = self.used
+        self.used += 1
+        return pltpu.make_async_remote_copy(
+            src_ref=source,
+            dst_ref=target,
+            send_sem=self.sends.at[slot],
+            recv_sem=self.recvs.at[slot],
+            device_id=device,
+            device_id_type=MESH_ID,
+        )
+
+
+def greet(devices, conditions=()):
+    barrier = pltpu.get_barrier_semaphore()
+    for device in devices:
+        pl.semaphore_signal(barrier, inc=1, device_id=device, device_id_type=MESH_ID)
+    for condition, device in conditions:
+
+        @pl.when(condition)
+        def _():
+            pl.semaphore_signal(barrier, inc=1, device_id=device, device_id_type=MESH_ID)
+
+    count = len(devices)
+    for condition, _ in conditions:
+        count = count + jnp.where(condition, 1, 0)
+    pl.semaphore_wait(barrier, count)
+
+
+def spread_kernel(extent, own, everyone, sends, recvs, local):
+    depth, width = extent
+    row, place = lax.axis_index("dp"), lax.axis_index("seq")
+    links = Links(sends, recvs)
+    others = [
+        (lax.rem(row + up, depth), lax.rem(place + right, width))
+        for up in range(depth)
+        for right in range(width)
+        if up or right
+    ]
+    greet(others)
+    mine = everyone.at[row, place]
+    copies = [links.copy(own, mine, device) for device in others]
+    for copy in copies:
+        copy.start()
+    kept = pltpu.make_async_copy(own, mine, local)
+    kept.start()
+    kept.wait()
+    for copy in copies:
+        copy.wait()
+
+
+def spread(block, extent, collective):
+    count = extent[0] * extent[1] - 1
+    return pl.pallas_call(
+        functools.partial(spread_kernel, extent),
+        out_shape=jax.ShapeDtypeStruct(extent + block.shape, block.dtype),
+        in_specs=[INVMEM],
+        out_specs=INVMEM,
+        scratch_shapes=[
+            pltpu.SemaphoreType.DMA((count,)),
+            pltpu.SemaphoreType.DMA((count,)),
+            pltpu.SemaphoreType.DMA,
+        ],
+        compiler_params=pltpu.CompilerParams(collective_id=collective, has_side_effects=True),
+        name="spread_small",
+    )(block)
+
+
+def plane_rows_kernel(parts, total, landed, sends, recvs):
+    row, place = lax.axis_index("dp"), lax.axis_index("seq")
+    links = Links(sends, recvs)
+    peers = [(row, flip_all(place, mask)) for mask in range(1, 8)]
+    greet(peers)
+    copies = [
+        links.copy(parts.at[peer[1]], landed.at[k], peer) for k, peer in enumerate(peers)
+    ]
+    for copy in copies:
+        copy.start()
+    for copy in copies:
+        copy.wait()
+    result = parts[place].astype(F32)
+    for k in range(7):
+        result = result + landed[k].astype(F32)
+    total[...] = result
+
+
+def plane_rows(parts, collective):
+    return pl.pallas_call(
+        plane_rows_kernel,
+        out_shape=jax.ShapeDtypeStruct(parts.shape[1:], F32),
+        in_specs=[INVMEM],
+        out_specs=INVMEM,
+        scratch_shapes=[
+            pltpu.VMEM((7,) + parts.shape[1:], parts.dtype),
+            pltpu.SemaphoreType.DMA((7,)),
+            pltpu.SemaphoreType.DMA((7,)),
+        ],
+        compiler_params=pltpu.CompilerParams(collective_id=collective, has_side_effects=True),
+        name="plane_rows",
+    )(parts)
+
+
+def add_rows(target, first, second, step=32):
+    def one(number, carry):
+        rows = pl.ds(pl.multiple_of(number * step, step), step)
+        target[rows] = (first[rows].astype(F32) + second[rows].astype(F32)).astype(target.dtype)
+        return carry
+
+    lax.fori_loop(0, target.shape[0] // step, one, 0)
+
+
+def cast_rows(target, source, step=32):
+    def one(number, carry):
+        rows = pl.ds(pl.multiple_of(number * step, step), step)
+        target[rows] = source[rows].astype(target.dtype)
+        return carry
+
+    lax.fori_loop(0, target.shape[0] // step, one, 0)
+
+
+class LineSum:
+    def __init__(self, links, depth, row, place, own, valid, up_in, up_out, down_in, down_out):
+        self.depth, self.row, self.own, self.valid = depth, row, own, valid
+        self.up_in, self.up_out, self.down_in, self.down_out = up_in, up_out, down_in, down_out
+        above, below = lax.min(row + 1, depth - 1), lax.max(row - 1, 0)
+        self.ups = {
+            q: links.copy(up_out.at[q - 1], up_in.at[q - 1], (above, place)) for q in range(1, depth)
+        }
+        self.downs = {
+            q: links.copy(down_out.at[q], down_in.at[q], (below, place)) for q in range(depth - 1)
+        }
+
+    def up(self, q):
+        row = self.row
+
+        @pl.when(self.valid(q) & (row < q))
+        def _():
+            @pl.when(row == 0)
+            def _():
+                cast_rows(self.up_out.at[q - 1], self.own(q))
+
+            @pl.when(row > 0)
+            def _():
+                self.ups[q].wait_recv()
+                add_rows(self.up_out.at[q - 1], self.own(q), self.up_in.at[q - 1])
+
+            self.ups[q].start()
+
+    def down(self, q):
+        row, depth = self.row, self.depth
+
+        @pl.when(self.valid(q) & (row > q))
+        def _():
+            @pl.when(row == depth - 1)
+            def _():
+                cast_rows(self.down_out.at[q], self.own(q))
+
+            @pl.when(row < depth - 1)
+            def _():
+                self.downs[q].wait_recv()
+                add_rows(self.down_out.at[q], self.own(q), self.down_in.at[q])
+
+            self.downs[q].start()
+
+    def step(self, number):
+        up_q, down_q = self.depth - 1 - number, number
+
+        @pl.when(self.row < self.depth // 2)
+        def _():
+            self.up(up_q)
+            self.down(down_q)
+
+        @pl.when(self.row >= self.depth // 2)
+        def _():
+            self.down(down_q)
+            self.up(up_q)
+
+    def finish(self, total):
+        depth, row = self.depth, self.row
+        for q in range(depth):
+
+            @pl.when(self.valid(q) & (row == q))
+            def _():
+                if q > 0:
+                    self.ups[q].wait_recv()
+                if q < depth - 1:
+                    self.downs[q].wait_recv()
+                if 0 < q < depth - 1:
+                    add_rows(total, self.up_in.at[q - 1], self.down_in.at[q])
+                    add_rows(total, total, self.own(q))
+                elif q > 0:
+                    add_rows(total, self.own(q), self.up_in.at[q - 1])
+                else:
+                    add_rows(total, self.own(q), self.down_in.at[q])
+
+    def drain(self):
+        for q, copy in self.ups.items():
+            pl.when(self.valid(q) & (self.row < q))(copy.wait_send)
+        for q, copy in self.downs.items():
+            pl.when(self.valid(q) & (self.row > q))(copy.wait_send)
+
+
+class PlaneSum:
+    def __init__(self, links, row, place, parts, total, pair_in, sums, relay_in, last_in):
+        self.place, self.parts, self.total = place, parts, total
+        self.pair_in, self.sums, self.relay_in, self.last_in = pair_in, sums, relay_in, last_in
+        peer = {mask: (row, flip_all(place, mask)) for mask in range(1, 8)}
+        self.peer = peer
+        rows = total.shape[0] // 2
+        self.halves = (pl.ds(0, rows), pl.ds(rows, rows))
+        self.pair = {
+            mask: links.copy(parts.at[peer[mask ^ 1][1]], pair_in.at[mask // 2], peer[1])
+            for mask in (6, 2, 4, 0)
+        }
+        top, low = self.halves
+        self.relay4 = links.copy(sums.at[3, top], relay_in.at[0], peer[4])
+        self.relay2 = links.copy(sums.at[3, low], relay_in.at[1], peer[2])
+        self.last2 = links.copy(sums.at[1], last_in.at[0], peer[2])
+        self.last4 = links.copy(sums.at[2], last_in.at[1], peer[4])
+
+    def begin(self):
+        for copy in self.pair.values():
+            copy.start()
+
+    def chip(self, mask):
+        index = mask // 2
+        self.pair[mask].wait_recv()
+        mine = self.parts.at[self.peer[mask][1] if mask else self.place]
+        add_rows(self.sums.at[index], mine, self.pair_in.at[index])
+
+    def first(self):
+        self.chip(6)
+        self.relay4.start()
+        self.relay2.start()
+        self.chip(2)
+        self.chip(4)
+        self.chip(0)
+
+    def second(self):
+        top, low = self.halves
+        self.relay4.wait_recv()
+        add_rows(self.sums.at[1, top], self.sums.at[1, top], self.relay_in.at[0])
+        self.last2.start()
+        self.relay2.wait_recv()
+        add_rows(self.sums.at[2, low], self.sums.at[2, low], self.relay_in.at[1])
+        self.last4.start()
+
+    def finish(self):
+        self.last2.wait_recv()
+        self.last4.wait_recv()
+        add_rows(self.total, self.last_in.at[0], self.last_in.at[1])
+        add_rows(self.total, self.total, self.sums.at[0])
+
+    def drain(self):
+        for copy in self.pair.values():
+            copy.wait_send()
+        for copy in (self.relay4, self.relay2, self.last2, self.last4):
+            copy.wait_send()
+
+
+def scatter_kernel(
+    depth,
+    d_parts,
+    o_parts,
+    g_in,
+    g_out,
+    d_total,
+    o_total,
+    in_total,
+    out_total,
+    d_pair,
+    d_sums,
+    d_relay,
+    d_last,
+    o_pair,
+    o_sums,
+    o_relay,
+    o_last,
+    in_up_in,
+    in_up_out,
+    in_down_in,
+    in_down_out,
+    in_sum,
+    in_sent,
+    out_up_in,
+    out_up_out,
+    out_down_in,
+    out_down_out,
+    out_sum,
+    out_far,
+    sends,
+    recvs,
+    local,
+):
+    row, place = lax.axis_index("dp"), lax.axis_index("seq")
+    core = lax.rem(place, 2)
+    half = depth // 2
+    links = Links(sends, recvs)
+    above, below = lax.min(row + 1, depth - 1), lax.max(row - 1, 0)
+    peer = {mask: (row, flip_all(place, mask)) for mask in range(1, 8)}
+    greet(
+        [peer[mask] for mask in range(1, 8)],
+        [(row < depth - 1, (above, place)), (row > 0, (below, place))],
+    )
+    always = row >= 0
+    in_line = LineSum(
+        links,
+        depth,
+        row,
+        place,
+        lambda q: g_in.at[q],
+        lambda q: always,
+        in_up_in,
+        in_up_out,
+        in_down_in,
+        in_down_out,
+    )
+    out_line = LineSum(
+        links,
+        depth,
+        row,
+        place,
+        lambda q: g_out.at[q % half],
+        lambda q: core == q // half,
+        out_up_in,
+        out_up_out,
+        out_down_in,
+        out_down_out,
+    )
+    d_plane = PlaneSum(links, row, place, d_parts, d_total, d_pair, d_sums, d_relay, d_last)
+    o_plane = PlaneSum(links, row, place, o_parts, o_total, o_pair, o_sums, o_relay, o_last)
+    d_plane.begin()
+    o_plane.begin()
+    in_line.step(0)
+    d_plane.first()
+    o_plane.first()
+    d_plane.second()
+    for number in range(1, depth - 1):
+        in_line.step(number)
+    o_plane.second()
+    for number in range(depth - 1):
+        out_line.step(number)
+    d_plane.finish()
+    o_plane.finish()
+    in_line.finish(in_sum)
+    cast_rows(in_sent, in_sum)
+    rows = in_sum.shape[0] // 8
+    mine = in_total.at[place]
+    back = []
+    for mask in (6, 2, 4, 7, 3, 5, 1):
+        target = peer[mask][1]
+        block = in_sent.at[pl.ds(pl.multiple_of(target * rows, rows), rows)]
+        back.append(links.copy(block, mine, peer[mask]))
+        back[-1].start()
+    kept = pltpu.make_async_copy(
+        in_sent.at[pl.ds(pl.multiple_of(place * rows, rows), rows)], mine, local
+    )
+    kept.start()
+    out_line.finish(out_sum)
+    home = lax.div(row, half) == core
+    rows_out = out_total.shape[0]
+    far = links.copy(out_far, out_total, peer[1])
+    for this in range(2):
+
+        @pl.when(home & (core == this))
+        def _():
+            cast_rows(out_far, out_sum.at[pl.ds((1 - this) * rows_out, rows_out)])
+            far.start()
+            cast_rows(out_total, out_sum.at[pl.ds(this * rows_out, rows_out)])
+
+    pl.when(jnp.logical_not(home))(far.wait_recv)
+    pl.when(home)(far.wait_send)
+    kept.wait()
+    for copy in back:
+        copy.wait()
+    d_plane.drain()
+    o_plane.drain()
+    in_line.drain()
+    out_line.drain()
+
+
+def scatter(depth, d_parts, o_parts, g_in, g_out, collective):
+    shape = jax.ShapeDtypeStruct
+    width, rows, model = d_parts.shape
+    in_piece, out_piece = g_in.shape[1:], g_out.shape[1:]
+    plane = [
+        pltpu.VMEM((4, rows, model), BF16),
+        pltpu.VMEM((4, rows, model), BF16),
+        pltpu.VMEM((2, rows // 2, model), BF16),
+        pltpu.VMEM((2, rows, model), BF16),
+    ]
+    return pl.pallas_call(
+        functools.partial(scatter_kernel, depth),
+        out_shape=(
+            shape((rows, model), F32),
+            shape((rows, model), F32),
+            shape((width, in_piece[0] // width, in_piece[1]), BF16),
+            shape((out_piece[0] // 2, out_piece[1]), F32),
+        ),
+        in_specs=[INVMEM] * 4,
+        out_specs=(INVMEM,) * 4,
+        scratch_shapes=plane
+        + plane
+        + [pltpu.VMEM((depth - 1,) + in_piece, BF16)] * 4
+        + [pltpu.VMEM(in_piece, F32), pltpu.VMEM(in_piece, BF16)]
+        + [pltpu.VMEM((depth - 1,) + out_piece, BF16)] * 4
+        + [
+            pltpu.VMEM(out_piece, F32),
+            pltpu.VMEM((out_piece[0] // 2, out_piece[1]), F32),
+            pltpu.SemaphoreType.DMA((64,)),
+            pltpu.SemaphoreType.DMA((64,)),
+            pltpu.SemaphoreType.DMA,
+        ],
+        compiler_params=pltpu.CompilerParams(
+            collective_id=collective, has_side_effects=True, vmem_limit_bytes=VMEM_LIMIT
+        ),
+        name="scatter_plane_and_line",
+    )(d_parts, o_parts, g_in, g_out)
+
+
+def dot(left, right, contract, precision=None):
+    return lax.dot_general(
+        left, right, (contract, ((), ())), precision=precision, preferred_element_type=F32
+    )
+
+
+def mm(left, right):
+    return dot(left, right, ((1,), (0,)))
+
+
+def mm_t(left, right):
+    return dot(left, right, ((1,), (1,)))
+
+
+def t_mm(left, right):
+    return dot(left, right, ((0,), (0,)))
+
+
+def widen(values, heads, head_size):
+    rows = values.shape[0]
+    lane = lax.broadcasted_iota(jnp.int32, (rows, 2 * head_size), 1)
+    parts = []
+    for pair in range(heads // 2):
+        low = jnp.broadcast_to(values[:, 2 * pair : 2 * pair + 1], (rows, 2 * head_size))
+        high = jnp.broadcast_to(values[:, 2 * pair + 1 : 2 * pair + 2], (rows, 2 * head_size))
+        parts.append(jnp.where(lane < head_size, low, high))
+    return jnp.concatenate(parts, axis=1)
+
+
+def sigmoid(values):
+    return 1.0 / (1.0 + jnp.exp(-values))
+
+
+def softplus(values):
+    return jnp.maximum(values, 0.0) + jnp.log1p(jnp.exp(-jnp.abs(values)))
+
+
+def split_pair(values, head_size):
+    lane = lax.broadcasted_iota(jnp.int32, values.shape, 1)
+    zero = jnp.zeros_like(values)
+    return jnp.where(lane < head_size, values, zero), jnp.where(lane < head_size, zero, values)
+
+
+def triangles():
+    rows = lax.broadcasted_iota(jnp.int32, (CHUNK, CHUNK), 0)
+    cols = lax.broadcasted_iota(jnp.int32, (CHUNK, CHUNK), 1)
+    return rows >= cols
+
+
+def head_decays(cum, cum_t, head, causal):
+    gap = cum[:, head : head + 1] - cum_t[head : head + 1, :]
+    return jnp.exp(jnp.where(causal, gap, -1e30))
+
+
+class Line:
+    def __init__(self, links, depth, row, place, blocks, valid=None):
+        self.depth, self.row = depth, row
+        above, below = lax.min(row + 1, depth - 1), lax.max(row - 1, 0)
+        self.steps = []
+        for step in range(depth - 1):
+            up_sent, up_got = row - step, row - 1 - step
+            down_sent, down_got = row + step, row + 1 + step
+            ways = []
+            for sends, shard, gets, got, device in (
+                ((row < depth - 1) & (up_sent >= 0), up_sent, (row > 0) & (up_got >= 0), up_got, above),
+                ((row > 0) & (down_sent < depth), down_sent, (row < depth - 1) & (down_got < depth), down_got, below),
+            ):
+                shard = lax.clamp(0, shard, depth - 1)
+                got = lax.clamp(0, got, depth - 1)
+                if valid is not None:
+                    sends, gets = sends & valid(shard), gets & valid(got)
+                copies = [links.copy(block, block, (device, place)) for block in blocks(shard)]
+                ways.append((sends, gets, copies))
+            self.steps.append(ways)
+
+    def send(self, number):
+        for sends, _, copies in self.steps[number]:
+
+            @pl.when(sends)
+            def _():
+                for copy in copies:
+                    copy.start()
+
+    def wait(self, number):
+        for _, gets, copies in self.steps[number]:
+
+            @pl.when(gets)
+            def _():
+                for copy in copies:
+                    copy.wait_recv()
+
+    def drain(self):
+        for ways in self.steps:
+            for sends, _, copies in ways:
+
+                @pl.when(sends)
+                def _():
+                    for copy in copies:
+                        copy.wait_send()
+
+
+class Pass:
+    def __init__(self, links, peer, place, own, everyone):
+        rows = own.shape[0] // 2
+        mine = everyone.at[place]
+        from2, from4, far = (everyone.at[peer[mask][1]] for mask in (2, 4, 6))
+        top, low = pl.ds(0, rows), pl.ds(rows, rows)
+        self.kept = None
+        self.to2 = links.copy(own, mine, peer[2])
+        self.to4 = links.copy(own, mine, peer[4])
+        self.to1 = links.copy(own, mine, peer[1])
+        self.relay4 = links.copy(from2.at[top], from2.at[top], peer[4])
+        self.relay2 = links.copy(from4.at[low], from4.at[low], peer[2])
+        self.pair2 = links.copy(from2, from2, peer[1])
+        self.pair4 = links.copy(from4, from4, peer[1])
+        self.pair6 = links.copy(far.at[top], far.at[top], peer[1])
+        self.pair7 = links.copy(far.at[low], far.at[low], peer[1])
+
+    def first(self):
+        self.to2.start()
+        self.to4.start()
+        self.to1.start()
+
+    def relay(self):
+        self.to2.wait_recv()
+        self.relay4.start()
+        self.to4.wait_recv()
+        self.relay2.start()
+        self.pair2.start()
+        self.pair4.start()
+
+    def last(self):
+        self.relay4.wait_recv()
+        self.pair6.start()
+        self.relay2.wait_recv()
+        self.pair7.start()
+
+    def end(self):
+        for copy in (self.to1, self.pair2, self.pair4, self.pair6, self.pair7):
+            copy.wait_recv()
+
+    def drain(self):
+        for copy in (
+            self.to2,
+            self.to4,
+            self.to1,
+            self.relay4,
+            self.relay2,
+            self.pair2,
+            self.pair4,
+            self.pair6,
+            self.pair7,
+        ):
+            copy.wait_send()
+
+
+def lay_out(pieces, row, count):
+    tiles = [None] * -(-count * len(pieces) // 128)
+    for index, piece in enumerate(pieces):
+        tile, shift = divmod(index * count, 128)
+        moved = pltpu.roll(piece, shift, 1) if shift else piece
+        lane = lax.broadcasted_iota(jnp.int32, piece.shape, 1)
+        parts = [(tile, jnp.where((lane >= shift) & (lane < shift + count), moved, 0.0))]
+        if shift + count > 128:
+            parts.append((tile + 1, jnp.where(lane < shift + count - 128, moved, 0.0)))
+        for at, part in parts:
+            tiles[at] = part if tiles[at] is None else tiles[at] + part
+    return tiles
+
+
+def channel_windows(ref, place, plane, half, run):
+    core, chip = lax.rem(place, 2), lax.div(place, 2)
+    parts = []
+    for j in range(half):
+        start = ((core * half + j) * plane + chip) * run
+        base = pl.multiple_of(lax.div(start, 128) * 128, 128)
+        window = ref[:, pl.ds(base, run + 64)]
+        moved = pltpu.roll(window, run, 1)
+        parts.append(jnp.where(lax.rem(start, 128) == 0, window, moved)[:, :run])
+    return jnp.concatenate(parts, axis=1)
+
+
+def head_choice(place, plane, half, group, heads):
+    core, chip = lax.rem(place, 2), lax.div(place, 2)
+    head = lax.broadcasted_iota(jnp.int32, (128, 128), 0)
+    lane = lax.broadcasted_iota(jnp.int32, (128, 128), 1)
+    part = sum(((lane >= j * group).astype(jnp.int32) for j in range(1, half)), jnp.zeros_like(lane))
+    chosen = ((core * half + part) * plane + chip) * group + lane - part * group
+    return jnp.where((head == chosen) & (lane < heads), 1.0, 0.0)
+
+
+def forward_kernel(
+    dims,
+    x_own,
+    cot_own,
+    wg_send,
+    wx_send,
+    wb_send,
+    wo_own,
+    pack,
+    head_params,
+    normed_out,
+    cot_out,
+    wg_out,
+    wx_out,
+    wb_out,
+    wo_out,
+    conv_out,
+    pre_out,
+    dt_out,
+    gate_out,
+    y_out,
+    dgn_out,
+    states_out,
+    norms_out,
+    taps_out,
+    rows_out,
+    w_dt_out,
+    x_all,
+    normed_all,
+    cot_all,
+    wg,
+    wx,
+    wb,
+    wo,
+    packs,
+    conv_in,
+    pre_all,
+    dt_all,
+    gate_all,
+    y_all,
+    dgn_all,
+    states,
+    ext,
+    state,
+    full,
+    sums,
+    sums_in,
+    sends,
+    recvs,
+    locals_,
+    stores,
+):
+    depth, width, heads, head_size, size, kernel, own_ch, inner_all = dims
+    half, plane = depth // 2, width // 2
+    inner = heads * head_size
+    run = inner // half
+    model = x_own.shape[1]
+    piece = x_own.shape[0] // 2
+    rows = 2 * piece
+    slots = 2
+    blocks = slots * width // 2
+    row, place = lax.axis_index("dp"), lax.axis_index("seq")
+    core = lax.rem(place, 2)
+    links = Links(sends, recvs)
+    peer = {mask: (row, flip_all(place, mask)) for mask in range(1, width)}
+    line_peers = [(lax.rem(row + up, depth), place) for up in range(1, depth)]
+    greet([peer[mask] for mask in range(1, width)] + line_peers)
+
+    kept = [
+        pltpu.make_async_copy(wx_send.at[place], wx.at[row, place], locals_.at[0]),
+        pltpu.make_async_copy(wb_send.at[core], wb.at[core, row, place], locals_.at[1]),
+        pltpu.make_async_copy(wg_send.at[place], wg.at[row, place], locals_.at[2]),
+        pltpu.make_async_copy(x_own, x_all.at[place], locals_.at[3]),
+        pltpu.make_async_copy(cot_own, cot_all.at[place], locals_.at[4]),
+        pltpu.make_async_copy(pack, packs.at[row, place], locals_.at[5]),
+    ]
+    for copy in kept:
+        copy.start()
+
+    out_home = lax.div(row, half) == core
+    out_block = wo.at[lax.rem(row, half), core]
+    out_kept = pltpu.make_async_copy(wo_own, out_block, locals_.at[6])
+    out_pair = links.copy(wo_own, out_block, peer[1])
+    pl.when(out_home)(out_kept.start)
+    pl.when(jnp.logical_not(out_home))(out_pair.start)
+
+    order = (6, 2, 4, 7, 3, 5, 1)
+    plane_x, plane_g = [], []
+    for mask in order:
+        target = peer[mask][1]
+        its_core = lax.rem(target, 2)
+        plane_x.append(links.copy(wx_send.at[target], wx.at[row, place], peer[mask]))
+        plane_x.append(
+            links.copy(wb_send.at[its_core], wb.at[its_core, row, place], peer[mask])
+        )
+        plane_g.append(links.copy(wg_send.at[target], wg.at[row, place], peer[mask]))
+    for copy in plane_x:
+        copy.start()
+    pack_line = [links.copy(pack, packs.at[row, place], device) for device in line_peers]
+    for copy in pack_line:
+        copy.start()
+    x_pass = Pass(links, peer, place, x_own, x_all)
+    cot_pass = Pass(links, peer, place, cot_own, cot_all)
+    x_pass.first()
+
+    out_line = Line(
+        links,
+        depth,
+        row,
+        place,
+        lambda shard: [wo.at[lax.rem(shard, half)]],
+        lambda shard: lax.div(shard, half) == core,
+    )
+    x_line = Line(links, depth, row, place, lambda shard: [wx.at[shard], wb.at[core, shard]])
+    gate_line = Line(links, depth, row, place, lambda shard: [wg.at[shard]])
+
+    pl.when(out_home)(out_kept.wait)
+    pl.when(out_home)(out_pair.wait_recv)
+    out_line.send(0)
+    kept[0].wait()
+    kept[1].wait()
+    for copy in plane_x:
+        copy.wait_recv()
+    x_line.send(0)
+    kept[5].wait()
+    for copy in pack_line:
+        copy.wait_recv()
+    mine = packs.at[:, place]
+    pack_plane = [links.copy(mine, mine, peer[mask]) for mask in order]
+    for copy in pack_plane:
+        copy.start()
+    for copy in plane_g:
+        copy.start()
+    x_pass.relay()
+    x_line.wait(0)
+    if depth > 2:
+        x_line.send(1)
+    for copy in pack_plane:
+        copy.wait_recv()
+
+    small = [
+        packs[z, s, model // (depth * width) : model // (depth * width) + 16, :].astype(F32)[:8]
+        for z in range(depth)
+        for s in range(width)
+    ]
+    choice = head_choice(place, plane, half, run // head_size, heads)
+    tap_tiles = lay_out(small, 0, own_ch)
+    for at, tile in enumerate(tap_tiles):
+        full[:, at * 128 : (at + 1) * 128] = tile
+    taps_out[:, :inner] = channel_windows(full, place, plane, half, run)
+    taps_out[:, inner:] = full[:, inner_all : inner_all + 2 * size]
+    gate_tiles = lay_out(small, 5, inner_all // (depth * width))
+    for at, tile in enumerate(gate_tiles):
+        full[:, at * 128 : (at + 1) * 128] = tile
+    gate_gain = channel_windows(full, place, plane, half, run)[5:6]
+    norm_tiles = lay_out(small, 6, model // (depth * width))
+    norm_gain = jnp.concatenate([tile[6:7] for tile in norm_tiles], axis=1)
+    chosen = dot(head_params[...], choice, ((1,), (0,)), lax.Precision.HIGHEST)
+    lane = lax.broadcasted_iota(jnp.int32, (1, 128), 1)
+    rates = jnp.where(lane < heads, -jnp.exp(chosen[1:2]), 0.0)
+    skip = widen(chosen[2:3], heads, head_size)
+    dt_rows = packs[:, :, 0 : model // (depth * width), :].reshape(model, 128)
+    w_dt_out[...] = mm(dt_rows, choice.astype(BF16)).astype(BF16)
+    rows_out[...] = jnp.zeros_like(rows_out)
+    rows_out[0:1, :] = norm_gain
+    rows_out[1:2, :inner] = gate_gain
+    rows_out[2:3, :inner] = skip
+    rows_out[3:4, :128] = chosen[0:1]
+    rows_out[4:5, :128] = rates
+
+    x_pass.last()
+    cot_pass.first()
+
+    def normalise(index, carry):
+        for part in range(2):
+            held = x_all[index, part * piece : (part + 1) * piece, :].astype(F32)
+            inv = lax.rsqrt(jnp.mean(held * held, axis=1, keepdims=True) + EPS)
+            normed_all[index, part * piece : (part + 1) * piece, :] = (
+                held * inv * rows_out[0:1, :]
+            ).astype(BF16)
+        return carry
+
+    x_line.wait(1) if depth > 2 else None
+    if depth > 3:
+        x_line.send(2)
+    for copy in plane_g:
+        copy.wait_recv()
+    kept[2].wait()
+    x_pass.end()
+    kept[3].wait()
+    lax.fori_loop(0, width, normalise, 0)
+    if depth > 3:
+        x_line.wait(2)
+    gate_line.send(0)
+    mine_bc = wb.at[core]
+    pair_bc = links.copy(mine_bc, mine_bc, peer[1])
+    pair_bc.start()
+    saves = [pltpu.make_async_copy(normed_all, normed_out, locals_.at[7])]
+    saves[0].start()
+    pair_bc.wait_recv()
+
+    causal = triangles()
+    ones = causal.astype(F32)
+
+    def stored(index):
+        at = pl.ds(pl.multiple_of(index * rows, rows), rows)
+        pairs = [
+            (conv_in.at[at], conv_out.at[at]),
+            (pre_all.at[at], pre_out.at[at]),
+            (dt_all.at[at], dt_out.at[at]),
+            (y_all.at[at], y_out.at[at]),
+            (
+                states.at[pl.ds(index * (rows // CHUNK), rows // CHUNK)],
+                states_out.at[pl.ds(index * (rows // CHUNK), rows // CHUNK)],
+            ),
+        ]
+        return [
+            pltpu.make_async_copy(source, target, stores.at[k, index])
+            for k, (source, target) in enumerate(pairs)
+        ]
+
+    per_slot = blocks // slots
+
+    def scan_block(index, carry):
+        slot, block = lax.div(index, per_slot), lax.rem(index, per_slot)
+        at = pl.multiple_of(index * rows, rows)
+
+        @pl.when(block == 0)
+        def _():
+            ext[0:8, :] = jnp.zeros((8, ext.shape[1]), F32)
+            state[...] = jnp.zeros_like(state)
+
+        tokens = normed_all[
+            pl.ds(2 * block, 2), pl.ds(pl.multiple_of(slot * piece, piece), piece), :
+        ].reshape(rows, model)
+        ext[8:, :inner] = mm(tokens, wx[...].reshape(model, inner))
+        ext[8:, inner : inner + size] = mm(tokens, wb[0].reshape(model, size))
+        ext[8:, inner + size :] = mm(tokens, wb[1].reshape(model, size))
+        dt_arg = mm(tokens, w_dt_out[...]) + rows_out[3:4, :128]
+        dt_all[pl.ds(at, rows), :] = dt_arg
+        pre = taps_out[kernel : kernel + 1, :] + sum(
+            taps_out[k : k + 1, :] * ext[9 - kernel + k : 9 - kernel + k + rows, :]
+            for k in range(kernel)
+        )
+        conv_in[pl.ds(at, rows), :] = ext[8:, :inner]
+        ext[0:8, :] = ext[rows : rows + 8, :]
+        pre_all[pl.ds(at, rows), :] = pre
+        act = pre * sigmoid(pre)
+        dt_block = softplus(dt_arg)
+        steps_block = dt_block * rows_out[4:5, :128]
+        for sub in range(rows // CHUNK):
+            part = slice(sub * CHUNK, (sub + 1) * CHUNK)
+            x = act[part, :inner]
+            b = act[part, inner : inner + size].astype(BF16)
+            c = act[part, inner + size :].astype(BF16)
+            cum = dot(ones, steps_block[part], ((1,), (0,)), lax.Precision.HIGHEST)
+            cum_t = cum.T
+            total = cum[CHUNK - 1 : CHUNK, :]
+            x_dt = x * widen(dt_block[part], heads, head_size)
+            x_dt16 = x_dt.astype(BF16)
+            held = state[...]
+            held16 = held.astype(BF16)
+            states[index * (rows // CHUNK) + sub] = held16
+            y = mm(c, held16) * widen(jnp.exp(cum), heads, head_size)
+            y = y + rows_out[2:3, :inner] * x
+            cb = mm_t(c, b)
+            pieces = []
+            for pair in range(heads // 2):
+                lanes = slice(2 * pair * head_size, 2 * (pair + 1) * head_size)
+                mixing = jnp.concatenate(
+                    [
+                        (head_decays(cum, cum_t, 2 * pair + k, causal) * cb).astype(BF16)
+                        for k in range(2)
+                    ],
+                    axis=1,
+                )
+                pieces.append(
+                    mm(mixing, jnp.concatenate(split_pair(x_dt16[:, lanes], head_size), axis=0))
+                )
+            y_all[pl.ds(pl.multiple_of(at + sub * CHUNK, CHUNK), CHUNK), :] = y + jnp.concatenate(
+                pieces, axis=1
+            )
+            weighted = (x_dt * widen(jnp.exp(total - cum), heads, head_size)).astype(BF16)
+            state[...] = held * widen(jnp.exp(total), heads, head_size) + t_mm(b, weighted)
+        for copy in stored(index):
+            copy.start()
+
+        @pl.when(index == 1)
+        def _():
+            gate_line.wait(0)
+            if depth > 2:
+                gate_line.send(1)
+
+        @pl.when(index == 2)
+        def _():
+            cot_pass.relay()
+
+        if depth > 2:
+
+            @pl.when(index == 4)
+            def _():
+                gate_line.wait(1)
+                if depth > 3:
+                    gate_line.send(2)
+
+        @pl.when(index == 5)
+        def _():
+            cot_pass.last()
+            out_line.wait(0)
+            if depth <= 3 and depth > 2:
+                out_line.send(1)
+
+        if depth > 3:
+
+            @pl.when(index == 6)
+            def _():
+                gate_line.wait(2)
+                out_line.send(1)
+
+        return carry
+
+    lax.fori_loop(0, blocks, scan_block, 0)
+
+    chunk_lane = lax.broadcasted_iota(jnp.int32, (CHUNK, 128), 1)
+    sums[...] = jnp.zeros_like(sums)
+
+    def gate_block(index, carry):
+        slot, block = lax.div(index, per_slot), lax.rem(index, per_slot)
+        at = pl.multiple_of(index * rows, rows)
+        tokens = normed_all[
+            pl.ds(2 * block, 2), pl.ds(pl.multiple_of(slot * piece, piece), piece), :
+        ].reshape(rows, model)
+        gate = mm(tokens, wg[...].reshape(model, inner))
+        gate_all[pl.ds(at, rows), :] = gate
+        gated = y_all[pl.ds(at, rows), :] * (gate * sigmoid(gate))
+        for sub in range(rows // CHUNK):
+            part = gated[sub * CHUNK : (sub + 1) * CHUNK]
+            total = jnp.sum(part * part, axis=1, keepdims=True)
+            sums[...] = jnp.where(chunk_lane == index * (rows // CHUNK) + sub, total, sums[...])
+        if depth > 2:
+
+            @pl.when(index == blocks // 2)
+            def _():
+                out_line.wait(1)
+                if depth > 3:
+                    out_line.send(2)
+
+        return carry
+
+    lax.fori_loop(0, blocks, gate_block, 0)
+    save_gate = pltpu.make_async_copy(gate_all, gate_out, locals_.at[8])
+    save_gate.start()
+    cot_pass.end()
+    kept[4].wait()
+    save_cot = pltpu.make_async_copy(cot_all, cot_out, locals_.at[9])
+    save_cot.start()
+    if depth > 3:
+        out_line.wait(2)
+    save_weights = [
+        pltpu.make_async_copy(source, target, locals_.at[10 + k])
+        for k, (source, target) in enumerate(
+            ((wg, wg_out), (wx, wx_out), (wb, wb_out), (wo, wo_out))
+        )
+    ]
+    for copy in save_weights:
+        copy.start()
+
+    def cot_block(index, carry):
+        slot, block = lax.div(index, per_slot), lax.rem(index, per_slot)
+        at = pl.multiple_of(index * rows, rows)
+        tokens = cot_all[
+            pl.ds(2 * block, 2), pl.ds(pl.multiple_of(slot * piece, piece), piece), :
+        ].reshape(rows, model)
+        dgn = mm_t(tokens, wo[...].reshape(inner, model))
+        dgn_all[pl.ds(at, rows), :] = dgn
+        gate = gate_all[pl.ds(at, rows), :]
+        gated = y_all[pl.ds(at, rows), :] * (gate * sigmoid(gate))
+        cross = dgn * rows_out[1:2, :inner] * gated
+        for sub in range(rows // CHUNK):
+            part = cross[sub * CHUNK : (sub + 1) * CHUNK]
+            total = jnp.sum(part, axis=1, keepdims=True)
+            sums[...] = jnp.where(
+                chunk_lane == 2 * blocks + index * (rows // CHUNK) + sub, total, sums[...]
+            )
+        return carry
+
+    lax.fori_loop(0, blocks, cot_block, 0)
+    save_dgn = pltpu.make_async_copy(dgn_all, dgn_out, locals_.at[14])
+    save_dgn.start()
+    count = 4 * blocks
+    sums_in[0] = sums[...].T[:count]
+    sum_copies = [
+        links.copy(sums_in.at[0], sums_in.at[mask], peer[mask]) for mask in range(1, width)
+    ]
+    for copy in sum_copies:
+        copy.start()
+    for copy in sum_copies:
+        copy.wait_recv()
+    got = [sums_in[mask] for mask in range(width)]
+    while len(got) > 1:
+        got = [got[k] + got[k + 1] for k in range(0, len(got), 2)]
+    squares, cross = got[0][: 2 * blocks], got[0][2 * blocks :]
+    inv_gate = lax.rsqrt(squares / inner_all + EPS)
+    mean = inv_gate * cross / inner_all
+    norms = jnp.concatenate([inv_gate, mean, jnp.zeros((128 - count, 128), F32)], axis=0)
+    norms_out[...] = norms.T
+
+    for copies in (plane_x, plane_g, pack_line, pack_plane, sum_copies, [pair_bc]):
+        for copy in copies:
+            copy.wait_send()
+    pl.when(jnp.logical_not(out_home))(out_pair.wait_send)
+    for line in (out_line, x_line, gate_line):
+        line.drain()
+    x_pass.drain()
+    cot_pass.drain()
+    for copy in saves + [save_gate, save_cot, save_dgn] + save_weights:
+        copy.wait()
+
+    def stores_end(index, carry):
+        for copy in stored(index):
+            copy.wait()
+        return carry
+
+    lax.fori_loop(0, blocks, stores_end, 0)
+
+
+def forward(dims, x_own, cot_own, wg_send, wx_send, wb_send, wo_own, pack, head_params, collective):
+    depth, width, heads, head_size, size, kernel, own_ch, inner_all = dims
+    inner = heads * head_size
+    rows, model = x_own.shape
+    tokens = rows * width
+    wide = inner + 2 * size
+    shape = jax.ShapeDtypeStruct
+    chunks = tokens // CHUNK
+    weights = [
+        ((depth,) + wg_send.shape, BF16),
+        ((depth,) + wx_send.shape, BF16),
+        ((2, depth, width) + wb_send.shape[1:], BF16),
+        ((depth // 2, 2) + wo_own.shape, BF16),
+    ]
+    kept = [
+        ((tokens, inner), F32),
+        ((tokens, wide), F32),
+        ((tokens, 128), F32),
+        ((tokens, inner), F32),
+        ((tokens, inner), F32),
+        ((tokens, inner), F32),
+        ((chunks, size, inner), BF16),
+    ]
+    in_hbm = [((width, rows, model), BF16)] * 2 + weights + kept
+    in_vmem = [((CHUNK, 128), F32), ((8, wide), F32), ((8, model), F32), ((model, 128), BF16)]
+    return pl.pallas_call(
+        functools.partial(forward_kernel, dims),
+        out_shape=tuple(shape(*s) for s in in_hbm + in_vmem),
+        in_specs=[INVMEM] * 8,
+        out_specs=(ANY,) * len(in_hbm) + (INVMEM,) * len(in_vmem),
+        scratch_shapes=[pltpu.VMEM((width, rows, model), BF16)] * 3
+        + [pltpu.VMEM(*s) for s in weights]
+        + [pltpu.VMEM((depth, width) + pack.shape, BF16)]
+        + [pltpu.VMEM(*s) for s in kept]
+        + [
+            pltpu.VMEM((rows + 8, wide), F32),
+            pltpu.VMEM((size, inner), F32),
+            pltpu.VMEM((8, -(-own_ch * depth * width // 128) * 128), F32),
+            pltpu.VMEM((CHUNK, 128), F32),
+            pltpu.VMEM((width, 2 * chunks, 128), F32),
+            pltpu.SemaphoreType.DMA((112,)),
+            pltpu.SemaphoreType.DMA((112,)),
+            pltpu.SemaphoreType.DMA((16,)),
+            pltpu.SemaphoreType.DMA((5, tokens // rows)),
+        ],
+        compiler_params=pltpu.CompilerParams(
+            collective_id=collective, has_side_effects=True, vmem_limit_bytes=VMEM_LIMIT
+        ),
+        name="forward_fused",
+    )(x_own, cot_own, wg_send, wx_send, wb_send, wo_own, pack, head_params)
+
+
+def backward_kernel(
+    heads,
+    head_size,
+    blocks,
+    cot,
+    y_in,
+    gate_in,
+    dgn_in,
+    pre_in,
+    conv_in,
+    dt_in,
+    states,
+    norms,
+    w_out,
+    taps,
+    gains,
+    head_rows,
+    head_sum,
+    o_parts,
+    d_proj,
+    d_bc,
+    d_arg_out,
+    g_out,
+    channel_sums,
+    head_sums,
+    later,
+    d_ext,
+):
+    inner = heads * head_size
+    slot, step = pl.program_id(0), pl.program_id(1)
+    rows = y_in.shape[0]
+    size = (pre_in.shape[1] - inner) // 2
+
+    @pl.when(step == 0)
+    def _():
+        later[...] = jnp.zeros_like(later)
+        d_ext[rows:, :] = jnp.zeros((8, inner), F32)
+
+    @pl.when((step == 0) & (slot == 0))
+    def _():
+        g_out[...] = jnp.zeros_like(g_out)
+        channel_sums[...] = jnp.zeros_like(channel_sums)
+        head_sums[...] = jnp.zeros_like(head_sums)
+
+    gate = gate_in[...]
+    gate_sig = sigmoid(gate)
+    gate_act = gate * gate_sig
+    y = y_in[...]
+    inv = norms[:, 0:1]
+    mean = norms[:, 1:2]
+    hat = y * gate_act * inv
+    gate_normed = (hat * gains[0:1, :]).astype(BF16)
+    o_parts[...] = mm(gate_normed, w_out[...]).astype(BF16).reshape(o_parts.shape)
+    cot_rows = cot[...].reshape(rows, cot.shape[2])
+    g_out[...] += t_mm(gate_normed, cot_rows)
+    d_gated = inv * (dgn_in[...] * gains[0:1, :] - hat * mean)
+    d_y_all = d_gated * gate_act
+    d_proj[:, :inner] = (d_gated * y * gate_sig * (1.0 + gate * (1.0 - gate_sig))).astype(BF16)
+
+    pre = pre_in[...]
+    pre_sig = sigmoid(pre)
+    act = pre * pre_sig
+    slope = pre_sig[:, :inner] * (1.0 + pre[:, :inner] * (1.0 - pre_sig[:, :inner]))
+    dt_arg = dt_in[...]
+    dt_all = softplus(dt_arg)
+    steps_all = dt_all * head_rows[1:2, :]
+    causal = triangles()
+    ones = causal.astype(F32)
+    before = 1.0 - ones.T
+
+    def head_totals(values):
+        return dot(values, head_sum[...], ((1,), (0,)), lax.Precision.HIGHEST)
+
+    for sub in reversed(range(rows // CHUNK)):
+        part = slice(sub * CHUNK, (sub + 1) * CHUNK)
+        x = act[part, :inner]
+        b = act[part, inner : inner + size].astype(BF16)
+        c = act[part, inner + size :].astype(BF16)
+        dt = dt_all[part]
+        cum = dot(ones, steps_all[part], ((1,), (0,)), lax.Precision.HIGHEST)
+        cum_t = cum.T
+        total = cum[CHUNK - 1 : CHUNK, :]
+        dt_wide = widen(dt, heads, head_size)
+        x_dt = x * dt_wide
+        x_dt16 = x_dt.astype(BF16)
+        d_y = d_y_all[part]
+        d_y16 = d_y.astype(BF16)
+        cum_wide = widen(jnp.exp(cum), heads, head_size)
+        d_read = (d_y * cum_wide).astype(BF16)
+        out_wide = widen(jnp.exp(total - cum), heads, head_size)
+        held16 = states[sub]
+        read = mm(c, held16) * cum_wide
+        grown = later[...]
+        grown16 = grown.astype(BF16)
+        d_x_later = out_wide * mm(b, grown16)
+        d_b = mm_t(grown16, (x_dt * out_wide).astype(BF16))
+        d_c = mm_t(held16, d_read)
+        later[...] = grown * widen(jnp.exp(total), heads, head_size) + t_mm(c, d_read)
+        cb = mm_t(c, b)
+        d_cb = jnp.zeros((CHUNK, CHUNK), F32)
+        pieces = []
+        for pair in range(heads // 2):
+            lanes = slice(2 * pair * head_size, 2 * (pair + 1) * head_size)
+            d_y_split = split_pair(d_y16[:, lanes], head_size)
+            mixing = []
+            for k in range(2):
+                decay = head_decays(cum, cum_t, 2 * pair + k, causal)
+                mixing.append((decay * cb).astype(BF16))
+                d_cb = d_cb + decay * mm_t(d_y_split[k], x_dt16[:, lanes])
+            pieces.append(
+                t_mm(jnp.concatenate(mixing, axis=0), jnp.concatenate(d_y_split, axis=0))
+            )
+        d_x_near = jnp.concatenate(pieces, axis=1)
+        d_x_dt = d_x_later + d_x_near
+        d_cb16 = d_cb.astype(BF16)
+        d_b = d_b + t_mm(c, d_cb16)
+        d_c = d_c + dot(b, d_cb16, ((0,), (1,)))
+        d_bc[:size, part] = d_b.astype(BF16)
+        d_bc[size:, part] = d_c.astype(BF16)
+        skip = gains[1:2, :]
+        d_x = d_x_dt * dt_wide + skip * d_y
+        near = y[part] - skip * x - read
+        cross_wide = (
+            d_y * read + d_y16.astype(F32) * near - x_dt16.astype(F32) * d_x_near
+        )
+        d_dt_direct = head_totals(x * d_x_dt)
+        d_cum = head_totals(cross_wide)
+        through = head_totals(x_dt * d_x_later)
+        over = head_totals(
+            jnp.broadcast_to(jnp.sum(grown * held16.astype(F32), axis=0, keepdims=True), (8, inner))
+        )
+        d_log = (
+            dot(ones, d_cum, ((0,), (0,)), lax.Precision.HIGHEST)
+            + dot(before, through, ((1,), (0,)), lax.Precision.HIGHEST)
+            + over[0:1, :] * jnp.exp(total)
+        )
+        d_dt = d_dt_direct + head_rows[1:2, :] * d_log
+        d_arg = d_dt * sigmoid(dt_arg[part])
+        d_arg_out[part, :] = d_arg.astype(BF16)
+        head_sums[0:1, :] += jnp.sum(d_arg, axis=0, keepdims=True)
+        head_sums[1:2, :] += jnp.sum(d_log * dt, axis=0, keepdims=True)
+        channel_sums[5:6, :] += jnp.sum(d_y * x, axis=0, keepdims=True)
+        d_ext[part, :] = d_x * slope[part]
+
+    kernel = 4
+    d_conv = jnp.zeros((rows, inner), F32)
+    x_in = conv_in[...]
+    for k in range(kernel):
+        moved = d_ext[kernel - 1 - k : kernel - 1 - k + rows, :]
+        d_conv = d_conv + taps[k : k + 1, :inner] * moved
+        channel_sums[k : k + 1, :] += jnp.sum(moved * x_in, axis=0, keepdims=True)
+    channel_sums[4:5, :] += jnp.sum(d_ext[0:rows, :], axis=0, keepdims=True)
+    d_proj[:, inner:] = d_conv.astype(BF16)
+    d_ext[rows:, :] = d_ext[0:8, :]
+
+
+def weight_kernel(normed, d_proj, d_small, w_cat, d_parts, g_in):
+    step = pl.program_id(0) * pl.num_programs(1) + pl.program_id(1)
+
+    @pl.when(step == 0)
+    def _():
+        g_in[...] = jnp.zeros_like(g_in)
+
+    rows = d_proj.shape[0]
+    wide = d_proj.shape[1]
+    tokens = normed[...].reshape(rows, normed.shape[2])
+    g_in[:, :wide] += t_mm(tokens, d_proj[...])
+    g_in[:, wide:] += t_mm(tokens, d_small[...])
+    both = jnp.concatenate([d_proj[...], d_small[...]], axis=1)
+    d_parts[...] = mm_t(both, w_cat[...]).astype(BF16).reshape(d_parts.shape)
+
+
+def fast_body(
+    depth,
+    width,
+    block_input,
+    cotangent,
+    lengths,
+    in_weight,
+    out_weight,
+    norm_gain,
+    gate_gain,
+    conv_weight,
+    conv_bias,
+    dt_bias,
+    a_log,
+    d_skip,
+):
+    slots, piece, model = block_input.shape
+    heads_all = dt_bias.shape[0]
+    out_rows = out_weight.shape[0]
+    in_rows = in_weight.shape[0]
+    inner_all = out_rows * depth * width
+    head_size = inner_all // heads_all
+    taps_count = conv_weight.shape[0]
+    channels = conv_weight.shape[1] * depth * width
+    size = (channels - inner_all) // 2
+    heads = heads_all // width
+    inner = heads * head_size
+    plane = width // 2
+    half = depth // 2
+    pair_rows = 2 * out_rows
+    row, place = lax.axis_index("dp"), lax.axis_index("seq")
+    core, chip = lax.rem(place, 2), lax.div(place, 2)
+    slot_len = piece * width
+    tokens = slots * slot_len
+
+    def by_owner(values, axis):
+        shape = values.shape
+        return values.reshape(shape[:axis] + (2, half, plane, pair_rows) + shape[axis + 1 :])
+
+    def mine(values):
+        split = by_owner(values, values.ndim - 1)
+        at = values.ndim - 1
+        split = lax.dynamic_index_in_dim(split, core, at, False)
+        split = lax.dynamic_index_in_dim(split, chip, at + 1, False)
+        return split.reshape(values.shape[:-1] + (inner,))
+
+    def my_heads(values):
+        group = pair_rows // head_size
+        at = values.ndim - 1
+        split = values.reshape(values.shape[:-1] + (2, half, plane, group))
+        split = lax.dynamic_index_in_dim(split, core, at, False)
+        split = lax.dynamic_index_in_dim(split, chip, at + 1, False)
+        return split.reshape(values.shape[:-1] + (heads,))
+
+    gate_cols = inner_all
+    conv_cols = gate_cols + inner_all
+    bc_cols = conv_cols + 2 * size
+    own_ch = conv_bias.shape[0]
+
+    def padded(values, lanes=128):
+        return jnp.pad(values, ((0, 0), (0, lanes - values.shape[1])))
+
+    def placed(values, top):
+        return jnp.pad(
+            values, ((top, 16 + in_rows - top - values.shape[0]), (0, 128 - values.shape[1]))
+        )
+
+    pack = (
+        placed(in_weight[:, bc_cols:], 0)
+        + placed(conv_weight, in_rows)
+        + placed(conv_bias[None], in_rows + taps_count)
+        + placed(gate_gain[None], in_rows + 5)
+        + placed(norm_gain[None], in_rows + 6)
+    )
+    head_params = jnp.pad(
+        jnp.stack([dt_bias, a_log, d_skip]), ((0, 5), (0, 128 - heads_all))
+    )
+    input_f = block_input.astype(F32)
+    inv_rms = lax.rsqrt(jnp.mean(input_f * input_f, axis=-1, keepdims=True) + EPS)
+    positions = place * piece + jnp.arange(piece, dtype=jnp.int32)
+    live = (positions[None, :] < lengths[:, None]).astype(BF16)
+    masked = cotangent * live[..., None]
+
+    def cols_for_all(values):
+        split = by_owner(values, 1)
+        return jnp.transpose(split, (3, 1, 0, 2, 4)).reshape(width, in_rows, inner)
+
+    w_bc_send = jnp.swapaxes(in_weight[:, conv_cols:bc_cols].reshape(in_rows, 2, size), 0, 1)
+    tokens_dev = slots * piece
+    dims = (depth, width, heads, head_size, size, taps_count, own_ch, inner_all)
+    (
+        normed_all,
+        cot_all,
+        w_gate,
+        w_x,
+        w_bc,
+        w_out,
+        conv_in,
+        pre,
+        dt_arg,
+        gate,
+        y,
+        dgn,
+        states,
+        norms,
+        taps,
+        param_rows,
+        w_dt,
+    ) = forward(
+        dims,
+        block_input.reshape(tokens_dev, model),
+        masked.reshape(tokens_dev, model),
+        cols_for_all(in_weight[:, :gate_cols]),
+        cols_for_all(in_weight[:, gate_cols:conv_cols]),
+        w_bc_send,
+        out_weight,
+        pack,
+        head_params,
+        2,
+    )
+    w_in = jnp.concatenate([w_gate.reshape(model, inner), w_x.reshape(model, inner)], axis=1)
+    w_bc = w_bc.reshape(2, model, size)
+    w_out = w_out.reshape(inner, model)
+    norm_all = param_rows[0].reshape(1, 1, model)
+    gains = jnp.pad(param_rows[1:3, :inner], ((0, 6), (0, 0)))
+    rates = param_rows[4:5, :heads]
+    head_rows = jnp.pad(param_rows[3:5, :128], ((0, 6), (0, 0)))
+    head_sum = padded((jnp.arange(inner)[:, None] // head_size == jnp.arange(heads)).astype(F32))
+    chunks = tokens // CHUNK
+    norms = padded(jnp.stack([norms.T[:chunks].reshape(-1), norms.T[chunks : 2 * chunks].reshape(-1)], axis=1))
+
+    rows = 2 * piece
+    blocks = slot_len // rows
+    shape = jax.ShapeDtypeStruct
+    wide = inner + 2 * size
+
+    def flat(cols, order):
+        return pl.BlockSpec((rows, cols), lambda s, i: (s * blocks + order(i), 0))
+
+    def by_piece(order):
+        return pl.BlockSpec((2, piece, model), lambda s, i: (order(i), s, 0))
+
+    def whole(values):
+        return pl.BlockSpec(values.shape, lambda s, i: (0,) * values.ndim)
+
+    def ahead(i):
+        return i
+
+    def behind(i):
+        return blocks - 1 - i
+
+    o_parts, d_proj, d_bc, d_arg, g_out, channel_sums, head_sums = pl.pallas_call(
+        functools.partial(backward_kernel, heads, head_size, blocks),
+        grid=(slots, blocks),
+        out_shape=(
+            shape(normed_all.shape, BF16),
+            shape((tokens, 2 * inner), BF16),
+            shape((2 * size, tokens), BF16),
+            shape((tokens, 128), BF16),
+            shape((inner, model), F32),
+            shape((8, inner), F32),
+            shape((8, 128), F32),
+        ),
+        in_specs=[
+            by_piece(behind),
+            flat(inner, behind),
+            flat(inner, behind),
+            flat(inner, behind),
+            flat(wide, behind),
+            flat(inner, behind),
+            flat(128, behind),
+            pl.BlockSpec((rows // CHUNK, size, inner), lambda s, i: (s * blocks + behind(i), 0, 0)),
+            flat(128, behind),
+        ]
+        + [whole(v) for v in (w_out, taps, gains, head_rows, head_sum)],
+        out_specs=(
+            by_piece(behind),
+            flat(2 * inner, behind),
+            pl.BlockSpec((2 * size, rows), lambda s, i: (0, s * blocks + behind(i))),
+            flat(128, behind),
+            pl.BlockSpec((inner, model), lambda s, i: (0, 0)),
+            pl.BlockSpec((8, inner), lambda s, i: (0, 0)),
+            pl.BlockSpec((8, 128), lambda s, i: (0, 0)),
+        ),
+        scratch_shapes=[
+            pltpu.VMEM((size, inner), F32),
+            pltpu.VMEM((rows + 8, inner), F32),
+        ],
+        compiler_params=pltpu.CompilerParams(vmem_limit_bytes=VMEM_LIMIT),
+        name="block_backward",
+    )(
+        cot_all,
+        y,
+        gate,
+        dgn,
+        pre,
+        conv_in,
+        dt_arg,
+        states,
+        norms,
+        w_out,
+        taps,
+        gains,
+        head_rows,
+        head_sum,
+    )
+
+    bc_own = 2 * size // width
+    d_bc_own = plane_rows(d_bc.reshape(width, bc_own, tokens), 4).T
+    pre_own = lax.dynamic_slice_in_dim(pre, inner + place * bc_own, bc_own, 1)
+    sig = jax.nn.sigmoid(pre_own)
+    d_pre = (d_bc_own * sig * (1.0 + pre_own * (1.0 - sig))).reshape(slots, slot_len, bc_own)
+    w_bc_own = lax.dynamic_slice_in_dim(
+        jnp.swapaxes(w_bc, 0, 1).reshape(model, 2 * size), place * bc_own, bc_own, 1
+    )
+    bc_in = mm(
+        jnp.transpose(normed_all.reshape(width, slots, piece, model), (1, 0, 2, 3)).reshape(
+            tokens, model
+        ),
+        w_bc_own,
+    ).reshape(slots, slot_len, bc_own)
+    taps_own = lax.dynamic_slice_in_dim(taps, inner + place * bc_own, bc_own, 1)
+    moved = [
+        jnp.pad(d_pre[:, taps_count - 1 - k :], ((0, 0), (0, taps_count - 1 - k), (0, 0)))
+        for k in range(taps_count)
+    ]
+    d_bc_in = sum(taps_own[k] * moved[k] for k in range(taps_count))
+    bc_sums = jnp.stack(
+        [jnp.sum(moved[k] * bc_in, axis=(0, 1)) for k in range(taps_count)]
+        + [jnp.sum(d_pre, axis=(0, 1))]
+    )
+    d_small = padded(
+        jnp.concatenate(
+            [d_bc_in.reshape(tokens, bc_own).astype(BF16), d_arg[:, :heads]], axis=1
+        )
+    )
+    w_cat = jnp.concatenate(
+        [w_in, padded(jnp.concatenate([w_bc_own, w_dt[:, :heads]], axis=1))], axis=1
+    )
+
+    d_parts, g_in = pl.pallas_call(
+        weight_kernel,
+        grid=(slots, blocks),
+        out_shape=(shape(normed_all.shape, BF16), shape((model, 2 * inner + 128), F32)),
+        in_specs=[by_piece(ahead), flat(2 * inner, ahead), flat(128, ahead), whole(w_cat)],
+        out_specs=(
+            by_piece(ahead),
+            pl.BlockSpec((model, 2 * inner + 128), lambda s, i: (0, 0)),
+        ),
+        compiler_params=pltpu.CompilerParams(vmem_limit_bytes=VMEM_LIMIT),
+        name="weight_backward",
+    )(normed_all, d_proj, d_small, w_cat)
+
+    skip_sum = jnp.sum(channel_sums[5].reshape(heads, head_size), axis=1)
+    head_part = jnp.stack([head_sums[0, :heads], head_sums[1, :heads] * rates[0], skip_sum])
+    small = jnp.concatenate(
+        [
+            jnp.concatenate([channel_sums[:5], bc_sums], axis=1),
+            jnp.pad(head_part, ((0, 0), (0, inner + bc_own - heads))),
+        ],
+        axis=0,
+    )
+    lanes = -(-small.shape[1] // 128) * 128
+    smalls = jnp.sum(spread(padded(small, lanes), (depth, width), 5), axis=0)
+
+    def to_whole(values, group):
+        count = values.shape[1]
+        split = values.reshape(plane, 2, count, half, group)
+        return jnp.transpose(split, (2, 1, 3, 0, 4)).reshape(count, -1)
+
+    conv_x = to_whole(smalls[:, :5, :inner], pair_rows)
+    conv_bc = jnp.swapaxes(smalls[:, :5, inner : inner + bc_own], 0, 1).reshape(5, 2 * size)
+    conv_grads = lax.dynamic_slice_in_dim(
+        jnp.concatenate([conv_x, conv_bc], axis=1), (row * width + place) * own_ch, own_ch, 1
+    )
+    head_grads = to_whole(smalls[:, 5:8, :heads], pair_rows // head_size)
+
+    d_total, o_total, in_total, out_grad = scatter(
+        depth,
+        d_parts,
+        o_parts,
+        g_in.reshape(depth, model // depth, 2 * inner + 128),
+        g_out.reshape(half, pair_rows, model),
+        6,
+    )
+    in_f = in_total.astype(F32)
+
+    def cols_from_all(values):
+        split = values.reshape(plane, 2, in_rows, half, pair_rows)
+        return jnp.transpose(split, (2, 1, 3, 0, 4)).reshape(in_rows, inner_all)
+
+    dt_cols = in_f[:, :, 2 * inner + bc_own : 2 * inner + bc_own + heads]
+    dt_cols = jnp.swapaxes(to_whole(jnp.swapaxes(dt_cols, 1, 1), pair_rows // head_size), 0, 0)
+    in_grad = jnp.concatenate(
+        [
+            cols_from_all(in_f[:, :, :inner]),
+            cols_from_all(in_f[:, :, inner : 2 * inner]),
+            jnp.swapaxes(in_f[:, :, 2 * inner : 2 * inner + bc_own], 0, 1).reshape(
+                in_rows, 2 * size
+            ),
+            dt_cols,
+        ],
+        axis=1,
+    )
+    norm_grad = jnp.sum(in_grad * in_weight.astype(F32), axis=1) / norm_gain.astype(F32)
+    gate_grad = jnp.sum(out_grad * out_weight.astype(F32), axis=1) / gate_gain.astype(F32)
+
+    output = (input_f + o_total.reshape(slots, piece, model)).astype(BF16)
+    in_hat = input_f * inv_rms
+    d_h = d_total.reshape(slots, piece, model) * norm_all.astype(F32)
+    input_grad = inv_rms * (d_h - in_hat * jnp.mean(d_h * in_hat, axis=-1, keepdims=True))
+    input_grad = (input_grad + masked.astype(F32)).astype(BF16)
+    return (
+        output,
+        input_grad,
+        in_grad,
+        out_grad,
+        norm_grad,
+        gate_grad,
+        conv_grads[:4],
+        conv_grads[4],
+        head_grads[0],
+        head_grads[1],
+        head_grads[2],
+    )
+
+
+def heads_fit(depth, width, arrays):
+    block_input, out_weight, dt_bias = arrays[0], arrays[4], arrays[9]
+    pair_rows = 2 * out_weight.shape[0]
+    head_size = out_weight.shape[0] * depth * width // dt_bias.shape[0]
+    return (
+        width == 8
+        and depth % 2 == 0
+        and pair_rows % head_size == 0
+        and (depth // 2 * pair_rows) % 128 == 0
+        and block_input.shape[1] % CHUNK == 0
+        and 2 * head_size == CHUNK
+    )
+
+
 def solution(mesh):
     placed = (
         P("dp", "seq", None),
@@ -404,8 +2034,15 @@
         P(),
         P(),
     )
+    depth, width = mesh.shape["dp"], mesh.shape["seq"]
+
+    def either(*arrays):
+        if heads_fit(depth, width, arrays):
+            return fast_body(depth, width, *arrays)
+        return body(*arrays)
+
     return jax.shard_map(
-        body,
+        either,
         mesh=mesh,
         in_specs=placed,
         out_specs=(

time: 2270 us -> 382 us (0.17)
  waiting for transfers between devices: 1260 us -> 0 us
  Pallas kernels: 0 us -> 316 us
  local copies, waits for them, and re-layouts: 276 us -> 40.6 us
  blocking collectives: 224 us -> 0 us
  matrix products: 191 us -> 2.07 us
  other arithmetic: 192 us -> 21 us
  starting transfers between devices: 84.3 us -> 0 us
    all_to_all x12 -> x0, waiting for transfers between devices: 1130 us -> none  [the longest x1 825 us: owner_sums(): lax.all_to_all(lifted[0], 'dp', split_axis=1, concat_axis=0, tiled=True)]
    pallas_call x0 -> x6, Pallas kernels: none -> 316 us  [the longest x1 105 us: scatter(): pl.pallas_call(functools.partial(scatter_kernel, depth), out_shape=(shape...]
    dot_general x34 -> x1, matrix products: 191 us -> 2.07 us  [dot(): lax.dot_general(left, right, (contract, ((), ())), precision=precision, p...]
    broadcast_in_dim x5 -> x0, local copies, waits for them, and re-layouts: 140 us -> none  [the longest x3 111 us: owner_sums(): lifted = tuple((grad[None] for grad in grads))]
    all_gather x6 -> x0, waiting for transfers between devices: 137 us -> none  [the longest x4 81.6 us: carried_in(): lax.all_gather(a.astype(kind), axis)]
    psum x1 -> x0, blocking collectives: 131 us -> none  [body(): head_sums = lax.psum(head_totals, ('dp', 'seq'))]
    unnamed x343 -> x34, local copies, waits for them, and re-layouts: 96.5 us -> 2.88 us
    all_to_all x12 -> x0, starting transfers between devices: 71.3 us -> none  [the longest x1 14.2 us: owner_sums(): lax.all_to_all(lifted[0], 'dp', split_axis=1, concat_axis=0, tiled=True)]
  transfers between devices with their start and end apart: 22 -> 0, of which waited for: 9 -> 0; matrix products, arithmetic and copies ran while one was open for 25% -> 0% of each run, Pallas kernels for 0% -> 0%
where the time goes in v1:
time: 382 us; the launch traced here: 381 us
  Pallas kernels  316 us (83%)
  local copies, waits for them, and re-layouts  40.6 us (11%)
  other arithmetic  21 us (5%)
    pallas_call x1, Pallas kernels, scatter(): pl.pallas_call(functools.partial(scatter_kernel, depth), out_shape=(shape...  105 us
    pallas_call x1, Pallas kernels, forward(): pl.pallas_call(functools.partial(forward_kernel, dims), out_shape=tuple((...  98.9 us
    pallas_call x1, Pallas kernels, fast_body(): pl.pallas_call(functools.partial(backward_kernel, heads, head_size, block...  48.9 us
    pallas_call x1, Pallas kernels, spread(): pl.pallas_call(functools.partial(spread_kernel, extent), out_shape=jax.Sh...  25.8 us
    pallas_call x1, Pallas kernels, fast_body(): pl.pallas_call(weight_kernel, grid=(slots, blocks), out_shape=(shape(norm...  20.3 us
    pallas_call x1, Pallas kernels, plane_rows(): pl.pallas_call(plane_rows_kernel, out_shape=jax.ShapeDtypeStruct(parts.sh...  17.3 us

profile of v1, /device:TPU:9, one launch (start us, length us, event | category | flops | bytes accessed | tf_op | source)
XLA Modules:
  0.0 381.3 jit_solution(9145639035558211079)
XLA Ops:
  0.7 0.8 compare_convert_fusion
  1.5 1.4 fusion.8
  2.9 1.3 select_maximum_fusion.4.head_params
  4.1 0.7 slice.111
  4.8 1.3 pad_add_fusion.pack
  6.2 1.3 bitcast_bitcast_fusion.wb_send
  7.6 0.7 pad_convert_fusion.head_sum
  8.4 0.5 reshape.216
  8.9 0.3 copy.207
  9.2 0.9 reshape.217.wx_send
  10.2 0.5 reshape.214
  10.6 0.3 copy.208
  11.0 0.9 reshape.215.wg_send
  11.9 1.0 broadcast_multiply_fusion
  12.9 98.9 %forward_fused.1 = (bf16[8,256,1536]{2,1,0:T(8,128)(2,1)}, bf16[8,256,1536]{2,1,0:T(8,128)(2,1)}, bf16[4,8,48,384]{3,2,1,0:T(8,128)(2,1)}, bf16[4,8,48,384]{3,2,...) custom-call(bf16[256,1536]{1,0:T(8,128)(2,1)} %bitcast.101, ...), custom_call_target="tpu_custom_call" | custom-call | tf_op jit(solution)/shard_map/forward_fused/pallas_call | solution.py:1482
  111.8 0.7 slice.115
  112.5 0.6 pad.78.head_rows
  113.1 0.7 slice.114
  113.8 0.7 constant_dynamic-slice_fusion.1
  114.5 0.8 slice_reduce_fusion
  115.4 0.6 pad.77.gains
  116.0 1.0 fusion.26
  117.1 6.7 %copy.173 = bf16[2,1536,128]{2,0,1:T(2,128)(2,1)S(1)} copy(bf16[2,1536,128]{2,1,0:T(8,128)(2,1)} %bitcast.123) | data formatting | bytes 1572864 | tf_op jit(solution)/shard_map/reshape | solution.py:1802
  124.0 0.2 constant_dynamic-slice_fusion
  124.2 0.7 copy-done.12
  124.8 0.3 fusion.14
  125.2 0.4 copy-done.10
  125.6 1.8 pad_maximum_fusion.w_cat
  127.4 0.4 copy.165
  127.7 1.0 pad.76.norms
  128.8 48.9 %block_backward.1 = (bf16[8,256,1536]{2,1,0:T(8,128)(2,1)}, bf16[2048,768]{1,0:T(8,128)(2,1)}, bf16[256,2048]{1,0:T(8,128)(2,1)}, bf16[2048,128]{1,0:T(8,128)(2,...) custom-call(bf16[8,256,1536]{2,1,0:T(8,128)(2,1)} %get-tuple-element.42.cot, ...), custom_call_target="tpu_custom_call" | custom-call | tf_op jit(solution)/shard_map/block_backward/pallas_call | solution.py:1832
  177.7 6.0 %copy.166 = f32[2048,640]{0,1:T(8,128)} copy(f32[2048,640]{1,0:T(8,128)} %get-tuple-element.46.pre_in) | data formatting | bytes 10485760 | tf_op jit(solution)/shard_map/forward_fused/pallas_call | solution.py:1482
  183.6 0.7 fusion.28
  184.4 17.3 %plane_rows.1 = f32[32,2048]{1,0:T(8,128)} custom-call(bf16[8,32,2048]{2,1,0:T(8,128)(2,1)} %bitcast.122), custom_call_target="tpu_custom_call" | custom-call | tf_op jit(solution)/shard_map/plane_rows/pallas_call | solution.py:507
  201.7 1.3 fusion.22
  203.6 3.4 copy.180
  207.0 2.1 multiply_reduce_fusion.2
  209.1 0.6 select_maximum_fusion.own
  209.7 25.8 %spread_small.1 = f32[4,8,8,512]{3,2,1,0:T(8,128)} custom-call(f32[8,512]{1,0:T(8,128)} %select_maximum_fusion.own), custom_call_target="tpu_custom_call" | custom-call | tf_op jit(solution)/shard_map/spread_small/pallas_call | solution.py:473
  235.5 1.1 reduce_sum.109
  236.7 0.6 squeeze.17
  237.3 0.6 squeeze.16
  237.9 0.6 squeeze.15
  239.0 0.5 slice_bitcast_fusion.3
  239.6 0.6 slice.137
  240.1 0.3 copy.191
  240.4 1.2 fusion.13.d_small
  241.6 20.3 %weight_backward.1 = (bf16[8,256,1536]{2,1,0:T(8,128)(2,1)}, f32[1536,896]{1,0:T(8,128)}) custom-call(bf16[8,256,1536]{2,1,0:T(8,128)(2,1)} %get-tuple-element.41.normed, bf16[2048,768]{1,0:T(8,128)(2,1)} %get-tuple-element.54.d_proj, bf16[2048,128]{1,0:T(8,128)(2,1)} %fusion.13.d_small, bf16[1536,896]{1,0:T(8,128)(2,1)} %pad_maximum_fusion.w_cat), custom_call_target="tpu_custom_call" | custom-call | tf_op jit(solution)/shard_map/weight_backward/pallas_call | solution.py:1921
  261.9 105.3 %scatter_plane_and_line.1 = (f32[256,1536]{1,0:T(8,128)}, f32[256,1536]{1,0:T(8,128)}, bf16[8,48,896]{2,1,0:T(8,128)(2,1)}, f32[96,1536]{1,0:T(8,128)}) custom-call(bf16[8,256,1536]{2,1,0:T(8,128)(2,1)} %get-tuple-element.61.d_parts, bf16[8,256,1536]{2,1,0:T(8,128)(2,1)} %get-tuple-element.62.o_parts, f32[4,384,896]{2,1,0:T(8,128)} %bitcast.103, ...), custom_call_target="tpu_custom_call" | custom-call | tf_op jit(solution)/shard_map/scatter_plane_and_line/pallas_call | solution.py:811
  367.3 1.4 multiply_reduce_fusion.1
  368.7 0.5 convert_divide_fusion
  369.2 1.8 fusion.2
  371.0 1.7 fusion.6
  373.0 0.9 fusion.24
  373.9 0.6 reshape.230
  374.5 0.5 copy.174
  375.0 0.7 reshape.231
  376.1 0.7 copy-done.6
  376.8 0.6 reshape.232
  377.4 0.5 copy.175
  377.9 0.7 reshape.233
  378.7 1.3 multiply_reduce_fusion
  380.0 0.5 convert_divide_fusion.1
  380.5 0.8 copy.211
  (74 shorter events, 2.5 us)
Async XLA Ops:
  0.6 7.7 %copy-start.4 = (bf16[48,6448]{1,0:T(8,128)(2,1)S(1)}, bf16[48,6448]{1,0:T(8,128)(2,1)}, u32[]{:S(2)}) copy-start(bf16[48,6448]{1,0:T(8,128)(2,1)} %param.15) | copy-start | bytes 1857028
  9.2 2.7 copy-start.3
  123.8 1.0 copy-start.12
  123.9 1.4 copy-start.9
  123.9 1.7 copy-start.10
  183.6 19.3 %copy-start.13 = (f32[8,384]{1,0:T(8,128)S(1)}, f32[8,384]{1,0:T(8,128)}, u32[]{:S(2)}) copy-start(f32[8,384]{1,0:T(8,128)} %get-tuple-element.69) | copy-start | bytes 36868
  209.7 30.7 %copy-start.11 = (bf16[2048,128]{1,0:T(8,128)(2,1)S(1)}, bf16[2048,128]{1,0:T(8,128)(2,1)}, u32[]{:S(2)}) copy-start(bf16[2048,128]{1,0:T(8,128)(2,1)} %get-tuple-element.56) | copy-start | bytes 1572868
  261.9 105.4 %copy-start.8 = (bf16[96,1536]{1,0:T(8,128)(2,1)S(1)}, bf16[96,1536]{1,0:T(8,128)(2,1)}, u32[]{:S(2)}) copy-start(bf16[96,1536]{1,0:T(8,128)(2,1)} %wo_own.1) | copy-start | bytes 884740
  261.9 106.8 %copy-start.14 = (bf16[96]{0:T(256)(128)(2,1)S(1)}, bf16[96]{0:T(256)(128)(2,1)}, u32[]{:S(2)}) copy-start(bf16[96]{0:T(256)(128)(2,1)} %param.18) | copy-start | bytes 580
  261.9 107.3 %copy-start = (bf16[2,128,1536]{2,1,0:T(8,128)(2,1)S(1)}, bf16[2,128,1536]{2,1,0:T(8,128)(2,1)}, u32[]{:S(2)}) copy-start(bf16[2,128,1536]{2,1,0:T(8,128)(2,1)} %param.12) | copy-start | bytes 2359300
  367.2 3.7 copy-start.1
  367.3 3.7 copy-start.7
  371.0 1.7 copy-start.2
  375.7 1.1 copy-start.6
  378.6 1.3 copy-start.15
  378.6 1.8 copy-start.5

commit v2 on v1

--- a/solution.py
+++ b/solution.py
@@ -398,7 +398,7 @@
 MESH_ID = pl.DeviceIdType.MESH
 ANY = pl.BlockSpec(memory_space=pl.ANY)
 INVMEM = pl.BlockSpec(memory_space=pltpu.VMEM)
-VMEM_LIMIT = 60 * 1024 * 1024
+VMEM_LIMIT = 63 * 1024 * 1024
 CHUNK = 128
 
 
@@ -446,79 +446,6 @@
     pl.semaphore_wait(barrier, count)
 
 
-def spread_kernel(extent, own, everyone, sends, recvs, local):
-    depth, width = extent
-    row, place = lax.axis_index("dp"), lax.axis_index("seq")
-    links = Links(sends, recvs)
-    others = [
-        (lax.rem(row + up, depth), lax.rem(place + right, width))
-        for up in range(depth)
-        for right in range(width)
-        if up or right
-    ]
-    greet(others)
-    mine = everyone.at[row, place]
-    copies = [links.copy(own, mine, device) for device in others]
-    for copy in copies:
-        copy.start()
-    kept = pltpu.make_async_copy(own, mine, local)
-    kept.start()
-    kept.wait()
-    for copy in copies:
-        copy.wait()
-
-
-def spread(block, extent, collective):
-    count = extent[0] * extent[1] - 1
-    return pl.pallas_call(
-        functools.partial(spread_kernel, extent),
-        out_shape=jax.ShapeDtypeStruct(extent + block.shape, block.dtype),
-        in_specs=[INVMEM],
-        out_specs=INVMEM,
-        scratch_shapes=[
-            pltpu.SemaphoreType.DMA((count,)),
-            pltpu.SemaphoreType.DMA((count,)),
-            pltpu.SemaphoreType.DMA,
-        ],
-        compiler_params=pltpu.CompilerParams(collective_id=collective, has_side_effects=True),
-        name="spread_small",
-    )(block)
-
-
-def plane_rows_kernel(parts, total, landed, sends, recvs):
-    row, place = lax.axis_index("dp"), lax.axis_index("seq")
-    links = Links(sends, recvs)
-    peers = [(row, flip_all(place, mask)) for mask in range(1, 8)]
-    greet(peers)
-    copies = [
-        links.copy(parts.at[peer[1]], landed.at[k], peer) for k, peer in enumerate(peers)
-    ]
-    for copy in copies:
-        copy.start()
-    for copy in copies:
-        copy.wait()
-    result = parts[place].astype(F32)
-    for k in range(7):
-        result = result + landed[k].astype(F32)
-    total[...] = result
-
-
-def plane_rows(parts, collective):
-    return pl.pallas_call(
-        plane_rows_kernel,
-        out_shape=jax.ShapeDtypeStruct(parts.shape[1:], F32),
-        in_specs=[INVMEM],
-        out_specs=INVMEM,
-        scratch_shapes=[
-            pltpu.VMEM((7,) + parts.shape[1:], parts.dtype),
-            pltpu.SemaphoreType.DMA((7,)),
-            pltpu.SemaphoreType.DMA((7,)),
-        ],
-        compiler_params=pltpu.CompilerParams(collective_id=collective, has_side_effects=True),
-        name="plane_rows",
-    )(parts)
-
-
 def add_rows(target, first, second, step=32):
     def one(number, carry):
         rows = pl.ds(pl.multiple_of(number * step, step), step)
@@ -538,15 +465,22 @@
 
 
 class LineSum:
-    def __init__(self, links, depth, row, place, own, valid, up_in, up_out, down_in, down_out):
+    def __init__(
+        self, links, depth, row, place, own, valid, up_in, up_out, down_in, down_out, shared=None
+    ):
         self.depth, self.row, self.own, self.valid = depth, row, own, valid
-        self.up_in, self.up_out, self.down_in, self.down_out = up_in, up_out, down_in, down_out
         above, below = lax.min(row + 1, depth - 1), lax.max(row - 1, 0)
+
+        def slots(ref, shift):
+            return {q: ref.at[q % shared if shared else q - shift] for q in range(shift, depth - 1 + shift)}
+
+        self.up_in, self.up_out = slots(up_in, 1), slots(up_out, 1)
+        self.down_in, self.down_out = slots(down_in, 0), slots(down_out, 0)
         self.ups = {
-            q: links.copy(up_out.at[q - 1], up_in.at[q - 1], (above, place)) for q in range(1, depth)
+            q: links.copy(self.up_out[q], self.up_in[q], (above, place)) for q in self.up_in
         }
         self.downs = {
-            q: links.copy(down_out.at[q], down_in.at[q], (below, place)) for q in range(depth - 1)
+            q: links.copy(self.down_out[q], self.down_in[q], (below, place)) for q in self.down_in
         }
 
     def up(self, q):
@@ -556,12 +490,12 @@
         def _():
             @pl.when(row == 0)
             def _():
-                cast_rows(self.up_out.at[q - 1], self.own(q))
+                cast_rows(self.up_out[q], self.own(q))
 
             @pl.when(row > 0)
             def _():
                 self.ups[q].wait_recv()
-                add_rows(self.up_out.at[q - 1], self.own(q), self.up_in.at[q - 1])
+                add_rows(self.up_out[q], self.own(q), self.up_in[q])
 
             self.ups[q].start()
 
@@ -572,12 +506,12 @@
         def _():
             @pl.when(row == depth - 1)
             def _():
-                cast_rows(self.down_out.at[q], self.own(q))
+                cast_rows(self.down_out[q], self.own(q))
 
             @pl.when(row < depth - 1)
             def _():
                 self.downs[q].wait_recv()
-                add_rows(self.down_out.at[q], self.own(q), self.down_in.at[q])
+                add_rows(self.down_out[q], self.own(q), self.down_in[q])
 
             self.downs[q].start()
 
@@ -605,12 +539,12 @@
                 if q < depth - 1:
                     self.downs[q].wait_recv()
                 if 0 < q < depth - 1:
-                    add_rows(total, self.up_in.at[q - 1], self.down_in.at[q])
+                    add_rows(total, self.up_in[q], self.down_in[q])
                     add_rows(total, total, self.own(q))
                 elif q > 0:
-                    add_rows(total, self.own(q), self.up_in.at[q - 1])
+                    add_rows(total, self.own(q), self.up_in[q])
                 else:
-                    add_rows(total, self.own(q), self.down_in.at[q])
+                    add_rows(total, self.own(q), self.down_in[q])
 
     def drain(self):
         for q, copy in self.ups.items():
@@ -675,166 +609,6 @@
             copy.wait_send()
         for copy in (self.relay4, self.relay2, self.last2, self.last4):
             copy.wait_send()
-
-
-def scatter_kernel(
-    depth,
-    d_parts,
-    o_parts,
-    g_in,
-    g_out,
-    d_total,
-    o_total,
-    in_total,
-    out_total,
-    d_pair,
-    d_sums,
-    d_relay,
-    d_last,
-    o_pair,
-    o_sums,
-    o_relay,
-    o_last,
-    in_up_in,
-    in_up_out,
-    in_down_in,
-    in_down_out,
-    in_sum,
-    in_sent,
-    out_up_in,
-    out_up_out,
-    out_down_in,
-    out_down_out,
-    out_sum,
-    out_far,
-    sends,
-    recvs,
-    local,
-):
-    row, place = lax.axis_index("dp"), lax.axis_index("seq")
-    core = lax.rem(place, 2)
-    half = depth // 2
-    links = Links(sends, recvs)
-    above, below = lax.min(row + 1, depth - 1), lax.max(row - 1, 0)
-    peer = {mask: (row, flip_all(place, mask)) for mask in range(1, 8)}
-    greet(
-        [peer[mask] for mask in range(1, 8)],
-        [(row < depth - 1, (above, place)), (row > 0, (below, place))],
-    )
-    always = row >= 0
-    in_line = LineSum(
-        links,
-        depth,
-        row,
-        place,
-        lambda q: g_in.at[q],
-        lambda q: always,
-        in_up_in,
-        in_up_out,
-        in_down_in,
-        in_down_out,
-    )
-    out_line = LineSum(
-        links,
-        depth,
-        row,
-        place,
-        lambda q: g_out.at[q % half],
-        lambda q: core == q // half,
-        out_up_in,
-        out_up_out,
-        out_down_in,
-        out_down_out,
-    )
-    d_plane = PlaneSum(links, row, place, d_parts, d_total, d_pair, d_sums, d_relay, d_last)
-    o_plane = PlaneSum(links, row, place, o_parts, o_total, o_pair, o_sums, o_relay, o_last)
-    d_plane.begin()
-    o_plane.begin()
-    in_line.step(0)
-    d_plane.first()
-    o_plane.first()
-    d_plane.second()
-    for number in range(1, depth - 1):
-        in_line.step(number)
-    o_plane.second()
-    for number in range(depth - 1):
-        out_line.step(number)
-    d_plane.finish()
-    o_plane.finish()
-    in_line.finish(in_sum)
-    cast_rows(in_sent, in_sum)
-    rows = in_sum.shape[0] // 8
-    mine = in_total.at[place]
-    back = []
-    for mask in (6, 2, 4, 7, 3, 5, 1):
-        target = peer[mask][1]
-        block = in_sent.at[pl.ds(pl.multiple_of(target * rows, rows), rows)]
-        back.append(links.copy(block, mine, peer[mask]))
-        back[-1].start()
-    kept = pltpu.make_async_copy(
-        in_sent.at[pl.ds(pl.multiple_of(place * rows, rows), rows)], mine, local
-    )
-    kept.start()
-    out_line.finish(out_sum)
-    home = lax.div(row, half) == core
-    rows_out = out_total.shape[0]
-    far = links.copy(out_far, out_total, peer[1])
-    for this in range(2):
-
-        @pl.when(home & (core == this))
-        def _():
-            cast_rows(out_far, out_sum.at[pl.ds((1 - this) * rows_out, rows_out)])
-            far.start()
-            cast_rows(out_total, out_sum.at[pl.ds(this * rows_out, rows_out)])
-
-    pl.when(jnp.logical_not(home))(far.wait_recv)
-    pl.when(home)(far.wait_send)
-    kept.wait()
-    for copy in back:
-        copy.wait()
-    d_plane.drain()
-    o_plane.drain()
-    in_line.drain()
-    out_line.drain()
-
-
-def scatter(depth, d_parts, o_parts, g_in, g_out, collective):
-    shape = jax.ShapeDtypeStruct
-    width, rows, model = d_parts.shape
-    in_piece, out_piece = g_in.shape[1:], g_out.shape[1:]
-    plane = [
-        pltpu.VMEM((4, rows, model), BF16),
-        pltpu.VMEM((4, rows, model), BF16),
-        pltpu.VMEM((2, rows // 2, model), BF16),
-        pltpu.VMEM((2, rows, model), BF16),
-    ]
-    return pl.pallas_call(
-        functools.partial(scatter_kernel, depth),
-        out_shape=(
-            shape((rows, model), F32),
-            shape((rows, model), F32),
-            shape((width, in_piece[0] // width, in_piece[1]), BF16),
-            shape((out_piece[0] // 2, out_piece[1]), F32),
-        ),
-        in_specs=[INVMEM] * 4,
-        out_specs=(INVMEM,) * 4,
-        scratch_shapes=plane
-        + plane
-        + [pltpu.VMEM((depth - 1,) + in_piece, BF16)] * 4
-        + [pltpu.VMEM(in_piece, F32), pltpu.VMEM(in_piece, BF16)]
-        + [pltpu.VMEM((depth - 1,) + out_piece, BF16)] * 4
-        + [
-            pltpu.VMEM(out_piece, F32),
-            pltpu.VMEM((out_piece[0] // 2, out_piece[1]), F32),
-            pltpu.SemaphoreType.DMA((64,)),
-            pltpu.SemaphoreType.DMA((64,)),
-            pltpu.SemaphoreType.DMA,
-        ],
-        compiler_params=pltpu.CompilerParams(
-            collective_id=collective, has_side_effects=True, vmem_limit_bytes=VMEM_LIMIT
-        ),
-        name="scatter_plane_and_line",
-    )(d_parts, o_parts, g_in, g_out)
 
 
 def dot(left, right, contract, precision=None):
@@ -1506,72 +1280,295 @@
     )(x_own, cot_own, wg_send, wx_send, wb_send, wo_own, pack, head_params)
 
 
-def backward_kernel(
-    heads,
-    head_size,
-    blocks,
-    cot,
-    y_in,
-    gate_in,
-    dgn_in,
-    pre_in,
-    conv_in,
-    dt_in,
-    states,
+class PlaneRows:
+    def __init__(self, links, row, place, parts, landed):
+        self.place, self.parts, self.landed = place, parts, landed
+        peers = [(row, flip_all(place, mask)) for mask in (6, 7, 2, 3, 4, 5, 1)]
+        self.copies = [
+            links.copy(parts.at[peer[1]], landed.at[k], peer) for k, peer in enumerate(peers)
+        ]
+
+    def begin(self):
+        for copy in self.copies:
+            copy.start()
+
+    def arrived(self):
+        for copy in self.copies:
+            copy.wait_recv()
+
+    def drain(self):
+        for copy in self.copies:
+            copy.wait_send()
+
+
+class SendBack:
+    def __init__(self, links, row, place, sent, back, local):
+        self.rows = back.shape[1]
+        self.sent, self.back, self.place = sent, back, place
+        mine = back.at[place]
+        self.copies = [
+            links.copy(self.block((row, flip_all(place, mask))[1]), mine, (row, flip_all(place, mask)))
+            for mask in (6, 2, 4, 7, 3, 5, 1)
+        ]
+        self.kept = pltpu.make_async_copy(self.block(place), mine, local)
+
+    def block(self, target):
+        return self.sent.at[pl.ds(pl.multiple_of(target * self.rows, self.rows), self.rows)]
+
+    def begin(self):
+        for copy in self.copies:
+            copy.start()
+        self.kept.start()
+
+    def end(self):
+        self.kept.wait()
+        for copy in self.copies:
+            copy.wait()
+
+
+def turn(target, source):
+    for at in range(0, source.shape[0], 128):
+        target[:, at : at + 128] = source[at : at + 128, :].T.astype(target.dtype)
+
+
+def reverse_kernel(
+    dims,
+    cot_hbm,
+    normed_hbm,
+    gate_hbm,
+    y_hbm,
+    dgn_hbm,
+    pre_hbm,
+    conv_hbm,
+    dt_hbm,
+    states_hbm,
+    wo_hbm,
     norms,
-    w_out,
     taps,
-    gains,
-    head_rows,
+    rows_in,
     head_sum,
-    o_parts,
-    d_proj,
-    d_bc,
-    d_arg_out,
-    g_out,
+    d_gate_hbm,
+    d_x_hbm,
+    d_bc_hbm,
+    d_arg_hbm,
+    o_total,
+    gate_back,
+    out_grad,
     channel_sums,
     head_sums,
+    cot_all,
+    normed_all,
+    gate_all,
+    y_all,
+    d_y_all,
+    wo,
+    d_gate,
+    d_x_all,
+    d_bc,
+    d_arg_all,
+    g_out,
+    g_gate,
+    pre_two,
+    conv_two,
+    dt_two,
+    states_two,
     later,
     d_ext,
+    o_pair,
+    o_sums,
+    o_relay,
+    o_last,
+    out_up_in,
+    out_up_out,
+    out_down_in,
+    out_down_out,
+    gate_up_in,
+    gate_up_out,
+    gate_down_in,
+    gate_down_out,
+    out_sum,
+    out_far,
+    gate_sum,
+    gate_sent,
+    sends,
+    recvs,
+    locals_,
+    streams,
 ):
+    depth, width, heads, head_size, size, kernel, own_ch, inner_all = dims
+    half = depth // 2
     inner = heads * head_size
-    slot, step = pl.program_id(0), pl.program_id(1)
-    rows = y_in.shape[0]
-    size = (pre_in.shape[1] - inner) // 2
-
-    @pl.when(step == 0)
-    def _():
-        later[...] = jnp.zeros_like(later)
-        d_ext[rows:, :] = jnp.zeros((8, inner), F32)
-
-    @pl.when((step == 0) & (slot == 0))
-    def _():
-        g_out[...] = jnp.zeros_like(g_out)
-        channel_sums[...] = jnp.zeros_like(channel_sums)
-        head_sums[...] = jnp.zeros_like(head_sums)
-
-    gate = gate_in[...]
-    gate_sig = sigmoid(gate)
-    gate_act = gate * gate_sig
-    y = y_in[...]
-    inv = norms[:, 0:1]
-    mean = norms[:, 1:2]
-    hat = y * gate_act * inv
-    gate_normed = (hat * gains[0:1, :]).astype(BF16)
-    o_parts[...] = mm(gate_normed, w_out[...]).astype(BF16).reshape(o_parts.shape)
-    cot_rows = cot[...].reshape(rows, cot.shape[2])
-    g_out[...] += t_mm(gate_normed, cot_rows)
-    d_gated = inv * (dgn_in[...] * gains[0:1, :] - hat * mean)
-    d_y_all = d_gated * gate_act
-    d_proj[:, :inner] = (d_gated * y * gate_sig * (1.0 + gate * (1.0 - gate_sig))).astype(BF16)
-
-    pre = pre_in[...]
-    pre_sig = sigmoid(pre)
-    act = pre * pre_sig
-    slope = pre_sig[:, :inner] * (1.0 + pre[:, :inner] * (1.0 - pre_sig[:, :inner]))
-    dt_arg = dt_in[...]
-    dt_all = softplus(dt_arg)
-    steps_all = dt_all * head_rows[1:2, :]
+    model = cot_all.shape[2]
+    piece = cot_all.shape[1] // 2
+    rows = 2 * piece
+    slots = 2
+    blocks = slots * width // 2
+    per_slot = blocks // slots
+    subs = rows // CHUNK
+    row, place = lax.axis_index("dp"), lax.axis_index("seq")
+    core = lax.rem(place, 2)
+    links = Links(sends, recvs)
+    above, below = lax.min(row + 1, depth - 1), lax.max(row - 1, 0)
+    peer = {mask: (row, flip_all(place, mask)) for mask in range(1, width)}
+
+    loads = [
+        pltpu.make_async_copy(source, target, locals_.at[k])
+        for k, (source, target) in enumerate(
+            (
+                (y_hbm, y_all),
+                (gate_hbm, gate_all),
+                (cot_hbm, cot_all),
+                (wo_hbm, wo),
+                (dgn_hbm, d_y_all),
+                (normed_hbm, normed_all),
+            )
+        )
+    ]
+    for copy in loads:
+        copy.start()
+
+    def place_of(number):
+        slot = lax.div(number, per_slot)
+        return slot, per_slot - 1 - lax.rem(number, per_slot)
+
+    def fetch(number):
+        slot, block = place_of(number)
+        index = slot * per_slot + block
+        at = pl.ds(pl.multiple_of(index * rows, rows), rows)
+        buffer = lax.rem(number, 2)
+        pairs = (
+            (pre_hbm.at[at], pre_two.at[buffer]),
+            (conv_hbm.at[at], conv_two.at[buffer]),
+            (dt_hbm.at[at], dt_two.at[buffer]),
+            (states_hbm.at[pl.ds(index * subs, subs)], states_two.at[buffer]),
+        )
+        return [
+            pltpu.make_async_copy(source, target, streams.at[buffer, k])
+            for k, (source, target) in enumerate(pairs)
+        ]
+
+    for copy in fetch(0):
+        copy.start()
+    greet(
+        [peer[mask] for mask in range(1, width)],
+        [(row < depth - 1, (above, place)), (row > 0, (below, place))],
+    )
+
+    out_line = LineSum(
+        links,
+        depth,
+        row,
+        place,
+        lambda q: g_out.at[pl.ds((q % half) * (inner // half), inner // half)],
+        lambda q: core == q // half,
+        out_up_in,
+        out_up_out,
+        out_down_in,
+        out_down_out,
+        half,
+    )
+    cols = model // depth
+    gate_line = LineSum(
+        links,
+        depth,
+        row,
+        place,
+        lambda q: g_gate.at[:, pl.ds(q * cols, cols)],
+        lambda q: row >= 0,
+        gate_up_in,
+        gate_up_out,
+        gate_down_in,
+        gate_down_out,
+    )
+    o_plane = PlaneSum(links, row, place, cot_all, o_total, o_pair, o_sums, o_relay, o_last)
+    send_gate = SendBack(links, row, place, gate_sent, gate_back, locals_.at[6])
+
+    chunk_lane = lax.broadcasted_iota(jnp.int32, (CHUNK, 128), 1)
+
+    def column(index, shift):
+        parts = [
+            jnp.sum(
+                jnp.where(chunk_lane == shift + index * subs + sub, norms[...], 0.0),
+                axis=1,
+                keepdims=True,
+            )
+            for sub in range(subs)
+        ]
+        return jnp.concatenate(parts, axis=0)
+
+    def tokens_of(ref, index):
+        slot, block = lax.div(index, per_slot), lax.rem(index, per_slot)
+        return ref.at[pl.ds(2 * block, 2), pl.ds(pl.multiple_of(slot * piece, piece), piece), :]
+
+    gate_gain = rows_in[1:2, :inner]
+    skip = rows_in[2:3, :inner]
+
+    def normed_block(index, carry):
+        at = pl.ds(pl.multiple_of(index * rows, rows), rows)
+        gate = gate_all[at, :]
+        hat = y_all[at, :] * (gate * sigmoid(gate)) * column(index, 0)
+        tokens_of(d_gate, index)[...] = (
+            (hat * gate_gain).astype(BF16).reshape(2, piece, inner)
+        )
+        return carry
+
+    loads[0].wait()
+    loads[1].wait()
+    lax.fori_loop(0, blocks, normed_block, 0)
+
+    everything = slots * width * piece
+
+    def out_grad_tile(number, carry):
+        at = pl.ds(pl.multiple_of(number * 128, 128), 128)
+        left = d_gate[:, :, at].reshape(everything, 128)
+        g_out[at, :] = t_mm(left, cot_all[...].reshape(everything, model))
+        return carry
+
+    loads[2].wait()
+    lax.fori_loop(0, inner // 128, out_grad_tile, 0)
+    out_line.step(0)
+
+    def out_block(index, carry):
+        cot_all[index] = mm(d_gate[index], wo[...].reshape(inner, model)).astype(BF16)
+        return carry
+
+    loads[3].wait()
+    lax.fori_loop(0, width, out_block, 0)
+    o_plane.begin()
+
+    def gate_block(index, carry):
+        at = pl.ds(pl.multiple_of(index * rows, rows), rows)
+        gate = gate_all[at, :]
+        sig = sigmoid(gate)
+        gate_act = gate * sig
+        y = y_all[at, :]
+        inv = column(index, 0)
+        hat = y * gate_act * inv
+        d_gated = inv * (d_y_all[at, :] * gate_gain - hat * column(index, 2 * blocks))
+        d_y_all[at, :] = d_gated * gate_act
+        tokens_of(d_gate, index)[...] = (
+            (d_gated * y * sig * (1.0 + gate * (1.0 - sig))).astype(BF16).reshape(2, piece, inner)
+        )
+        return carry
+
+    loads[4].wait()
+    lax.fori_loop(0, blocks, gate_block, 0)
+    save_gate = pltpu.make_async_copy(d_gate, d_gate_hbm, locals_.at[7])
+    save_gate.start()
+
+    def gate_grad_tile(number, carry):
+        at = pl.ds(pl.multiple_of(number * 128, 128), 128)
+        left = d_gate[:, :, at].reshape(everything, 128)
+        g_gate[at, :] = t_mm(left, normed_all[...].reshape(everything, model))
+        return carry
+
+    loads[5].wait()
+    lax.fori_loop(0, inner // 128, gate_grad_tile, 0)
+    gate_line.step(0)
+    o_plane.first()
+
+    channel_sums[...] = jnp.zeros_like(channel_sums)
+    head_sums[...] = jnp.zeros_like(head_sums)
     causal = triangles()
     ones = causal.astype(F32)
     before = 1.0 - ones.T
@@ -1579,103 +1576,566 @@
     def head_totals(values):
         return dot(values, head_sum[...], ((1,), (0,)), lax.Precision.HIGHEST)
 
-    for sub in reversed(range(rows // CHUNK)):
-        part = slice(sub * CHUNK, (sub + 1) * CHUNK)
-        x = act[part, :inner]
-        b = act[part, inner : inner + size].astype(BF16)
-        c = act[part, inner + size :].astype(BF16)
-        dt = dt_all[part]
-        cum = dot(ones, steps_all[part], ((1,), (0,)), lax.Precision.HIGHEST)
-        cum_t = cum.T
-        total = cum[CHUNK - 1 : CHUNK, :]
-        dt_wide = widen(dt, heads, head_size)
-        x_dt = x * dt_wide
-        x_dt16 = x_dt.astype(BF16)
-        d_y = d_y_all[part]
-        d_y16 = d_y.astype(BF16)
-        cum_wide = widen(jnp.exp(cum), heads, head_size)
-        d_read = (d_y * cum_wide).astype(BF16)
-        out_wide = widen(jnp.exp(total - cum), heads, head_size)
-        held16 = states[sub]
-        read = mm(c, held16) * cum_wide
-        grown = later[...]
-        grown16 = grown.astype(BF16)
-        d_x_later = out_wide * mm(b, grown16)
-        d_b = mm_t(grown16, (x_dt * out_wide).astype(BF16))
-        d_c = mm_t(held16, d_read)
-        later[...] = grown * widen(jnp.exp(total), heads, head_size) + t_mm(c, d_read)
-        cb = mm_t(c, b)
-        d_cb = jnp.zeros((CHUNK, CHUNK), F32)
-        pieces = []
-        for pair in range(heads // 2):
-            lanes = slice(2 * pair * head_size, 2 * (pair + 1) * head_size)
-            d_y_split = split_pair(d_y16[:, lanes], head_size)
-            mixing = []
-            for k in range(2):
-                decay = head_decays(cum, cum_t, 2 * pair + k, causal)
-                mixing.append((decay * cb).astype(BF16))
-                d_cb = d_cb + decay * mm_t(d_y_split[k], x_dt16[:, lanes])
-            pieces.append(
-                t_mm(jnp.concatenate(mixing, axis=0), jnp.concatenate(d_y_split, axis=0))
+    def scan_block(number, carry):
+        slot, block = place_of(number)
+        index = slot * per_slot + block
+        buffer = lax.rem(number, 2)
+        for copy in fetch(number):
+            copy.wait()
+
+        @pl.when(number + 1 < blocks)
+        def _():
+            for copy in fetch(number + 1):
+                copy.start()
+
+        @pl.when(block == per_slot - 1)
+        def _():
+            later[...] = jnp.zeros_like(later)
+            d_ext[rows:, :] = jnp.zeros((8, inner), F32)
+
+        pre = pre_two[buffer]
+        pre_sig = sigmoid(pre)
+        act = pre * pre_sig
+        slope = pre_sig[:, :inner] * (1.0 + pre[:, :inner] * (1.0 - pre_sig[:, :inner]))
+        dt_arg = dt_two[buffer]
+        dt_block = softplus(dt_arg)
+        rates = rows_in[4:5, :128]
+        steps_block = dt_block * rates
+        for sub in reversed(range(subs)):
+            part = slice(sub * CHUNK, (sub + 1) * CHUNK)
+            at = pl.ds(pl.multiple_of(index * rows + sub * CHUNK, CHUNK), CHUNK)
+            x = act[part, :inner]
+            b = act[part, inner : inner + size].astype(BF16)
+            c = act[part, inner + size :].astype(BF16)
+            dt = dt_block[part]
+            cum = dot(ones, steps_block[part], ((1,), (0,)), lax.Precision.HIGHEST)
+            cum_t = cum.T
+            total = cum[CHUNK - 1 : CHUNK, :]
+            dt_wide = widen(dt, heads, head_size)
+            x_dt = x * dt_wide
+            x_dt16 = x_dt.astype(BF16)
+            d_y = d_y_all[at, :]
+            d_y16 = d_y.astype(BF16)
+            cum_wide = widen(jnp.exp(cum), heads, head_size)
+            d_read = (d_y * cum_wide).astype(BF16)
+            out_wide = widen(jnp.exp(total - cum), heads, head_size)
+            held16 = states_two[buffer, sub]
+            read = mm(c, held16) * cum_wide
+            grown = later[...]
+            grown16 = grown.astype(BF16)
+            d_x_later = out_wide * mm(b, grown16)
+            d_b = mm_t(grown16, (x_dt * out_wide).astype(BF16))
+            d_c = mm_t(held16, d_read)
+            later[...] = grown * widen(jnp.exp(total), heads, head_size) + t_mm(c, d_read)
+            cb = mm_t(c, b)
+            d_cb = jnp.zeros((CHUNK, CHUNK), F32)
+            pieces = []
+            for pair in range(heads // 2):
+                lanes = slice(2 * pair * head_size, 2 * (pair + 1) * head_size)
+                d_y_split = split_pair(d_y16[:, lanes], head_size)
+                mixing = []
+                for k in range(2):
+                    decay = head_decays(cum, cum_t, 2 * pair + k, causal)
+                    mixing.append((decay * cb).astype(BF16))
+                    d_cb = d_cb + decay * mm_t(d_y_split[k], x_dt16[:, lanes])
+                pieces.append(
+                    t_mm(jnp.concatenate(mixing, axis=0), jnp.concatenate(d_y_split, axis=0))
+                )
+            d_x_near = jnp.concatenate(pieces, axis=1)
+            d_x_dt = d_x_later + d_x_near
+            d_cb16 = d_cb.astype(BF16)
+            d_b = d_b + t_mm(c, d_cb16)
+            d_c = d_c + dot(b, d_cb16, ((0,), (1,)))
+            d_bc[:size, at] = d_b.astype(BF16)
+            d_bc[size:, at] = d_c.astype(BF16)
+            d_x = d_x_dt * dt_wide + skip * d_y
+            near = y_all[at, :] - skip * x - read
+            cross_wide = d_y * read + d_y16.astype(F32) * near - x_dt16.astype(F32) * d_x_near
+            d_dt_direct = head_totals(x * d_x_dt)
+            d_cum = head_totals(cross_wide)
+            through = head_totals(x_dt * d_x_later)
+            over = head_totals(
+                jnp.broadcast_to(
+                    jnp.sum(grown * held16.astype(F32), axis=0, keepdims=True), (8, inner)
+                )
             )
-        d_x_near = jnp.concatenate(pieces, axis=1)
-        d_x_dt = d_x_later + d_x_near
-        d_cb16 = d_cb.astype(BF16)
-        d_b = d_b + t_mm(c, d_cb16)
-        d_c = d_c + dot(b, d_cb16, ((0,), (1,)))
-        d_bc[:size, part] = d_b.astype(BF16)
-        d_bc[size:, part] = d_c.astype(BF16)
-        skip = gains[1:2, :]
-        d_x = d_x_dt * dt_wide + skip * d_y
-        near = y[part] - skip * x - read
-        cross_wide = (
-            d_y * read + d_y16.astype(F32) * near - x_dt16.astype(F32) * d_x_near
+            d_log = (
+                dot(ones, d_cum, ((0,), (0,)), lax.Precision.HIGHEST)
+                + dot(before, through, ((1,), (0,)), lax.Precision.HIGHEST)
+                + over[0:1, :] * jnp.exp(total)
+            )
+            d_dt = d_dt_direct + rates * d_log
+            d_arg = d_dt * sigmoid(dt_arg[part])
+            d_arg_all[2 * block + sub, pl.ds(pl.multiple_of(slot * piece, piece), piece), :] = (
+                d_arg.astype(BF16)
+            )
+            head_sums[0:1, :] += jnp.sum(d_arg, axis=0, keepdims=True)
+            head_sums[1:2, :] += jnp.sum(d_log * dt, axis=0, keepdims=True) * rates
+            channel_sums[5:6, :] += jnp.sum(d_y * x, axis=0, keepdims=True)
+            d_ext[part, :] = d_x * slope[part]
+
+        d_conv = jnp.zeros((rows, inner), F32)
+        x_in = conv_two[buffer]
+        for k in range(kernel):
+            moved = d_ext[kernel - 1 - k : kernel - 1 - k + rows, :]
+            d_conv = d_conv + taps[k : k + 1, :inner] * moved
+            channel_sums[k : k + 1, :] += jnp.sum(moved * x_in, axis=0, keepdims=True)
+        channel_sums[4:5, :] += jnp.sum(d_ext[0:rows, :], axis=0, keepdims=True)
+        d_x_all[
+            pl.ds(2 * block, 2), pl.ds(pl.multiple_of(slot * piece, piece), piece), :
+        ] = d_conv.astype(BF16).reshape(2, piece, inner)
+        d_ext[rows:, :] = d_ext[0:8, :]
+
+        @pl.when(number == 0)
+        def _():
+            if depth > 2:
+                out_line.step(1)
+
+        @pl.when(number == 1)
+        def _():
+            o_plane.second()
+            if depth > 3:
+                out_line.step(2)
+
+        if depth > 2:
+
+            @pl.when(number == 3)
+            def _():
+                gate_line.step(1)
+
+        if depth > 3:
+
+            @pl.when(number == 4)
+            def _():
+                gate_line.step(2)
+
+        @pl.when(number == 6)
+        def _():
+            o_plane.finish()
+
+        return carry
+
+    lax.fori_loop(0, blocks, scan_block, 0)
+    saves = [
+        pltpu.make_async_copy(source, target, locals_.at[8 + k])
+        for k, (source, target) in enumerate(
+            ((d_x_all, d_x_hbm), (d_bc, d_bc_hbm), (d_arg_all, d_arg_hbm))
         )
-        d_dt_direct = head_totals(x * d_x_dt)
-        d_cum = head_totals(cross_wide)
-        through = head_totals(x_dt * d_x_later)
-        over = head_totals(
-            jnp.broadcast_to(jnp.sum(grown * held16.astype(F32), axis=0, keepdims=True), (8, inner))
+    ]
+    for copy in saves:
+        copy.start()
+
+    out_line.finish(out_sum)
+    home = lax.div(row, half) == core
+    rows_out = out_grad.shape[0]
+    far = links.copy(out_far, out_grad, peer[1])
+    for this in range(2):
+
+        @pl.when(home & (core == this))
+        def _():
+            cast_rows(out_far, out_sum.at[pl.ds((1 - this) * rows_out, rows_out)])
+            far.start()
+            cast_rows(out_grad, out_sum.at[pl.ds(this * rows_out, rows_out)])
+
+    gate_line.finish(gate_sum)
+    turn(gate_sent, gate_sum)
+    send_gate.begin()
+    pl.when(jnp.logical_not(home))(far.wait_recv)
+    pl.when(home)(far.wait_send)
+    o_plane.drain()
+    out_line.drain()
+    gate_line.drain()
+    send_gate.end()
+    save_gate.wait()
+    for copy in saves:
+        copy.wait()
+
+
+def line_buffers(count, extent):
+    return [pltpu.VMEM((count,) + extent, BF16)] * 4
+
+
+def plane_buffers(rows, model):
+    return [
+        pltpu.VMEM((4, rows, model), BF16),
+        pltpu.VMEM((4, rows, model), BF16),
+        pltpu.VMEM((2, rows // 2, model), BF16),
+        pltpu.VMEM((2, rows, model), BF16),
+    ]
+
+
+def reverse(dims, hbm, vmem, collective):
+    depth, width, heads, head_size, size, kernel, own_ch, inner_all = dims
+    inner = heads * head_size
+    _, rows, model = hbm[0].shape
+    tokens = rows * width
+    wide = inner + 2 * size
+    shape = jax.ShapeDtypeStruct
+    subs = rows // CHUNK
+    half = depth // 2
+    out_piece, in_piece = (inner // half, model), (inner, model // depth)
+    saved = [
+        ((width, rows, inner), BF16),
+        ((width, rows, inner), BF16),
+        ((2 * size, tokens), BF16),
+        ((width, rows, 128), BF16),
+    ]
+    kept = [
+        ((rows, model), F32),
+        ((width, model // depth // width, inner), BF16),
+        ((out_piece[0] // 2, model), F32),
+        ((8, inner), F32),
+        ((8, 128), F32),
+    ]
+    return pl.pallas_call(
+        functools.partial(reverse_kernel, dims),
+        out_shape=tuple(shape(*s) for s in saved + kept),
+        in_specs=[ANY] * len(hbm) + [INVMEM] * len(vmem),
+        out_specs=(ANY,) * len(saved) + (INVMEM,) * len(kept),
+        scratch_shapes=[pltpu.VMEM((width, rows, model), BF16)] * 2
+        + [pltpu.VMEM((tokens, inner), F32)] * 3
+        + [pltpu.VMEM(hbm[-1].shape, BF16)]
+        + [pltpu.VMEM(*s) for s in saved]
+        + [
+            pltpu.VMEM((inner, model), F32),
+            pltpu.VMEM((inner, model), F32),
+            pltpu.VMEM((2, rows, wide), F32),
+            pltpu.VMEM((2, rows, inner), F32),
+            pltpu.VMEM((2, rows, 128), F32),
+            pltpu.VMEM((2, subs, size, inner), BF16),
+            pltpu.VMEM((size, inner), F32),
+            pltpu.VMEM((rows + 8, inner), F32),
+        ]
+        + plane_buffers(rows, model)
+        + line_buffers(half, out_piece)
+        + line_buffers(depth - 1, in_piece)
+        + [
+            pltpu.VMEM(out_piece, F32),
+            pltpu.VMEM((out_piece[0] // 2, model), F32),
+            pltpu.VMEM(in_piece, F32),
+            pltpu.VMEM((in_piece[1], in_piece[0]), BF16),
+            pltpu.SemaphoreType.DMA((48,)),
+            pltpu.SemaphoreType.DMA((48,)),
+            pltpu.SemaphoreType.DMA((12,)),
+            pltpu.SemaphoreType.DMA((2, 4)),
+        ],
+        compiler_params=pltpu.CompilerParams(
+            collective_id=collective, has_side_effects=True, vmem_limit_bytes=VMEM_LIMIT
+        ),
+        name="reverse_fused",
+    )(*hbm, *vmem)
+
+
+def weights_kernel(
+    dims,
+    normed_hbm,
+    d_gate_hbm,
+    d_x_hbm,
+    d_arg_hbm,
+    wg_hbm,
+    wx_hbm,
+    wb_hbm,
+    w_dt_hbm,
+    pre_hbm,
+    d_bc,
+    taps,
+    channel_sums,
+    head_sums,
+    d_total,
+    x_back,
+    small_back,
+    sums_all,
+    normed_all,
+    d_gate,
+    d_x,
+    d_arg,
+    wg,
+    wx,
+    wb,
+    w_dt,
+    pre_own,
+    bc_in,
+    d_small,
+    w_small,
+    g_x,
+    g_small,
+    d_parts,
+    d_ext,
+    bc_landed,
+    bc_sums,
+    d_pair,
+    d_sums,
+    d_relay,
+    d_last,
+    x_up_in,
+    x_up_out,
+    x_down_in,
+    x_down_out,
+    small_up_in,
+    small_up_out,
+    small_down_in,
+    small_down_out,
+    x_sum,
+    x_sent,
+    small_sum,
+    small_sent,
+    sums_own,
+    sums_line,
+    sends,
+    recvs,
+    locals_,
+):
+    depth, width, heads, head_size, size, kernel, own_ch, inner_all = dims
+    inner = heads * head_size
+    model = normed_all.shape[2]
+    piece = normed_all.shape[1] // 2
+    rows = 2 * piece
+    slots = 2
+    blocks = slots * width // 2
+    per_slot = blocks // slots
+    everything = slots * width * piece
+    own = 2 * size // width
+    row, place = lax.axis_index("dp"), lax.axis_index("seq")
+    links = Links(sends, recvs)
+    above, below = lax.min(row + 1, depth - 1), lax.max(row - 1, 0)
+    peer = {mask: (row, flip_all(place, mask)) for mask in range(1, width)}
+    order = (6, 2, 4, 7, 3, 5, 1)
+    per_block = 128 // own
+    bc_block = lax.div(place, per_block)
+    bc_turn = 128 - own * lax.rem(place, per_block)
+    window = pl.ds(pl.multiple_of(inner + bc_block * 128, 128), 128)
+
+    loads = [
+        pltpu.make_async_copy(source, target, locals_.at[k])
+        for k, (source, target) in enumerate(
+            (
+                (d_x_hbm, d_x),
+                (normed_hbm, normed_all),
+                (pre_hbm.at[:, window], pre_own),
+                (wb_hbm, wb),
+                (w_dt_hbm, w_dt),
+                (d_arg_hbm, d_arg),
+                (wg_hbm, wg),
+                (wx_hbm, wx),
+                (d_gate_hbm, d_gate),
+            )
         )
-        d_log = (
-            dot(ones, d_cum, ((0,), (0,)), lax.Precision.HIGHEST)
-            + dot(before, through, ((1,), (0,)), lax.Precision.HIGHEST)
-            + over[0:1, :] * jnp.exp(total)
+    ]
+    for copy in loads:
+        copy.start()
+    line_peers = [(lax.rem(row + up, depth), place) for up in range(1, depth)]
+    greet([peer[mask] for mask in range(1, width)] + line_peers)
+
+    bc_rows = PlaneRows(links, row, place, d_bc, bc_landed)
+    bc_rows.begin()
+    cols = model // depth
+
+    def line(own_ref, buffers):
+        return LineSum(
+            links,
+            depth,
+            row,
+            place,
+            lambda q: own_ref.at[:, pl.ds(q * cols, cols)],
+            lambda q: row >= 0,
+            *buffers,
         )
-        d_dt = d_dt_direct + head_rows[1:2, :] * d_log
-        d_arg = d_dt * sigmoid(dt_arg[part])
-        d_arg_out[part, :] = d_arg.astype(BF16)
-        head_sums[0:1, :] += jnp.sum(d_arg, axis=0, keepdims=True)
-        head_sums[1:2, :] += jnp.sum(d_log * dt, axis=0, keepdims=True)
-        channel_sums[5:6, :] += jnp.sum(d_y * x, axis=0, keepdims=True)
-        d_ext[part, :] = d_x * slope[part]
-
-    kernel = 4
-    d_conv = jnp.zeros((rows, inner), F32)
-    x_in = conv_in[...]
-    for k in range(kernel):
-        moved = d_ext[kernel - 1 - k : kernel - 1 - k + rows, :]
-        d_conv = d_conv + taps[k : k + 1, :inner] * moved
-        channel_sums[k : k + 1, :] += jnp.sum(moved * x_in, axis=0, keepdims=True)
-    channel_sums[4:5, :] += jnp.sum(d_ext[0:rows, :], axis=0, keepdims=True)
-    d_proj[:, inner:] = d_conv.astype(BF16)
-    d_ext[rows:, :] = d_ext[0:8, :]
-
-
-def weight_kernel(normed, d_proj, d_small, w_cat, d_parts, g_in):
-    step = pl.program_id(0) * pl.num_programs(1) + pl.program_id(1)
-
-    @pl.when(step == 0)
-    def _():
-        g_in[...] = jnp.zeros_like(g_in)
-
-    rows = d_proj.shape[0]
-    wide = d_proj.shape[1]
-    tokens = normed[...].reshape(rows, normed.shape[2])
-    g_in[:, :wide] += t_mm(tokens, d_proj[...])
-    g_in[:, wide:] += t_mm(tokens, d_small[...])
-    both = jnp.concatenate([d_proj[...], d_small[...]], axis=1)
-    d_parts[...] = mm_t(both, w_cat[...]).astype(BF16).reshape(d_parts.shape)
+
+    x_line = line(g_x, (x_up_in, x_up_out, x_down_in, x_down_out))
+    small_line = line(g_small, (small_up_in, small_up_out, small_down_in, small_down_out))
+    d_plane = PlaneSum(links, row, place, d_parts, d_total, d_pair, d_sums, d_relay, d_last)
+    send_x = SendBack(links, row, place, x_sent, x_back, locals_.at[9])
+    send_small = SendBack(links, row, place, small_sent, small_back, locals_.at[10])
+
+    def x_grad_tile(number, carry):
+        at = pl.ds(pl.multiple_of(number * 128, 128), 128)
+        left = d_x[:, :, at].reshape(everything, 128)
+        g_x[at, :] = t_mm(left, normed_all[...].reshape(everything, model))
+        return carry
+
+    loads[0].wait()
+    loads[1].wait()
+    lax.fori_loop(0, inner // 128, x_grad_tile, 0)
+    x_line.step(0)
+
+    lane = lax.broadcasted_iota(jnp.int32, (1, 128), 1)
+    mine = lane < own
+
+    def to_front(values):
+        return pltpu.roll(values, bc_turn, 1)
+
+    loads[3].wait()
+    loads[4].wait()
+
+    def small_weight(number, carry):
+        at = pl.ds(pl.multiple_of(number * 128, 128), 128)
+        bc = to_front(wb[bc_block, at, :].astype(F32))
+        dt = pltpu.roll(w_dt[at, :].astype(F32), own, 1)
+        w_small[at, :] = jnp.where(mine, bc, dt).astype(BF16)
+        return carry
+
+    lax.fori_loop(0, model // 128, small_weight, 0)
+    own_taps = to_front(taps[:, window])
+
+    def project(index, carry):
+        bc_in[index] = mm(normed_all[index], w_small[...])
+        return carry
+
+    lax.fori_loop(0, width, project, 0)
+    loads[2].wait()
+    loads[5].wait()
+    bc_rows.arrived()
+    bc_sums[...] = jnp.zeros_like(bc_sums)
+    d_ext[...] = jnp.zeros_like(d_ext)
+
+    def small_block(number, carry):
+        slot, block = lax.div(number, per_slot), per_slot - 1 - lax.rem(number, per_slot)
+        at = pl.ds(pl.multiple_of((slot * per_slot + block) * rows, rows), rows)
+
+        @pl.when(block == per_slot - 1)
+        def _():
+            d_ext[rows:, :] = jnp.zeros((8, 128), F32)
+
+        total = d_bc[place, :, at].astype(F32)
+        for k in range(width - 1):
+            total = total + bc_landed[k, :, at].astype(F32)
+        total = jnp.concatenate([total, jnp.zeros((128 - own, rows), F32)], axis=0)
+        pre = to_front(pre_own[at, :])
+        sig = sigmoid(pre)
+        d_pre = jnp.where(mine, total.T * (sig * (1.0 + pre * (1.0 - sig))), 0.0)
+        d_ext[0:rows, :] = d_pre
+        where = (pl.ds(2 * block, 2), pl.ds(pl.multiple_of(slot * piece, piece), piece))
+        conv_in = bc_in[where[0], where[1], :].reshape(rows, 128)
+        d_conv = jnp.zeros((rows, 128), F32)
+        for k in range(kernel):
+            moved = d_ext[kernel - 1 - k : kernel - 1 - k + rows, :]
+            d_conv = d_conv + own_taps[k : k + 1, :] * moved
+            bc_sums[k : k + 1, :] += jnp.sum(moved * conv_in, axis=0, keepdims=True)
+        bc_sums[4:5, :] += jnp.sum(d_pre, axis=0, keepdims=True)
+        d_ext[rows:, :] = d_ext[0:8, :]
+        d_dt = pltpu.roll(
+            d_arg[where[0], where[1], :].astype(F32).reshape(rows, 128), own, 1
+        )
+        both = jnp.where(mine, d_conv, jnp.where(lane < own + heads, d_dt, 0.0))
+        d_small[where[0], where[1], :] = both.astype(BF16).reshape(2, piece, 128)
+        return carry
+
+    lax.fori_loop(0, blocks, small_block, 0)
+    g_small[...] = t_mm(
+        d_small[...].reshape(everything, 128), normed_all[...].reshape(everything, model)
+    )
+    small_line.step(0)
+    for copy in loads[6:]:
+        copy.wait()
+
+    def token_grads(index, carry):
+        total = (
+            mm_t(d_gate[index], wg[...])
+            + mm_t(d_x[index], wx[...])
+            + mm_t(d_small[index], w_small[...])
+        )
+        d_parts[index] = total.astype(BF16)
+        return carry
+
+    lax.fori_loop(0, width, token_grads, 0)
+    d_plane.begin()
+
+    sums_own[:, :inner] = channel_sums[...]
+    sums_own[:, inner : inner + 128] = bc_sums[...]
+    sums_own[:, inner + 128 :] = head_sums[...]
+    sums_copies = [
+        links.copy(sums_own, sums_line.at[k], device) for k, device in enumerate(line_peers)
+    ]
+    for copy in sums_copies:
+        copy.start()
+    if depth > 2:
+        x_line.step(1)
+        small_line.step(1)
+    d_plane.first()
+    for copy in sums_copies:
+        copy.wait()
+    total = jnp.zeros(sums_own.shape, F32)
+    for q in range(depth):
+        term = jnp.zeros(sums_own.shape, F32)
+        for up in range(1, depth):
+            term = jnp.where(lax.rem(row + depth - up, depth) == q, sums_line[up - 1], term)
+        total = total + jnp.where(row == q, sums_own[...], term)
+    sums_all[place] = total
+    mine_all = sums_all.at[place]
+    spread_sums = [links.copy(mine_all, mine_all, peer[mask]) for mask in order]
+    for copy in spread_sums:
+        copy.start()
+    if depth > 3:
+        x_line.step(2)
+        small_line.step(2)
+    d_plane.second()
+    x_line.finish(x_sum)
+    turn(x_sent, x_sum)
+    send_x.begin()
+    small_line.finish(small_sum)
+    turn(small_sent, small_sum)
+    send_small.begin()
+    d_plane.finish()
+    d_plane.drain()
+    x_line.drain()
+    small_line.drain()
+    send_x.end()
+    send_small.end()
+    bc_rows.drain()
+    for copy in spread_sums:
+        copy.wait()
+
+
+def weights(dims, hbm, vmem, collective):
+    depth, width, heads, head_size, size, kernel, own_ch, inner_all = dims
+    inner = heads * head_size
+    _, rows, model = hbm[0].shape
+    tokens = rows * width
+    shape = jax.ShapeDtypeStruct
+    cols = model // depth
+    kept = [
+        ((rows, model), F32),
+        ((width, cols // width, inner), BF16),
+        ((width, cols // width, 128), BF16),
+        ((width, 8, inner + 256), F32),
+    ]
+    return pl.pallas_call(
+        functools.partial(weights_kernel, dims),
+        out_shape=tuple(shape(*s) for s in kept),
+        in_specs=[ANY] * len(hbm) + [INVMEM] * len(vmem),
+        out_specs=(INVMEM,) * len(kept),
+        scratch_shapes=[pltpu.VMEM(v.shape, v.dtype) for v in hbm[:-1]]
+        + [
+            pltpu.VMEM((tokens, 128), F32),
+            pltpu.VMEM((width, rows, 128), F32),
+            pltpu.VMEM((width, rows, 128), BF16),
+            pltpu.VMEM((model, 128), BF16),
+            pltpu.VMEM((inner, model), F32),
+            pltpu.VMEM((128, model), F32),
+            pltpu.VMEM((width, rows, model), BF16),
+            pltpu.VMEM((rows + 8, 128), F32),
+            pltpu.VMEM((width - 1, 2 * size // width, tokens), BF16),
+            pltpu.VMEM((8, 128), F32),
+        ]
+        + plane_buffers(rows, model)
+        + line_buffers(depth - 1, (inner, cols))
+        + line_buffers(depth - 1, (128, cols))
+        + [
+            pltpu.VMEM((inner, cols), F32),
+            pltpu.VMEM((cols, inner), BF16),
+            pltpu.VMEM((128, cols), F32),
+            pltpu.VMEM((cols, 128), BF16),
+            pltpu.VMEM((8, inner + 256), F32),
+            pltpu.VMEM((depth - 1, 8, inner + 256), F32),
+            pltpu.SemaphoreType.DMA((80,)),
+            pltpu.SemaphoreType.DMA((80,)),
+            pltpu.SemaphoreType.DMA((12,)),
+        ],
+        compiler_params=pltpu.CompilerParams(
+            collective_id=collective, has_side_effects=True, vmem_limit_bytes=VMEM_LIMIT
+        ),
+        name="weights_fused",
+    )(*hbm, *vmem)
 
 
 def fast_body(
@@ -1717,21 +2177,6 @@
         shape = values.shape
         return values.reshape(shape[:axis] + (2, half, plane, pair_rows) + shape[axis + 1 :])
 
-    def mine(values):
-        split = by_owner(values, values.ndim - 1)
-        at = values.ndim - 1
-        split = lax.dynamic_index_in_dim(split, core, at, False)
-        split = lax.dynamic_index_in_dim(split, chip, at + 1, False)
-        return split.reshape(values.shape[:-1] + (inner,))
-
-    def my_heads(values):
-        group = pair_rows // head_size
-        at = values.ndim - 1
-        split = values.reshape(values.shape[:-1] + (2, half, plane, group))
-        split = lax.dynamic_index_in_dim(split, core, at, False)
-        split = lax.dynamic_index_in_dim(split, chip, at + 1, False)
-        return split.reshape(values.shape[:-1] + (heads,))
-
     gate_cols = inner_all
     conv_cols = gate_cols + inner_all
     bc_cols = conv_cols + 2 * size
@@ -1798,150 +2243,41 @@
         head_params,
         2,
     )
-    w_in = jnp.concatenate([w_gate.reshape(model, inner), w_x.reshape(model, inner)], axis=1)
-    w_bc = w_bc.reshape(2, model, size)
-    w_out = w_out.reshape(inner, model)
     norm_all = param_rows[0].reshape(1, 1, model)
-    gains = jnp.pad(param_rows[1:3, :inner], ((0, 6), (0, 0)))
-    rates = param_rows[4:5, :heads]
-    head_rows = jnp.pad(param_rows[3:5, :128], ((0, 6), (0, 0)))
     head_sum = padded((jnp.arange(inner)[:, None] // head_size == jnp.arange(heads)).astype(F32))
-    chunks = tokens // CHUNK
-    norms = padded(jnp.stack([norms.T[:chunks].reshape(-1), norms.T[chunks : 2 * chunks].reshape(-1)], axis=1))
-
-    rows = 2 * piece
-    blocks = slot_len // rows
-    shape = jax.ShapeDtypeStruct
-    wide = inner + 2 * size
-
-    def flat(cols, order):
-        return pl.BlockSpec((rows, cols), lambda s, i: (s * blocks + order(i), 0))
-
-    def by_piece(order):
-        return pl.BlockSpec((2, piece, model), lambda s, i: (order(i), s, 0))
-
-    def whole(values):
-        return pl.BlockSpec(values.shape, lambda s, i: (0,) * values.ndim)
-
-    def ahead(i):
-        return i
-
-    def behind(i):
-        return blocks - 1 - i
-
-    o_parts, d_proj, d_bc, d_arg, g_out, channel_sums, head_sums = pl.pallas_call(
-        functools.partial(backward_kernel, heads, head_size, blocks),
-        grid=(slots, blocks),
-        out_shape=(
-            shape(normed_all.shape, BF16),
-            shape((tokens, 2 * inner), BF16),
-            shape((2 * size, tokens), BF16),
-            shape((tokens, 128), BF16),
-            shape((inner, model), F32),
-            shape((8, inner), F32),
-            shape((8, 128), F32),
+    (
+        d_gate,
+        d_x,
+        d_bc,
+        d_arg,
+        o_total,
+        gate_back,
+        out_grad,
+        channel_sums,
+        head_sums,
+    ) = reverse(
+        dims,
+        (cot_all, normed_all, gate, y, dgn, pre, conv_in, dt_arg, states, w_out),
+        (norms, taps, param_rows, head_sum),
+        3,
+    )
+    bc_own = 2 * size // width
+    d_total, x_back, small_back, smalls = weights(
+        dims,
+        (
+            normed_all,
+            d_gate,
+            d_x,
+            d_arg,
+            w_gate.reshape(model, inner),
+            w_x.reshape(model, inner),
+            w_bc.reshape(2, model, size),
+            w_dt,
+            pre,
         ),
-        in_specs=[
-            by_piece(behind),
-            flat(inner, behind),
-            flat(inner, behind),
-            flat(inner, behind),
-            flat(wide, behind),
-            flat(inner, behind),
-            flat(128, behind),
-            pl.BlockSpec((rows // CHUNK, size, inner), lambda s, i: (s * blocks + behind(i), 0, 0)),
-            flat(128, behind),
-        ]
-        + [whole(v) for v in (w_out, taps, gains, head_rows, head_sum)],
-        out_specs=(
-            by_piece(behind),
-            flat(2 * inner, behind),
-            pl.BlockSpec((2 * size, rows), lambda s, i: (0, s * blocks + behind(i))),
-            flat(128, behind),
-            pl.BlockSpec((inner, model), lambda s, i: (0, 0)),
-            pl.BlockSpec((8, inner), lambda s, i: (0, 0)),
-            pl.BlockSpec((8, 128), lambda s, i: (0, 0)),
-        ),
-        scratch_shapes=[
-            pltpu.VMEM((size, inner), F32),
-            pltpu.VMEM((rows + 8, inner), F32),
-        ],
-        compiler_params=pltpu.CompilerParams(vmem_limit_bytes=VMEM_LIMIT),
-        name="block_backward",
-    )(
-        cot_all,
-        y,
-        gate,
-        dgn,
-        pre,
-        conv_in,
-        dt_arg,
-        states,
-        norms,
-        w_out,
-        taps,
-        gains,
-        head_rows,
-        head_sum,
-    )
-
-    bc_own = 2 * size // width
-    d_bc_own = plane_rows(d_bc.reshape(width, bc_own, tokens), 4).T
-    pre_own = lax.dynamic_slice_in_dim(pre, inner + place * bc_own, bc_own, 1)
-    sig = jax.nn.sigmoid(pre_own)
-    d_pre = (d_bc_own * sig * (1.0 + pre_own * (1.0 - sig))).reshape(slots, slot_len, bc_own)
-    w_bc_own = lax.dynamic_slice_in_dim(
-        jnp.swapaxes(w_bc, 0, 1).reshape(model, 2 * size), place * bc_own, bc_own, 1
-    )
-    bc_in = mm(
-        jnp.transpose(normed_all.reshape(width, slots, piece, model), (1, 0, 2, 3)).reshape(
-            tokens, model
-        ),
-        w_bc_own,
-    ).reshape(slots, slot_len, bc_own)
-    taps_own = lax.dynamic_slice_in_dim(taps, inner + place * bc_own, bc_own, 1)
-    moved = [
-        jnp.pad(d_pre[:, taps_count - 1 - k :], ((0, 0), (0, taps_count - 1 - k), (0, 0)))
-        for k in range(taps_count)
-    ]
-    d_bc_in = sum(taps_own[k] * moved[k] for k in range(taps_count))
-    bc_sums = jnp.stack(
-        [jnp.sum(moved[k] * bc_in, axis=(0, 1)) for k in range(taps_count)]
-        + [jnp.sum(d_pre, axis=(0, 1))]
-    )
-    d_small = padded(
-        jnp.concatenate(
-            [d_bc_in.reshape(tokens, bc_own).astype(BF16), d_arg[:, :heads]], axis=1
-        )
-    )
-    w_cat = jnp.concatenate(
-        [w_in, padded(jnp.concatenate([w_bc_own, w_dt[:, :heads]], axis=1))], axis=1
-    )
-
-    d_parts, g_in = pl.pallas_call(
-        weight_kernel,
-        grid=(slots, blocks),
-        out_shape=(shape(normed_all.shape, BF16), shape((model, 2 * inner + 128), F32)),
-        in_specs=[by_piece(ahead), flat(2 * inner, ahead), flat(128, ahead), whole(w_cat)],
-        out_specs=(
-            by_piece(ahead),
-            pl.BlockSpec((model, 2 * inner + 128), lambda s, i: (0, 0)),
-        ),
-        compiler_params=pltpu.CompilerParams(vmem_limit_bytes=VMEM_LIMIT),
-        name="weight_backward",
-    )(normed_all, d_proj, d_small, w_cat)
-
-    skip_sum = jnp.sum(channel_sums[5].reshape(heads, head_size), axis=1)
-    head_part = jnp.stack([head_sums[0, :heads], head_sums[1, :heads] * rates[0], skip_sum])
-    small = jnp.concatenate(
-        [
-            jnp.concatenate([channel_sums[:5], bc_sums], axis=1),
-            jnp.pad(head_part, ((0, 0), (0, inner + bc_own - heads))),
-        ],
-        axis=0,
-    )
-    lanes = -(-small.shape[1] // 128) * 128
-    smalls = jnp.sum(spread(padded(small, lanes), (depth, width), 5), axis=0)
+        (d_bc.reshape(width, bc_own, tokens), taps, channel_sums, head_sums),
+        4,
+    )
 
     def to_whole(values, group):
         count = values.shape[1]
@@ -1953,32 +2289,18 @@
     conv_grads = lax.dynamic_slice_in_dim(
         jnp.concatenate([conv_x, conv_bc], axis=1), (row * width + place) * own_ch, own_ch, 1
     )
-    head_grads = to_whole(smalls[:, 5:8, :heads], pair_rows // head_size)
-
-    d_total, o_total, in_total, out_grad = scatter(
-        depth,
-        d_parts,
-        o_parts,
-        g_in.reshape(depth, model // depth, 2 * inner + 128),
-        g_out.reshape(half, pair_rows, model),
-        6,
-    )
-    in_f = in_total.astype(F32)
-
-    def cols_from_all(values):
-        split = values.reshape(plane, 2, in_rows, half, pair_rows)
-        return jnp.transpose(split, (2, 1, 3, 0, 4)).reshape(in_rows, inner_all)
-
-    dt_cols = in_f[:, :, 2 * inner + bc_own : 2 * inner + bc_own + heads]
-    dt_cols = jnp.swapaxes(to_whole(jnp.swapaxes(dt_cols, 1, 1), pair_rows // head_size), 0, 0)
+    skip_sum = jnp.sum(smalls[:, 5:6, :inner].reshape(width, 1, heads, head_size), axis=3)
+    head_grads = to_whole(
+        jnp.concatenate([smalls[:, :2, inner + 128 : inner + 128 + heads], skip_sum], axis=1),
+        pair_rows // head_size,
+    )
+    small_f = small_back.astype(F32)
     in_grad = jnp.concatenate(
         [
-            cols_from_all(in_f[:, :, :inner]),
-            cols_from_all(in_f[:, :, inner : 2 * inner]),
-            jnp.swapaxes(in_f[:, :, 2 * inner : 2 * inner + bc_own], 0, 1).reshape(
-                in_rows, 2 * size
-            ),
-            dt_cols,
+            to_whole(gate_back.astype(F32), pair_rows),
+            to_whole(x_back.astype(F32), pair_rows),
+            jnp.swapaxes(small_f[:, :, :bc_own], 0, 1).reshape(in_rows, 2 * size),
+            to_whole(small_f[:, :, bc_own : bc_own + heads], pair_rows // head_size),
         ],
         axis=1,
     )

time: 382 us -> 308 us (0.81)
  Pallas kernels: 316 us -> 278 us
  local copies, waits for them, and re-layouts: 40.6 us -> 18 us
  other arithmetic: 21 us -> 9.93 us
    pallas_call x5 -> x2, Pallas kernels: 218 us -> 179 us  [the longest x1 93.5 us: reverse(): pl.pallas_call(functools.partial(reverse_kernel, dims), out_shape=tuple((...]
    reshape x7 -> x2, local copies, waits for them, and re-layouts: 9.43 us -> 0.18 us  [the longest x1 0.11 us: fast_body(): jnp.swapaxes(small_f[:, :, :bc_own], 0, 1).reshape(in_rows, 2 * size)]
    pallas_call x1 -> x0, local copies, waits for them, and re-layouts: 5.97 us -> none  [forward(): pl.pallas_call(functools.partial(forward_kernel, dims), out_shape=tuple((...]
    transpose x5 -> x2, local copies, waits for them, and re-layouts: 4.51 us -> 0.08 us  [fast_body(): jnp.swapaxes(small_f[:, :, :bc_own], 0, 1).reshape(in_rows, 2 * size)]
where the time goes in v2:
time: 308 us; the launch traced here: 307 us
  Pallas kernels  278 us (90%)
  local copies, waits for them, and re-layouts  18 us (6%)
  other arithmetic  9.93 us (3%)
    pallas_call x1, Pallas kernels, forward(): pl.pallas_call(functools.partial(forward_kernel, dims), out_shape=tuple((...  98.7 us
    pallas_call x1, Pallas kernels, reverse(): pl.pallas_call(functools.partial(reverse_kernel, dims), out_shape=tuple((...  93.5 us
    pallas_call x1, Pallas kernels, weights(): pl.pallas_call(functools.partial(weights_kernel, dims), out_shape=tuple((...  86 us

profile of v2, /device:TPU:9, one launch (start us, length us, event | category | flops | bytes accessed | tf_op | source)
XLA Modules:
  0.0 307.2 jit_solution(72086851636921045)
XLA Ops:
  0.6 0.0 copy-start.3
  0.7 0.8 compare_convert_fusion
  1.5 2.1 broadcast_multiply_fusion
  3.6 0.5 reshape.199
  4.1 0.3 copy.69
  4.4 0.0 slice-start
  4.5 0.0 copy-start.10
  4.5 0.0 copy-start.11
  4.5 0.0 copy-start.12
  4.5 0.0 copy-start.13
  4.5 0.0 copy-start.14
  4.5 0.0 copy-start.15
  4.5 0.0 copy-start.16
  4.5 0.9 reshape.200.wg_send
  5.5 0.5 reshape.201
  6.0 0.3 copy.68
  6.3 0.9 reshape.202.wx_send
  7.2 0.6 pad_add_fusion.pack
  7.9 0.6 bitcast_bitcast_fusion.wb_send
  8.5 0.6 select_maximum_fusion.head_params
  9.1 98.7 %forward_fused.1 = (bf16[8,256,1536]{2,1,0:T(8,128)(2,1)}, bf16[8,256,1536]{2,1,0:T(8,128)(2,1)}, bf16[4,8,48,384]{3,2,1,0:T(8,128)(2,1)}, bf16[4,8,48,384]{3,2,...) custom-call(bf16[256,1536]{1,0:T(8,128)(2,1)} %bitcast.48, ...), custom_call_target="tpu_custom_call" | custom-call | tf_op jit(solution)/shard_map/forward_fused/pallas_call | solution.py:1256
  107.8 0.1 iota_compare_fusion
  107.9 0.7 pad_convert_fusion.head_sum
  108.6 93.5 %reverse_fused.1 = (bf16[8,256,384]{2,1,0:T(8,128)(2,1)}, bf16[8,256,384]{2,1,0:T(8,128)(2,1)}, bf16[256,2048]{1,0:T(8,128)(2,1)}, bf16[8,256,128]{2,1,0:T(8,128...) custom-call(bf16[8,256,1536]{2,1,0:T(8,128)(2,1)} %get-tuple-element, ...), custom_call_target="tpu_custom_call" | custom-call | tf_op jit(solution)/shard_map/reverse_fused/pallas_call | solution.py:1790
  202.2 86.0 %weights_fused.1 = (f32[256,1536]{1,0:T(8,128)}, bf16[8,48,384]{2,1,0:T(8,128)(2,1)}, bf16[8,48,128]{2,1,0:T(8,128)(2,1)}, f32[8,8,640]{2,1,0:T(8,128)}) custom-call(bf16[8,256,1536]{2,1,0:T(8,128)(2,1)} %get-tuple-element.42.normed_hbm, bf16[8,256,384]{2,1,0:T(8,128)(2,1)} %get-tuple-element.55.d_gate_hbm, bf16[8,256,384]{2,1,0:T(8,128)(2,1)} %get-tuple-element.56.d_x_hbm, ...), custom_call_target="tpu_custom_call" | custom-call | tf_op jit(solution)/shard_map/weights_fused/pallas_call | solution.py:2102
  288.2 1.0 slice_reduce_fusion
  289.1 0.1 reshape.222
  289.2 0.1 reduce_sum.49
  289.3 0.1 concatenate.17
  289.4 0.8 slice.62
  290.1 0.1 concatenate.16
  290.3 0.6 squeeze.13
  290.9 0.6 squeeze.14
  291.5 0.6 squeeze.15
  292.1 0.9 slice.58
  293.0 0.1 reshape.219
  293.2 0.1 reshape.220
  293.3 0.8 slice_bitcast_fusion.1
  294.1 0.1 reshape.221
  294.1 0.1 fusion.9
  294.2 0.6 slice.60
  294.8 0.5 slice_bitcast_fusion.3
  295.3 0.6 reshape.232
  296.0 0.5 copy.52
  296.5 0.7 reshape.226
  297.3 0.1 copy.53
  297.3 0.1 reshape.216
  297.5 0.1 slice.68
  297.6 0.1 copy.54
  297.7 0.1 copy.56
  297.8 0.6 reshape.230
  298.4 0.5 copy.51
  299.0 0.7 reshape.224
  299.7 1.3 multiply_reduce_fusion
  301.0 0.5 convert_divide_fusion.1
  301.5 0.8 slice_reduce_fusion.1
  302.4 0.2 fusion.8
  302.6 0.4 fusion.2
  303.0 0.5 copy-done.2
  303.5 0.5 copy-done.5
  304.0 1.6 fusion.6
  305.7 0.2 multiply_reduce_fusion.1
  305.8 0.5 convert_divide_fusion
  306.4 0.8 copy.71
  (43 shorter events, 0.3 us)
Async XLA Ops:
  0.6 3.0 copy-start.3
  4.4 2.8 slice-start
  4.5 2.8 copy-start.10
  4.5 2.8 copy-start.11
  4.5 2.7 copy-start.12
  4.5 2.7 copy-start.13
  4.5 4.0 %copy-start.14 = (f32[48]{0:T(128)S(1)}, f32[48]{0:T(128)}, u32[]{:S(2)}) copy-start(f32[48]{0:T(128)} %param.23) | copy-start | bytes 580
  4.5 4.0 %copy-start.15 = (f32[48]{0:T(128)S(1)}, f32[48]{0:T(128)}, u32[]{:S(2)}) copy-start(f32[48]{0:T(128)} %param.22) | copy-start | bytes 580
  4.5 3.9 %copy-start.16 = (f32[48]{0:T(128)S(1)}, f32[48]{0:T(128)}, u32[]{:S(2)}) copy-start(f32[48]{0:T(128)} %param.21) | copy-start | bytes 580
  288.1 7.2 %copy-start.9 = (bf16[8,48,384]{2,1,0:T(8,128)(2,1)S(1)}, bf16[8,48,384]{2,1,0:T(8,128)(2,1)}, u32[]{:S(2)}) copy-start(bf16[8,48,384]{2,1,0:T(8,128)(2,1)} %get-tuple-element.67) | copy-start | bytes 884740
  296.0 1.3 copy-start.7
  296.5 1.3 copy-start.8
  299.7 2.7 copy-start
  299.7 2.9 copy-start.1
  302.4 1.1 copy-start.2
  302.4 1.6 copy-start.5
  304.0 1.6 copy-start.4
  304.0 1.6 copy-start.6

commit v3 on v2

--- a/solution.py
+++ b/solution.py
@@ -483,50 +483,34 @@
             q: links.copy(self.down_out[q], self.down_in[q], (below, place)) for q in self.down_in
         }
 
-    def up(self, q):
-        row = self.row
-
-        @pl.when(self.valid(q) & (row < q))
+    def up(self, q, row):
+        @pl.when(self.valid(q) & (self.row == row))
         def _():
-            @pl.when(row == 0)
-            def _():
+            if row == 0:
                 cast_rows(self.up_out[q], self.own(q))
-
-            @pl.when(row > 0)
-            def _():
+            else:
                 self.ups[q].wait_recv()
                 add_rows(self.up_out[q], self.own(q), self.up_in[q])
-
             self.ups[q].start()
 
-    def down(self, q):
-        row, depth = self.row, self.depth
-
-        @pl.when(self.valid(q) & (row > q))
+    def down(self, q, row):
+        @pl.when(self.valid(q) & (self.row == row))
         def _():
-            @pl.when(row == depth - 1)
-            def _():
+            if row == self.depth - 1:
                 cast_rows(self.down_out[q], self.own(q))
-
-            @pl.when(row < depth - 1)
-            def _():
+            else:
                 self.downs[q].wait_recv()
                 add_rows(self.down_out[q], self.own(q), self.down_in[q])
-
             self.downs[q].start()
 
-    def step(self, number):
-        up_q, down_q = self.depth - 1 - number, number
-
-        @pl.when(self.row < self.depth // 2)
-        def _():
-            self.up(up_q)
-            self.down(down_q)
-
-        @pl.when(self.row >= self.depth // 2)
-        def _():
-            self.down(down_q)
-            self.up(up_q)
+    def phase(self, number):
+        for row in range(self.depth):
+            up_q = self.depth - 1 + row - number
+            if row < up_q < self.depth:
+                self.up(up_q, row)
+            down_q = number - (self.depth - 1 - row)
+            if 0 <= down_q < row:
+                self.down(down_q, row)
 
     def finish(self, total):
         depth, row = self.depth, self.row
@@ -554,12 +538,12 @@
 
 
 class PlaneSum:
-    def __init__(self, links, row, place, parts, total, pair_in, sums, relay_in, last_in):
-        self.place, self.parts, self.total = place, parts, total
+    def __init__(self, links, row, place, parts, pair_in, sums, relay_in, last_in):
+        self.place, self.parts = place, parts
         self.pair_in, self.sums, self.relay_in, self.last_in = pair_in, sums, relay_in, last_in
         peer = {mask: (row, flip_all(place, mask)) for mask in range(1, 8)}
         self.peer = peer
-        rows = total.shape[0] // 2
+        rows = last_in.shape[1] // 2
         self.halves = (pl.ds(0, rows), pl.ds(rows, rows))
         self.pair = {
             mask: links.copy(parts.at[peer[mask ^ 1][1]], pair_in.at[mask // 2], peer[1])
@@ -568,8 +552,12 @@
         top, low = self.halves
         self.relay4 = links.copy(sums.at[3, top], relay_in.at[0], peer[4])
         self.relay2 = links.copy(sums.at[3, low], relay_in.at[1], peer[2])
-        self.last2 = links.copy(sums.at[1], last_in.at[0], peer[2])
-        self.last4 = links.copy(sums.at[2], last_in.at[1], peer[4])
+        self.last2 = [
+            links.copy(sums.at[1, half], last_in.at[0, half], peer[2]) for half in self.halves
+        ]
+        self.last4 = [
+            links.copy(sums.at[2, half], last_in.at[1, half], peer[4]) for half in self.halves
+        ]
 
     def begin(self):
         for copy in self.pair.values():
@@ -581,33 +569,46 @@
         mine = self.parts.at[self.peer[mask][1] if mask else self.place]
         add_rows(self.sums.at[index], mine, self.pair_in.at[index])
 
-    def first(self):
+    def far(self):
         self.chip(6)
         self.relay4.start()
         self.relay2.start()
-        self.chip(2)
-        self.chip(4)
-        self.chip(0)
+
+    def near(self, mask):
+        self.chip(mask)
+        if mask:
+            (self.last2[1] if mask == 2 else self.last4[0]).start()
+
+    def first(self):
+        self.far()
+        for mask in (2, 4, 0):
+            self.near(mask)
 
     def second(self):
         top, low = self.halves
         self.relay4.wait_recv()
         add_rows(self.sums.at[1, top], self.sums.at[1, top], self.relay_in.at[0])
-        self.last2.start()
+        self.last2[0].start()
         self.relay2.wait_recv()
         add_rows(self.sums.at[2, low], self.sums.at[2, low], self.relay_in.at[1])
-        self.last4.start()
-
-    def finish(self):
-        self.last2.wait_recv()
-        self.last4.wait_recv()
-        add_rows(self.total, self.last_in.at[0], self.last_in.at[1])
-        add_rows(self.total, self.total, self.sums.at[0])
+        self.last4[1].start()
+
+    def finish(self, store):
+        for copy in self.last2 + self.last4:
+            copy.wait_recv()
+
+        def one(number, carry):
+            at = pl.ds(pl.multiple_of(number * 32, 32), 32)
+            total = self.last_in[0, at].astype(F32) + self.last_in[1, at].astype(F32)
+            store(at, total + self.sums[0, at].astype(F32))
+            return carry
+
+        lax.fori_loop(0, self.last_in.shape[1] // 32, one, 0)
 
     def drain(self):
         for copy in self.pair.values():
             copy.wait_send()
-        for copy in (self.relay4, self.relay2, self.last2, self.last4):
+        for copy in [self.relay4, self.relay2] + self.last2 + self.last4:
             copy.wait_send()
 
 
@@ -663,6 +664,27 @@
 def head_decays(cum, cum_t, head, causal):
     gap = cum[:, head : head + 1] - cum_t[head : head + 1, :]
     return jnp.exp(jnp.where(causal, gap, -1e30))
+
+
+def plane_total(links, sums, landed, peer, count):
+    landed[0] = sums[...].T[:count]
+    copies = [links.copy(landed.at[0], landed.at[mask], peer[mask]) for mask in peer]
+    for copy in copies:
+        copy.start()
+
+    def end():
+        for copy in copies:
+            copy.wait()
+        got = [landed[mask] for mask in range(len(peer) + 1)]
+        while len(got) > 1:
+            got = [got[k] + got[k + 1] for k in range(0, len(got), 2)]
+        return got[0]
+
+    return end
+
+
+def by_column(values):
+    return jnp.concatenate([values, jnp.zeros((128 - values.shape[0], CHUNK), F32)], axis=0).T
 
 
 class Line:
@@ -823,12 +845,12 @@
     dt_out,
     gate_out,
     y_out,
-    dgn_out,
     states_out,
     norms_out,
     taps_out,
     rows_out,
     w_dt_out,
+    w_dt_all_out,
     x_all,
     normed_all,
     cot_all,
@@ -842,7 +864,6 @@
     dt_all,
     gate_all,
     y_all,
-    dgn_all,
     states,
     ext,
     state,
@@ -964,6 +985,7 @@
     rates = jnp.where(lane < heads, -jnp.exp(chosen[1:2]), 0.0)
     skip = widen(chosen[2:3], heads, head_size)
     dt_rows = packs[:, :, 0 : model // (depth * width), :].reshape(model, 128)
+    w_dt_all_out[...] = dt_rows
     w_dt_out[...] = mm(dt_rows, choice.astype(BF16)).astype(BF16)
     rows_out[...] = jnp.zeros_like(rows_out)
     rows_out[0:1, :] = norm_gain
@@ -1046,7 +1068,7 @@
             taps_out[k : k + 1, :] * ext[9 - kernel + k : 9 - kernel + k + rows, :]
             for k in range(kernel)
         )
-        conv_in[pl.ds(at, rows), :] = ext[8:, :inner]
+        conv_in[pl.ds(at, rows), :] = ext[8:, :]
         ext[0:8, :] = ext[rows : rows + 8, :]
         pre_all[pl.ds(at, rows), :] = pre
         act = pre * sigmoid(pre)
@@ -1169,47 +1191,11 @@
     for copy in save_weights:
         copy.start()
 
-    def cot_block(index, carry):
-        slot, block = lax.div(index, per_slot), lax.rem(index, per_slot)
-        at = pl.multiple_of(index * rows, rows)
-        tokens = cot_all[
-            pl.ds(2 * block, 2), pl.ds(pl.multiple_of(slot * piece, piece), piece), :
-        ].reshape(rows, model)
-        dgn = mm_t(tokens, wo[...].reshape(inner, model))
-        dgn_all[pl.ds(at, rows), :] = dgn
-        gate = gate_all[pl.ds(at, rows), :]
-        gated = y_all[pl.ds(at, rows), :] * (gate * sigmoid(gate))
-        cross = dgn * rows_out[1:2, :inner] * gated
-        for sub in range(rows // CHUNK):
-            part = cross[sub * CHUNK : (sub + 1) * CHUNK]
-            total = jnp.sum(part, axis=1, keepdims=True)
-            sums[...] = jnp.where(
-                chunk_lane == 2 * blocks + index * (rows // CHUNK) + sub, total, sums[...]
-            )
-        return carry
-
-    lax.fori_loop(0, blocks, cot_block, 0)
-    save_dgn = pltpu.make_async_copy(dgn_all, dgn_out, locals_.at[14])
-    save_dgn.start()
-    count = 4 * blocks
-    sums_in[0] = sums[...].T[:count]
-    sum_copies = [
-        links.copy(sums_in.at[0], sums_in.at[mask], peer[mask]) for mask in range(1, width)
-    ]
-    for copy in sum_copies:
-        copy.start()
-    for copy in sum_copies:
-        copy.wait_recv()
-    got = [sums_in[mask] for mask in range(width)]
-    while len(got) > 1:
-        got = [got[k] + got[k + 1] for k in range(0, len(got), 2)]
-    squares, cross = got[0][: 2 * blocks], got[0][2 * blocks :]
-    inv_gate = lax.rsqrt(squares / inner_all + EPS)
-    mean = inv_gate * cross / inner_all
-    norms = jnp.concatenate([inv_gate, mean, jnp.zeros((128 - count, 128), F32)], axis=0)
-    norms_out[...] = norms.T
-
-    for copies in (plane_x, plane_g, pack_line, pack_plane, sum_copies, [pair_bc]):
+    squares = plane_total(links, sums, sums_in, peer, 2 * blocks)
+    inv_gate = lax.rsqrt(squares() / inner_all + EPS)
+    norms_out[...] = by_column(inv_gate)
+
+    for copies in (plane_x, plane_g, pack_line, pack_plane, [pair_bc]):
         for copy in copies:
             copy.wait_send()
     pl.when(jnp.logical_not(out_home))(out_pair.wait_send)
@@ -1217,7 +1203,7 @@
         line.drain()
     x_pass.drain()
     cot_pass.drain()
-    for copy in saves + [save_gate, save_cot, save_dgn] + save_weights:
+    for copy in saves + [save_gate, save_cot] + save_weights:
         copy.wait()
 
     def stores_end(index, carry):
@@ -1243,16 +1229,15 @@
         ((depth // 2, 2) + wo_own.shape, BF16),
     ]
     kept = [
-        ((tokens, inner), F32),
+        ((tokens, wide), F32),
         ((tokens, wide), F32),
         ((tokens, 128), F32),
-        ((tokens, inner), F32),
         ((tokens, inner), F32),
         ((tokens, inner), F32),
         ((chunks, size, inner), BF16),
     ]
     in_hbm = [((width, rows, model), BF16)] * 2 + weights + kept
-    in_vmem = [((CHUNK, 128), F32), ((8, wide), F32), ((8, model), F32), ((model, 128), BF16)]
+    in_vmem = [((CHUNK, 128), F32), ((8, wide), F32), ((8, model), F32)] + [((model, 128), BF16)] * 2
     return pl.pallas_call(
         functools.partial(forward_kernel, dims),
         out_shape=tuple(shape(*s) for s in in_hbm + in_vmem),
@@ -1267,7 +1252,7 @@
             pltpu.VMEM((size, inner), F32),
             pltpu.VMEM((8, -(-own_ch * depth * width // 128) * 128), F32),
             pltpu.VMEM((CHUNK, 128), F32),
-            pltpu.VMEM((width, 2 * chunks, 128), F32),
+            pltpu.VMEM((width, chunks, 128), F32),
             pltpu.SemaphoreType.DMA((112,)),
             pltpu.SemaphoreType.DMA((112,)),
             pltpu.SemaphoreType.DMA((16,)),
@@ -1281,18 +1266,19 @@
 
 
 class PlaneRows:
-    def __init__(self, links, row, place, parts, landed):
-        self.place, self.parts, self.landed = place, parts, landed
+    def __init__(self, links, row, place, parts, landed, local):
+        mine = landed.at[place]
         peers = [(row, flip_all(place, mask)) for mask in (6, 7, 2, 3, 4, 5, 1)]
-        self.copies = [
-            links.copy(parts.at[peer[1]], landed.at[k], peer) for k, peer in enumerate(peers)
-        ]
+        self.copies = [links.copy(parts.at[peer[1]], mine, peer) for peer in peers]
+        self.kept = pltpu.make_async_copy(parts.at[place], mine, local)
 
     def begin(self):
         for copy in self.copies:
             copy.start()
+        self.kept.start()
 
     def arrived(self):
+        self.kept.wait()
         for copy in self.copies:
             copy.wait_recv()
 
@@ -1337,7 +1323,6 @@
     normed_hbm,
     gate_hbm,
     y_hbm,
-    dgn_hbm,
     pre_hbm,
     conv_hbm,
     dt_hbm,
@@ -1347,11 +1332,12 @@
     taps,
     rows_in,
     head_sum,
+    x_own,
     d_gate_hbm,
     d_x_hbm,
     d_bc_hbm,
     d_arg_hbm,
-    o_total,
+    output,
     gate_back,
     out_grad,
     channel_sums,
@@ -1390,6 +1376,8 @@
     out_far,
     gate_sum,
     gate_sent,
+    means,
+    sums_in,
     sends,
     recvs,
     locals_,
@@ -1419,7 +1407,6 @@
                 (gate_hbm, gate_all),
                 (cot_hbm, cot_all),
                 (wo_hbm, wo),
-                (dgn_hbm, d_y_all),
                 (normed_hbm, normed_all),
             )
         )
@@ -1438,7 +1425,7 @@
         buffer = lax.rem(number, 2)
         pairs = (
             (pre_hbm.at[at], pre_two.at[buffer]),
-            (conv_hbm.at[at], conv_two.at[buffer]),
+            (conv_hbm.at[at, pl.ds(0, inner)], conv_two.at[buffer]),
             (dt_hbm.at[at], dt_two.at[buffer]),
             (states_hbm.at[pl.ds(index * subs, subs)], states_two.at[buffer]),
         )
@@ -1480,15 +1467,15 @@
         gate_down_in,
         gate_down_out,
     )
-    o_plane = PlaneSum(links, row, place, cot_all, o_total, o_pair, o_sums, o_relay, o_last)
+    o_plane = PlaneSum(links, row, place, cot_all, o_pair, o_sums, o_relay, o_last)
     send_gate = SendBack(links, row, place, gate_sent, gate_back, locals_.at[6])
 
     chunk_lane = lax.broadcasted_iota(jnp.int32, (CHUNK, 128), 1)
 
-    def column(index, shift):
+    def column(ref, index):
         parts = [
             jnp.sum(
-                jnp.where(chunk_lane == shift + index * subs + sub, norms[...], 0.0),
+                jnp.where(chunk_lane == index * subs + sub, ref[...], 0.0),
                 axis=1,
                 keepdims=True,
             )
@@ -1506,7 +1493,7 @@
     def normed_block(index, carry):
         at = pl.ds(pl.multiple_of(index * rows, rows), rows)
         gate = gate_all[at, :]
-        hat = y_all[at, :] * (gate * sigmoid(gate)) * column(index, 0)
+        hat = y_all[at, :] * (gate * sigmoid(gate)) * column(norms, index)
         tokens_of(d_gate, index)[...] = (
             (hat * gate_gain).astype(BF16).reshape(2, piece, inner)
         )
@@ -1526,15 +1513,33 @@
 
     loads[2].wait()
     lax.fori_loop(0, inner // 128, out_grad_tile, 0)
-    out_line.step(0)
+    out_line.phase(0)
+
+    def cot_block(index, carry):
+        at = pl.ds(pl.multiple_of(index * rows, rows), rows)
+        tokens = tokens_of(cot_all, index)[...].reshape(rows, model)
+        dgn = mm_t(tokens, wo[...].reshape(inner, model))
+        d_y_all[at, :] = dgn
+        gate = gate_all[at, :]
+        cross = dgn * gate_gain * y_all[at, :] * (gate * sigmoid(gate))
+        for sub in range(subs):
+            part = cross[sub * CHUNK : (sub + 1) * CHUNK]
+            total = jnp.sum(part, axis=1, keepdims=True)
+            means[...] = jnp.where(chunk_lane == index * subs + sub, total, means[...])
+        return carry
+
+    loads[3].wait()
+    means[...] = jnp.zeros_like(means)
+    lax.fori_loop(0, blocks, cot_block, 0)
+    crosses = plane_total(links, means, sums_in, peer, 2 * blocks)
 
     def out_block(index, carry):
         cot_all[index] = mm(d_gate[index], wo[...].reshape(inner, model)).astype(BF16)
         return carry
 
-    loads[3].wait()
     lax.fori_loop(0, width, out_block, 0)
     o_plane.begin()
+    means[...] = norms[...] * by_column(crosses() / inner_all)
 
     def gate_block(index, carry):
         at = pl.ds(pl.multiple_of(index * rows, rows), rows)
@@ -1542,16 +1547,15 @@
         sig = sigmoid(gate)
         gate_act = gate * sig
         y = y_all[at, :]
-        inv = column(index, 0)
+        inv = column(norms, index)
         hat = y * gate_act * inv
-        d_gated = inv * (d_y_all[at, :] * gate_gain - hat * column(index, 2 * blocks))
+        d_gated = inv * (d_y_all[at, :] * gate_gain - hat * column(means, index))
         d_y_all[at, :] = d_gated * gate_act
         tokens_of(d_gate, index)[...] = (
             (d_gated * y * sig * (1.0 + gate * (1.0 - sig))).astype(BF16).reshape(2, piece, inner)
         )
         return carry
 
-    loads[4].wait()
     lax.fori_loop(0, blocks, gate_block, 0)
     save_gate = pltpu.make_async_copy(d_gate, d_gate_hbm, locals_.at[7])
     save_gate.start()
@@ -1562,9 +1566,9 @@
         g_gate[at, :] = t_mm(left, normed_all[...].reshape(everything, model))
         return carry
 
-    loads[5].wait()
+    loads[4].wait()
     lax.fori_loop(0, inner // 128, gate_grad_tile, 0)
-    gate_line.step(0)
+    gate_line.phase(0)
     o_plane.first()
 
     channel_sums[...] = jnp.zeros_like(channel_sums)
@@ -1575,6 +1579,34 @@
 
     def head_totals(values):
         return dot(values, head_sum[...], ((1,), (0,)), lax.Precision.HIGHEST)
+
+    def pump_first():
+        if depth > 2:
+            out_line.phase(1)
+
+    def pump_second():
+        o_plane.second()
+        if depth > 3:
+            out_line.phase(2)
+
+    def pump_gate():
+        if depth > 2:
+            gate_line.phase(1)
+
+    def pump_gate_last():
+        if depth > 3:
+            gate_line.phase(2)
+
+    pumps = {
+        0: pump_first,
+        2: pump_second,
+        4: pump_gate,
+        5: lambda: o_plane.finish(store_output),
+        6: pump_gate_last,
+    }
+
+    def store_output(at, total):
+        output[at] = (x_own[at].astype(F32) + total).astype(BF16)
 
     def scan_block(number, carry):
         slot, block = place_of(number)
@@ -1686,32 +1718,8 @@
         ] = d_conv.astype(BF16).reshape(2, piece, inner)
         d_ext[rows:, :] = d_ext[0:8, :]
 
-        @pl.when(number == 0)
-        def _():
-            if depth > 2:
-                out_line.step(1)
-
-        @pl.when(number == 1)
-        def _():
-            o_plane.second()
-            if depth > 3:
-                out_line.step(2)
-
-        if depth > 2:
-
-            @pl.when(number == 3)
-            def _():
-                gate_line.step(1)
-
-        if depth > 3:
-
-            @pl.when(number == 4)
-            def _():
-                gate_line.step(2)
-
-        @pl.when(number == 6)
-        def _():
-            o_plane.finish()
+        for at_step, action in pumps.items():
+            pl.when(number == at_step)(action)
 
         return carry
 
@@ -1781,7 +1789,7 @@
         ((width, rows, 128), BF16),
     ]
     kept = [
-        ((rows, model), F32),
+        ((rows, model), BF16),
         ((width, model // depth // width, inner), BF16),
         ((out_piece[0] // 2, model), F32),
         ((8, inner), F32),
@@ -1814,6 +1822,8 @@
             pltpu.VMEM((out_piece[0] // 2, model), F32),
             pltpu.VMEM(in_piece, F32),
             pltpu.VMEM((in_piece[1], in_piece[0]), BF16),
+            pltpu.VMEM((CHUNK, 128), F32),
+            pltpu.VMEM((width, tokens // CHUNK, 128), F32),
             pltpu.SemaphoreType.DMA((48,)),
             pltpu.SemaphoreType.DMA((48,)),
             pltpu.SemaphoreType.DMA((12,)),
@@ -1826,40 +1836,62 @@
     )(*hbm, *vmem)
 
 
+def runs_of(width, half, run):
+    plane = width // 2
+    for place in range(width):
+        for j in range(half):
+            yield place, j * run, (((place % 2) * half + j) * plane + place // 2) * run
+
+
+def head_places(place, half, plane, group, heads, shift):
+    lane = lax.broadcasted_iota(jnp.int32, (128, 128), 0) - shift
+    head = lax.broadcasted_iota(jnp.int32, (128, 128), 1)
+    part = sum(((lane >= j * group).astype(jnp.int32) for j in range(1, half)), jnp.zeros_like(lane))
+    chosen = ((place % 2 * half + part) * plane + place // 2) * group + lane - part * group
+    return jnp.where((head == chosen) & (lane >= 0) & (lane < heads), 1.0, 0.0)
+
+
 def weights_kernel(
     dims,
+    d_x_hbm,
     normed_hbm,
-    d_gate_hbm,
-    d_x_hbm,
-    d_arg_hbm,
     wg_hbm,
     wx_hbm,
+    d_gate_hbm,
+    pre_hbm,
+    conv_hbm,
+    d_arg_hbm,
     wb_hbm,
-    w_dt_hbm,
-    pre_hbm,
+    cot_hbm,
     d_bc,
     taps,
     channel_sums,
     head_sums,
-    d_total,
-    x_back,
-    small_back,
-    sums_all,
+    head_sum,
+    rows_in,
+    x_own,
+    w_dt_all,
+    gate_back,
+    input_grad,
+    in_grad,
+    smalls,
+    d_x,
     normed_all,
-    d_gate,
-    d_x,
-    d_arg,
     wg,
     wx,
+    d_gate,
+    pre_own,
+    conv_own,
+    d_arg,
     wb,
-    w_dt,
-    pre_own,
-    bc_in,
+    cot_own,
+    w_turned,
     d_small,
-    w_small,
+    small_in,
     g_x,
     g_small,
     d_parts,
+    d_extra,
     d_ext,
     bc_landed,
     bc_sums,
@@ -1879,14 +1911,21 @@
     x_sent,
     small_sum,
     small_sent,
+    x_back,
+    small_back,
     sums_own,
     sums_line,
+    sums_all,
+    full,
     sends,
     recvs,
     locals_,
 ):
     depth, width, heads, head_size, size, kernel, own_ch, inner_all = dims
+    half, plane = depth // 2, width // 2
     inner = heads * head_size
+    run = inner // half
+    group = run // head_size
     model = normed_all.shape[2]
     piece = normed_all.shape[1] // 2
     rows = 2 * piece
@@ -1897,13 +1936,11 @@
     own = 2 * size // width
     row, place = lax.axis_index("dp"), lax.axis_index("seq")
     links = Links(sends, recvs)
-    above, below = lax.min(row + 1, depth - 1), lax.max(row - 1, 0)
     peer = {mask: (row, flip_all(place, mask)) for mask in range(1, width)}
     order = (6, 2, 4, 7, 3, 5, 1)
     per_block = 128 // own
-    bc_block = lax.div(place, per_block)
     bc_turn = 128 - own * lax.rem(place, per_block)
-    window = pl.ds(pl.multiple_of(inner + bc_block * 128, 128), 128)
+    window = pl.ds(pl.multiple_of(inner + lax.div(place, per_block) * 128, 128), 128)
 
     loads = [
         pltpu.make_async_copy(source, target, locals_.at[k])
@@ -1911,13 +1948,14 @@
             (
                 (d_x_hbm, d_x),
                 (normed_hbm, normed_all),
-                (pre_hbm.at[:, window], pre_own),
-                (wb_hbm, wb),
-                (w_dt_hbm, w_dt),
-                (d_arg_hbm, d_arg),
                 (wg_hbm, wg),
                 (wx_hbm, wx),
                 (d_gate_hbm, d_gate),
+                (pre_hbm.at[:, window], pre_own),
+                (conv_hbm.at[:, window], conv_own),
+                (d_arg_hbm, d_arg),
+                (wb_hbm, wb),
+                (cot_hbm.at[place], cot_own),
             )
         )
     ]
@@ -1926,8 +1964,9 @@
     line_peers = [(lax.rem(row + up, depth), place) for up in range(1, depth)]
     greet([peer[mask] for mask in range(1, width)] + line_peers)
 
-    bc_rows = PlaneRows(links, row, place, d_bc, bc_landed)
+    bc_rows = PlaneRows(links, row, place, d_bc, bc_landed, locals_.at[10])
     bc_rows.begin()
+    small_rows = PlaneRows(links, row, place, d_small, small_in, locals_.at[11])
     cols = model // depth
 
     def line(own_ref, buffers):
@@ -1943,9 +1982,9 @@
 
     x_line = line(g_x, (x_up_in, x_up_out, x_down_in, x_down_out))
     small_line = line(g_small, (small_up_in, small_up_out, small_down_in, small_down_out))
-    d_plane = PlaneSum(links, row, place, d_parts, d_total, d_pair, d_sums, d_relay, d_last)
-    send_x = SendBack(links, row, place, x_sent, x_back, locals_.at[9])
-    send_small = SendBack(links, row, place, small_sent, small_back, locals_.at[10])
+    d_plane = PlaneSum(links, row, place, d_parts, d_pair, d_sums, d_relay, d_last)
+    send_x = SendBack(links, row, place, x_sent, x_back, locals_.at[12])
+    send_small = SendBack(links, row, place, small_sent, small_back, locals_.at[13])
 
     def x_grad_tile(number, carry):
         at = pl.ds(pl.multiple_of(number * 128, 128), 128)
@@ -1956,7 +1995,36 @@
     loads[0].wait()
     loads[1].wait()
     lax.fori_loop(0, inner // 128, x_grad_tile, 0)
-    x_line.step(0)
+    x_line.phase(0)
+
+    for copy in loads[2:5]:
+        copy.wait()
+
+    def turn_weights(number, carry):
+        at = pl.ds(pl.multiple_of(number * 128, 128), 128)
+        w_turned[:inner, at] = wg[at, :].T
+        w_turned[inner:, at] = wx[at, :].T
+        return carry
+
+    lax.fori_loop(0, model // 128, turn_weights, 0)
+
+    def token_grads(index):
+        both = jnp.concatenate([d_gate[index], d_x[index]], axis=1)
+        d_parts[index] = mm(both, w_turned[...]).astype(BF16)
+
+    for mask in (6, 2, 4, 0):
+        token_grads(peer[mask ^ 1][1])
+        d_plane.pair[mask].start()
+    token_grads(peer[6][1])
+    d_plane.far()
+    token_grads(peer[2][1])
+    d_plane.near(2)
+    token_grads(peer[4][1])
+    d_plane.near(4)
+    if depth > 2:
+        x_line.phase(1)
+    token_grads(place)
+    d_plane.near(0)
 
     lane = lax.broadcasted_iota(jnp.int32, (1, 128), 1)
     mine = lane < own
@@ -1964,29 +2032,11 @@
     def to_front(values):
         return pltpu.roll(values, bc_turn, 1)
 
-    loads[3].wait()
-    loads[4].wait()
-
-    def small_weight(number, carry):
-        at = pl.ds(pl.multiple_of(number * 128, 128), 128)
-        bc = to_front(wb[bc_block, at, :].astype(F32))
-        dt = pltpu.roll(w_dt[at, :].astype(F32), own, 1)
-        w_small[at, :] = jnp.where(mine, bc, dt).astype(BF16)
-        return carry
-
-    lax.fori_loop(0, model // 128, small_weight, 0)
     own_taps = to_front(taps[:, window])
-
-    def project(index, carry):
-        bc_in[index] = mm(normed_all[index], w_small[...])
-        return carry
-
-    lax.fori_loop(0, width, project, 0)
-    loads[2].wait()
-    loads[5].wait()
+    for copy in loads[5:8]:
+        copy.wait()
     bc_rows.arrived()
     bc_sums[...] = jnp.zeros_like(bc_sums)
-    d_ext[...] = jnp.zeros_like(d_ext)
 
     def small_block(number, carry):
         slot, block = lax.div(number, per_slot), per_slot - 1 - lax.rem(number, per_slot)
@@ -1996,16 +2046,14 @@
         def _():
             d_ext[rows:, :] = jnp.zeros((8, 128), F32)
 
-        total = d_bc[place, :, at].astype(F32)
-        for k in range(width - 1):
-            total = total + bc_landed[k, :, at].astype(F32)
+        total = sum(bc_landed[k, :, at].astype(F32) for k in range(width))
         total = jnp.concatenate([total, jnp.zeros((128 - own, rows), F32)], axis=0)
         pre = to_front(pre_own[at, :])
         sig = sigmoid(pre)
         d_pre = jnp.where(mine, total.T * (sig * (1.0 + pre * (1.0 - sig))), 0.0)
         d_ext[0:rows, :] = d_pre
         where = (pl.ds(2 * block, 2), pl.ds(pl.multiple_of(slot * piece, piece), piece))
-        conv_in = bc_in[where[0], where[1], :].reshape(rows, 128)
+        conv_in = to_front(conv_own[at, :])
         d_conv = jnp.zeros((rows, 128), F32)
         for k in range(kernel):
             moved = d_ext[kernel - 1 - k : kernel - 1 - k + rows, :]
@@ -2021,37 +2069,27 @@
         return carry
 
     lax.fori_loop(0, blocks, small_block, 0)
+    small_rows.begin()
     g_small[...] = t_mm(
         d_small[...].reshape(everything, 128), normed_all[...].reshape(everything, model)
     )
-    small_line.step(0)
-    for copy in loads[6:]:
-        copy.wait()
-
-    def token_grads(index, carry):
-        total = (
-            mm_t(d_gate[index], wg[...])
-            + mm_t(d_x[index], wx[...])
-            + mm_t(d_small[index], w_small[...])
-        )
-        d_parts[index] = total.astype(BF16)
-        return carry
-
-    lax.fori_loop(0, width, token_grads, 0)
-    d_plane.begin()
-
+    small_line.phase(0)
     sums_own[:, :inner] = channel_sums[...]
     sums_own[:, inner : inner + 128] = bc_sums[...]
     sums_own[:, inner + 128 :] = head_sums[...]
+    sums_own[2:3, inner + 128 :] = dot(
+        channel_sums[...], head_sum[...], ((1,), (0,)), lax.Precision.HIGHEST
+    )[5:6]
     sums_copies = [
         links.copy(sums_own, sums_line.at[k], device) for k, device in enumerate(line_peers)
     ]
     for copy in sums_copies:
         copy.start()
+    d_plane.second()
+    if depth > 3:
+        x_line.phase(2)
     if depth > 2:
-        x_line.step(1)
-        small_line.step(1)
-    d_plane.first()
+        small_line.phase(1)
     for copy in sums_copies:
         copy.wait()
     total = jnp.zeros(sums_own.shape, F32)
@@ -2065,56 +2103,124 @@
     spread_sums = [links.copy(mine_all, mine_all, peer[mask]) for mask in order]
     for copy in spread_sums:
         copy.start()
-    if depth > 3:
-        x_line.step(2)
-        small_line.step(2)
-    d_plane.second()
+
+    small_rows.arrived()
+    for copy in loads[8:]:
+        copy.wait()
+    bc_tiles = [jnp.zeros((rows, 128), F32)] * (2 * size // 128)
+    d_dt_all = jnp.zeros((rows, 128), F32)
+    for source in range(width):
+        got = small_in[source]
+        moved = jnp.where(mine, got.astype(F32), 0.0)
+        turn_by = own * (source % per_block)
+        if turn_by:
+            moved = pltpu.roll(moved, turn_by, 1)
+        bc_tiles[source // per_block] = bc_tiles[source // per_block] + moved
+        places = head_places(source, half, plane, group, heads, own).astype(BF16)
+        d_dt_all = d_dt_all + mm(got, places)
+    extra = mm_t(d_dt_all.astype(BF16), w_dt_all[...])
+    for k, tile in enumerate(bc_tiles):
+        extra = extra + mm_t(tile.astype(BF16), wb[k])
+    d_extra[...] = extra
     x_line.finish(x_sum)
     turn(x_sent, x_sum)
     send_x.begin()
+    if depth > 3:
+        small_line.phase(2)
+
+    for source, at, to in runs_of(width, half, run):
+        in_grad[:, to : to + run] = gate_back[source, :, at : at + run].astype(F32)
     small_line.finish(small_sum)
     turn(small_sent, small_sum)
     send_small.begin()
-    d_plane.finish()
+    for copy in spread_sums:
+        copy.wait()
+    for source, at, to in runs_of(width, half, run):
+        full[:, to : to + run] = sums_all[source, :, at : at + run]
+    for source in range(width):
+        to = inner_all + source * own
+        full[:, to : to + own] = sums_all[source, :, inner : inner + own]
+    first = (row * width + place) * own_ch
+    base = pl.multiple_of(lax.div(first, 128) * 128, 128)
+    view = pltpu.roll(full[:, pl.ds(base, 256)], 256 - lax.rem(first, 128), 1)
+    smalls[0:8, :] = view[:, :128]
+    smalls[8:16, :] = sum(
+        dot(
+            sums_all[source, :, inner + 128 :],
+            head_places(source, half, plane, group, heads, 0),
+            ((1,), (0,)),
+            lax.Precision.HIGHEST,
+        )
+        for source in range(width)
+    )
+    send_x.end()
+    for source, at, to in runs_of(width, half, run):
+        in_grad[:, inner_all + to : inner_all + to + run] = x_back[
+            source, :, at : at + run
+        ].astype(F32)
+    send_small.end()
+    for source in range(width):
+        to = 2 * inner_all + source * own
+        in_grad[:, to : to + own] = small_back[source, :, :own].astype(F32)
+    for source, at, to in runs_of(width, half, group):
+        to = 2 * inner_all + 2 * size + to
+        in_grad[:, to : to + group] = small_back[
+            source, :, own + at : own + at + group
+        ].astype(F32)
+
+    norm_gain = rows_in[0:1, :]
+
+    def store_grad(at, total):
+        held = x_own[at].astype(F32)
+        inv = lax.rsqrt(jnp.mean(held * held, axis=1, keepdims=True) + EPS)
+        hat = held * inv
+        d_h = (total + d_extra[at]) * norm_gain
+        grad = inv * (d_h - hat * jnp.mean(d_h * hat, axis=1, keepdims=True))
+        input_grad[at] = (grad + cot_own[at].astype(F32)).astype(BF16)
+
+    d_plane.finish(store_grad)
     d_plane.drain()
     x_line.drain()
     small_line.drain()
-    send_x.end()
-    send_small.end()
     bc_rows.drain()
-    for copy in spread_sums:
-        copy.wait()
+    small_rows.drain()
 
 
 def weights(dims, hbm, vmem, collective):
     depth, width, heads, head_size, size, kernel, own_ch, inner_all = dims
     inner = heads * head_size
-    _, rows, model = hbm[0].shape
+    _, rows, model = hbm[1].shape
     tokens = rows * width
     shape = jax.ShapeDtypeStruct
     cols = model // depth
+    owned = cols // width
+    own = 2 * size // width
     kept = [
-        ((rows, model), F32),
-        ((width, cols // width, inner), BF16),
-        ((width, cols // width, 128), BF16),
-        ((width, 8, inner + 256), F32),
+        ((rows, model), BF16),
+        ((owned, 2 * inner_all + 2 * size + heads * width), F32),
+        ((16, 128), F32),
     ]
     return pl.pallas_call(
         functools.partial(weights_kernel, dims),
         out_shape=tuple(shape(*s) for s in kept),
         in_specs=[ANY] * len(hbm) + [INVMEM] * len(vmem),
         out_specs=(INVMEM,) * len(kept),
-        scratch_shapes=[pltpu.VMEM(v.shape, v.dtype) for v in hbm[:-1]]
+        scratch_shapes=[pltpu.VMEM(v.shape, v.dtype) for v in hbm[:5]]
         + [
             pltpu.VMEM((tokens, 128), F32),
-            pltpu.VMEM((width, rows, 128), F32),
+            pltpu.VMEM((tokens, 128), F32),
+            pltpu.VMEM(hbm[7].shape, BF16),
+            pltpu.VMEM(hbm[8].shape, BF16),
+            pltpu.VMEM((rows, model), BF16),
+            pltpu.VMEM((2 * inner, model), BF16),
             pltpu.VMEM((width, rows, 128), BF16),
-            pltpu.VMEM((model, 128), BF16),
+            pltpu.VMEM((width, rows, 128), BF16),
             pltpu.VMEM((inner, model), F32),
             pltpu.VMEM((128, model), F32),
             pltpu.VMEM((width, rows, model), BF16),
+            pltpu.VMEM((rows, model), F32),
             pltpu.VMEM((rows + 8, 128), F32),
-            pltpu.VMEM((width - 1, 2 * size // width, tokens), BF16),
+            pltpu.VMEM((width, own, tokens), BF16),
             pltpu.VMEM((8, 128), F32),
         ]
         + plane_buffers(rows, model)
@@ -2125,11 +2231,15 @@
             pltpu.VMEM((cols, inner), BF16),
             pltpu.VMEM((128, cols), F32),
             pltpu.VMEM((cols, 128), BF16),
+            pltpu.VMEM((width, owned, inner), BF16),
+            pltpu.VMEM((width, owned, 128), BF16),
             pltpu.VMEM((8, inner + 256), F32),
             pltpu.VMEM((depth - 1, 8, inner + 256), F32),
-            pltpu.SemaphoreType.DMA((80,)),
-            pltpu.SemaphoreType.DMA((80,)),
-            pltpu.SemaphoreType.DMA((12,)),
+            pltpu.VMEM((width, 8, inner + 256), F32),
+            pltpu.VMEM((8, inner_all + 2 * size + 256), F32),
+            pltpu.SemaphoreType.DMA((88,)),
+            pltpu.SemaphoreType.DMA((88,)),
+            pltpu.SemaphoreType.DMA((14,)),
         ],
         compiler_params=pltpu.CompilerParams(
             collective_id=collective, has_side_effects=True, vmem_limit_bytes=VMEM_LIMIT
@@ -2200,8 +2310,6 @@
     head_params = jnp.pad(
         jnp.stack([dt_bias, a_log, d_skip]), ((0, 5), (0, 128 - heads_all))
     )
-    input_f = block_input.astype(F32)
-    inv_rms = lax.rsqrt(jnp.mean(input_f * input_f, axis=-1, keepdims=True) + EPS)
     positions = place * piece + jnp.arange(piece, dtype=jnp.int32)
     live = (positions[None, :] < lengths[:, None]).astype(BF16)
     masked = cotangent * live[..., None]
@@ -2225,12 +2333,12 @@
         dt_arg,
         gate,
         y,
-        dgn,
         states,
         norms,
         taps,
         param_rows,
         w_dt,
+        w_dt_all,
     ) = forward(
         dims,
         block_input.reshape(tokens_dev, model),
@@ -2243,87 +2351,66 @@
         head_params,
         2,
     )
-    norm_all = param_rows[0].reshape(1, 1, model)
+    x_own = block_input.reshape(tokens_dev, model)
     head_sum = padded((jnp.arange(inner)[:, None] // head_size == jnp.arange(heads)).astype(F32))
     (
         d_gate,
         d_x,
         d_bc,
         d_arg,
-        o_total,
+        output,
         gate_back,
         out_grad,
         channel_sums,
         head_sums,
     ) = reverse(
         dims,
-        (cot_all, normed_all, gate, y, dgn, pre, conv_in, dt_arg, states, w_out),
-        (norms, taps, param_rows, head_sum),
+        (cot_all, normed_all, gate, y, pre, conv_in, dt_arg, states, w_out),
+        (norms, taps, param_rows, head_sum, x_own),
         3,
     )
     bc_own = 2 * size // width
-    d_total, x_back, small_back, smalls = weights(
+    input_grad, in_grad, smalls = weights(
         dims,
         (
+            d_x,
             normed_all,
-            d_gate,
-            d_x,
-            d_arg,
             w_gate.reshape(model, inner),
             w_x.reshape(model, inner),
+            d_gate,
+            pre,
+            conv_in,
+            d_arg,
             w_bc.reshape(2, model, size),
-            w_dt,
-            pre,
+            cot_all,
         ),
-        (d_bc.reshape(width, bc_own, tokens), taps, channel_sums, head_sums),
+        (
+            d_bc.reshape(width, bc_own, tokens),
+            taps,
+            channel_sums,
+            head_sums,
+            head_sum,
+            param_rows,
+            x_own,
+            w_dt_all,
+            gate_back,
+        ),
         4,
-    )
-
-    def to_whole(values, group):
-        count = values.shape[1]
-        split = values.reshape(plane, 2, count, half, group)
-        return jnp.transpose(split, (2, 1, 3, 0, 4)).reshape(count, -1)
-
-    conv_x = to_whole(smalls[:, :5, :inner], pair_rows)
-    conv_bc = jnp.swapaxes(smalls[:, :5, inner : inner + bc_own], 0, 1).reshape(5, 2 * size)
-    conv_grads = lax.dynamic_slice_in_dim(
-        jnp.concatenate([conv_x, conv_bc], axis=1), (row * width + place) * own_ch, own_ch, 1
-    )
-    skip_sum = jnp.sum(smalls[:, 5:6, :inner].reshape(width, 1, heads, head_size), axis=3)
-    head_grads = to_whole(
-        jnp.concatenate([smalls[:, :2, inner + 128 : inner + 128 + heads], skip_sum], axis=1),
-        pair_rows // head_size,
-    )
-    small_f = small_back.astype(F32)
-    in_grad = jnp.concatenate(
-        [
-            to_whole(gate_back.astype(F32), pair_rows),
-            to_whole(x_back.astype(F32), pair_rows),
-            jnp.swapaxes(small_f[:, :, :bc_own], 0, 1).reshape(in_rows, 2 * size),
-            to_whole(small_f[:, :, bc_own : bc_own + heads], pair_rows // head_size),
-        ],
-        axis=1,
     )
     norm_grad = jnp.sum(in_grad * in_weight.astype(F32), axis=1) / norm_gain.astype(F32)
     gate_grad = jnp.sum(out_grad * out_weight.astype(F32), axis=1) / gate_gain.astype(F32)
-
-    output = (input_f + o_total.reshape(slots, piece, model)).astype(BF16)
-    in_hat = input_f * inv_rms
-    d_h = d_total.reshape(slots, piece, model) * norm_all.astype(F32)
-    input_grad = inv_rms * (d_h - in_hat * jnp.mean(d_h * in_hat, axis=-1, keepdims=True))
-    input_grad = (input_grad + masked.astype(F32)).astype(BF16)
     return (
-        output,
-        input_grad,
+        output.reshape(slots, piece, model),
+        input_grad.reshape(slots, piece, model),
         in_grad,
         out_grad,
         norm_grad,
         gate_grad,
-        conv_grads[:4],
-        conv_grads[4],
-        head_grads[0],
-        head_grads[1],
-        head_grads[2],
+        smalls[:4, :own_ch],
+        smalls[4, :own_ch],
+        smalls[8, :heads_all],
+        smalls[9, :heads_all],
+        smalls[10, :heads_all],
     )
 
 

time: 308 us -> 258 us (0.84)
  Pallas kernels: 278 us -> 234 us
  local copies, waits for them, and re-layouts: 18 us -> 11.9 us
    pallas_call x1, Pallas kernels: 86 us -> 59.9 us  [weights(): pl.pallas_call(functools.partial(weights_kernel, dims), out_shape=tuple((...]
    pallas_call x1, Pallas kernels: 93.5 us -> 80.2 us  [reverse(): pl.pallas_call(functools.partial(reverse_kernel, dims), out_shape=tuple((...]
    pallas_call x1, Pallas kernels: 98.7 us -> 94.3 us  [forward(): pl.pallas_call(functools.partial(forward_kernel, dims), out_shape=tuple((...]
    reshape x13 -> x0, local copies, waits for them, and re-layouts: 4.33 us -> none  [the longest x9 3.95 us: to_whole(): return jnp.transpose(split, (2, 1, 3, 0, 4)).reshape(count, -1)]
    slice x13 -> x1, local copies, waits for them, and re-layouts: 4.26 us -> 0.58 us  [fast_body(): smalls[:4, :own_ch]]
where the time goes in v3:
time: 258 us; the launch traced here: 255 us
  Pallas kernels  234 us (91%)
  local copies, waits for them, and re-layouts  11.9 us (5%)
  other arithmetic  8.03 us (3%)
    pallas_call x1, Pallas kernels, forward(): pl.pallas_call(functools.partial(forward_kernel, dims), out_shape=tuple((...  94.3 us
    pallas_call x1, Pallas kernels, reverse(): pl.pallas_call(functools.partial(reverse_kernel, dims), out_shape=tuple((...  80.2 us
    pallas_call x1, Pallas kernels, weights(): pl.pallas_call(functools.partial(weights_kernel, dims), out_shape=tuple((...  59.9 us

profile of v3, /device:TPU:9, one launch (start us, length us, event | category | flops | bytes accessed | tf_op | source)
XLA Modules:
  0.0 255.1 jit_solution(1753517325218789740)
XLA Ops:
  0.7 0.7 compare_convert_fusion
  1.4 1.3 select_maximum_fusion.head_params
  2.7 0.7 slice.30
  3.4 1.3 pad_add_fusion.pack
  4.7 1.3 bitcast_bitcast_fusion.wb_send
  6.1 0.1 iota_compare_fusion
  6.2 0.7 pad_convert_fusion.head_sum
  6.9 1.1 fusion.3
  8.0 0.5 reshape.136
  8.5 0.3 copy.32
  8.8 0.0 copy-start.4
  8.8 0.9 reshape.137.wx_send
  9.7 0.5 reshape.134
  10.2 0.3 copy.33
  10.5 0.9 reshape.135.wg_send
  11.5 0.0 copy-done.4
  11.5 1.0 broadcast_multiply_fusion
  12.5 94.3 %forward_fused.1 = (bf16[8,256,1536]{2,1,0:T(8,128)(2,1)}, bf16[8,256,1536]{2,1,0:T(8,128)(2,1)}, bf16[4,8,48,384]{3,2,1,0:T(8,128)(2,1)}, bf16[4,8,48,384]{3,2,...) custom-call(bf16[256,1536]{1,0:T(8,128)(2,1)} %bitcast.35, ...), custom_call_target="tpu_custom_call" | custom-call | tf_op jit(solution)/shard_map/forward_fused/pallas_call | solution.py:1241
  106.8 80.2 %reverse_fused.1 = (bf16[8,256,384]{2,1,0:T(8,128)(2,1)}, bf16[8,256,384]{2,1,0:T(8,128)(2,1)}, bf16[256,2048]{1,0:T(8,128)(2,1)}, bf16[8,256,128]{2,1,0:T(8,128...) custom-call(bf16[8,256,1536]{2,1,0:T(8,128)(2,1)} %get-tuple-element, ...), custom_call_target="tpu_custom_call" | custom-call | tf_op jit(solution)/shard_map/reverse_fused/pallas_call | solution.py:1798
  187.0 0.0 copy-start.1
  187.0 59.9 %weights_fused.1 = (bf16[256,1536]{1,0:T(8,128)(2,1)}, f32[48,6448]{1,0:T(8,128)}, f32[16,128]{1,0:T(8,128)}) custom-call(bf16[8,256,384]{2,1,0:T(8,128)(2,1)} %get-tuple-element.52.d_x_hbm, bf16[8,256,1536]{2,1,0:T(8,128)(2,1)} %get-tuple-element.40.normed_hbm, bf16[1536,384]{1,0:T(8,128)(2,1)} %bitcast.41, bf16[1536,384]{1,0:T(8,128)(2,1)} %bitcast.42, ...), custom_call_target="tpu_custom_call" | custom-call | tf_op jit(solution)/shard_map/weights_fused/pallas_call | solution.py:2203
  246.9 0.0 copy-start.8
  246.9 0.0 copy-start.7
  246.9 0.0 copy-start.2
  247.0 0.0 copy-start.3
  247.0 0.0 copy-start.9
  247.0 0.0 copy-start.5
  247.0 0.0 copy-done.1
  247.0 1.6 multiply_reduce_fusion
  248.6 0.0 copy-done.8
  248.7 0.0 copy-start.6
  248.7 0.5 convert_divide_fusion.1
  249.2 0.0 copy-done.7
  249.2 0.5 slice_bitcast_fusion.4
  249.7 0.0 copy-done.2
  249.7 0.0 copy-done.3
  249.7 0.2 multiply_reduce_fusion.1
  249.9 0.0 copy-done.9
  249.9 0.5 convert_divide_fusion
  250.4 0.5 slice_bitcast_fusion.1
  250.9 0.6 slice.31
  251.5 0.0 copy-done.5
  251.5 0.0 copy-start
  251.5 0.9 copy.38
  252.4 0.0 copy-done.6
  252.4 0.9 copy.39
  253.3 0.0 copy-done
  253.3 1.0 copy.40
  254.3 0.8 copy.41
  (2 shorter events, 0.0 us)
Async XLA Ops:
  8.8 2.7 %copy-start.4 = (bf16[2,128,1536]{2,1,0:T(8,128)(2,1)S(1)}, bf16[2,128,1536]{2,1,0:T(8,128)(2,1)}, u32[]{:S(2)}) copy-start(bf16[2,128,1536]{2,1,0:T(8,128)(2,1)} %param.13) | copy-start | bytes 2359300
  187.0 60.0 %copy-start.1 = (bf16[48,6448]{1,0:T(8,128)(2,1)S(1)}, bf16[48,6448]{1,0:T(8,128)(2,1)}, u32[]{:S(2)}) copy-start(bf16[48,6448]{1,0:T(8,128)(2,1)} %param.15) | copy-start | bytes 1857028
  246.9 1.7 copy-start.8
  246.9 2.2 copy-start.7
  246.9 2.8 %copy-start.2 = (f32[96,1536]{1,0:T(8,128)S(1)}, f32[96,1536]{1,0:T(8,128)}, u32[]{:S(2)}) copy-start(f32[96,1536]{1,0:T(8,128)} %get-tuple-element.86) | copy-start | bytes 1769476
  247.0 2.7 %copy-start.3 = (bf16[96,1536]{1,0:T(8,128)(2,1)S(1)}, bf16[96,1536]{1,0:T(8,128)(2,1)}, u32[]{:S(2)}) copy-start(bf16[96,1536]{1,0:T(8,128)(2,1)} %wo_own.1) | copy-start | bytes 884740
  247.0 2.9 %copy-start.9 = (bf16[96]{0:T(256)(128)(2,1)S(1)}, bf16[96]{0:T(256)(128)(2,1)}, u32[]{:S(2)}) copy-start(bf16[96]{0:T(256)(128)(2,1)} %param.18) | copy-start | bytes 580
  247.0 4.5 %copy-start.5 = (bf16[256,1536]{1,0:T(8,128)(2,1)S(1)}, bf16[256,1536]{1,0:T(8,128)(2,1)}, u32[]{:S(2)}) copy-start(bf16[256,1536]{1,0:T(8,128)(2,1)} %get-tuple-element.51) | copy-start | bytes 2359300
  248.7 3.7 %copy-start.6 = (bf16[256,1536]{1,0:T(8,128)(2,1)S(1)}, bf16[256,1536]{1,0:T(8,128)(2,1)}, u32[]{:S(2)}) copy-start(bf16[256,1536]{1,0:T(8,128)(2,1)} %get-tuple-element.63) | copy-start | bytes 2359300
  251.5 1.8 copy-start

commit v4 on v3

--- a/solution.py
+++ b/solution.py
@@ -430,7 +430,7 @@
         )
 
 
-def greet(devices, conditions=()):
+def greet(devices, conditions=(), between=None):
     barrier = pltpu.get_barrier_semaphore()
     for device in devices:
         pl.semaphore_signal(barrier, inc=1, device_id=device, device_id_type=MESH_ID)
@@ -443,6 +443,8 @@
     count = len(devices)
     for condition, _ in conditions:
         count = count + jnp.where(condition, 1, 0)
+    if between is not None:
+        between()
     pl.semaphore_wait(barrier, count)
 
 
@@ -641,8 +643,22 @@
     return jnp.concatenate(parts, axis=1)
 
 
+def head_of_channel(inner, head_size):
+    channel = lax.broadcasted_iota(jnp.int32, (inner, 128), 0)
+    first = lax.broadcasted_iota(jnp.int32, (inner, 128), 1) * head_size
+    return jnp.where((channel >= first) & (channel < first + head_size), 1.0, 0.0)
+
+
 def sigmoid(values):
-    return 1.0 / (1.0 + jnp.exp(-values))
+    return 0.5 * jnp.tanh(0.5 * values) + 0.5
+
+
+def in_parts(values, count):
+    parts = []
+    for _ in range(count):
+        parts.append(values.astype(BF16))
+        values = values - parts[-1].astype(F32)
+    return parts
 
 
 def softplus(values):
@@ -659,6 +675,12 @@
     rows = lax.broadcasted_iota(jnp.int32, (CHUNK, CHUNK), 0)
     cols = lax.broadcasted_iota(jnp.int32, (CHUNK, CHUNK), 1)
     return rows >= cols
+
+
+def triangles_up():
+    rows = lax.broadcasted_iota(jnp.int32, (CHUNK, CHUNK), 0)
+    cols = lax.broadcasted_iota(jnp.int32, (CHUNK, CHUNK), 1)
+    return cols >= rows
 
 
 def head_decays(cum, cum_t, head, causal):
@@ -827,17 +849,20 @@
 def forward_kernel(
     dims,
     x_own,
-    cot_own,
-    wg_send,
-    wx_send,
-    wb_send,
+    cot_in,
+    lengths,
+    in_weight,
     wo_own,
-    pack,
-    head_params,
+    norm_in,
+    gate_in,
+    conv_w_in,
+    conv_b_in,
+    dt_bias_in,
+    a_log_in,
+    d_skip_in,
     normed_out,
     cot_out,
-    wg_out,
-    wx_out,
+    turned_out,
     wb_out,
     wo_out,
     conv_out,
@@ -850,15 +875,16 @@
     taps_out,
     rows_out,
     w_dt_out,
-    w_dt_all_out,
     x_all,
     normed_all,
     cot_all,
     wg,
     wx,
-    wb,
+    wb_far,
     wo,
     packs,
+    dt_got,
+    turned,
     conv_in,
     pre_all,
     dt_all,
@@ -870,6 +896,14 @@
     full,
     sums,
     sums_in,
+    cot_own,
+    wg_send,
+    wx_send,
+    pack,
+    dt_own,
+    dt_pack,
+    dt_send,
+    head_params,
     sends,
     recvs,
     locals_,
@@ -889,45 +923,76 @@
     links = Links(sends, recvs)
     peer = {mask: (row, flip_all(place, mask)) for mask in range(1, width)}
     line_peers = [(lax.rem(row + up, depth), place) for up in range(1, depth)]
-    greet([peer[mask] for mask in range(1, width)] + line_peers)
-
+    in_rows = in_weight.shape[0]
+    bc_cols = 2 * inner_all
+
+    def prepare():
+        for target, at, to in runs_of(width, half, run):
+            wx_send[target, :, at : at + run] = in_weight[:, inner_all + to : inner_all + to + run]
+        for target in range(width):
+            first = bc_cols + target % 2 * size
+            wx_send[target, :, inner:] = in_weight[:, first : first + size]
+
+    greet([peer[mask] for mask in range(1, width)] + line_peers, between=prepare)
     kept = [
         pltpu.make_async_copy(wx_send.at[place], wx.at[row, place], locals_.at[0]),
-        pltpu.make_async_copy(wb_send.at[core], wb.at[core, row, place], locals_.at[1]),
+        pltpu.make_async_copy(dt_send.at[place], dt_got.at[place], locals_.at[1]),
         pltpu.make_async_copy(wg_send.at[place], wg.at[row, place], locals_.at[2]),
         pltpu.make_async_copy(x_own, x_all.at[place], locals_.at[3]),
         pltpu.make_async_copy(cot_own, cot_all.at[place], locals_.at[4]),
         pltpu.make_async_copy(pack, packs.at[row, place], locals_.at[5]),
     ]
-    for copy in kept:
-        copy.start()
+    for number in (0, 3):
+        kept[number].start()
 
     out_home = lax.div(row, half) == core
     out_block = wo.at[lax.rem(row, half), core]
     out_kept = pltpu.make_async_copy(wo_own, out_block, locals_.at[6])
     out_pair = links.copy(wo_own, out_block, peer[1])
-    pl.when(out_home)(out_kept.start)
-    pl.when(jnp.logical_not(out_home))(out_pair.start)
-
     order = (6, 2, 4, 7, 3, 5, 1)
     plane_x, plane_g = [], []
     for mask in order:
         target = peer[mask][1]
-        its_core = lax.rem(target, 2)
         plane_x.append(links.copy(wx_send.at[target], wx.at[row, place], peer[mask]))
-        plane_x.append(
-            links.copy(wb_send.at[its_core], wb.at[its_core, row, place], peer[mask])
-        )
         plane_g.append(links.copy(wg_send.at[target], wg.at[row, place], peer[mask]))
     for copy in plane_x:
         copy.start()
-    pack_line = [links.copy(pack, packs.at[row, place], device) for device in line_peers]
-    for copy in pack_line:
-        copy.start()
+    pl.when(out_home)(out_kept.start)
+    pl.when(jnp.logical_not(out_home))(out_pair.start)
     x_pass = Pass(links, peer, place, x_own, x_all)
     cot_pass = Pass(links, peer, place, cot_own, cot_all)
     x_pass.first()
 
+    dt_own[...] = jnp.zeros_like(dt_own)
+    last = in_weight.shape[1]
+    dt_own[:, 0 : last - bc_cols - 2 * size] = in_weight[:, bc_cols + 2 * size : last]
+    dt_pack[row] = dt_own[...]
+    lines = [conv_w_in[...], conv_b_in[...], gate_in[...], norm_in[...]]
+    small_rows = jnp.concatenate(
+        [jnp.pad(v.astype(F32), ((0, 0), (0, 128 - v.shape[1]))) for v in lines]
+        + [jnp.zeros((16 - sum(v.shape[0] for v in lines), 128), F32)],
+        axis=0,
+    )
+    pack[...] = small_rows.astype(BF16)
+    pack_line = [links.copy(pack, packs.at[row, place], device) for device in line_peers]
+    pack_line += [
+        links.copy(dt_own, dt_pack.at[row], device) for device in line_peers
+    ]
+    for copy in pack_line:
+        copy.start()
+    kept[5].start()
+    head_params[...] = jnp.zeros_like(head_params)
+    for k, v in enumerate((dt_bias_in, a_log_in, d_skip_in)):
+        head_params[k : k + 1, 0 : v.shape[1]] = v[...]
+    for target, at, to in runs_of(width, half, run):
+        wg_send[target, :, at : at + run] = in_weight[:, to : to + run]
+    kept[2].start()
+    token = lax.broadcasted_iota(jnp.int32, (piece, model), 0) + place * piece
+    for slot in range(slots):
+        live = token < lengths[0:1, slot : slot + 1]
+        part = slice(slot * piece, (slot + 1) * piece)
+        cot_own[part, :] = jnp.where(live, cot_in[part, :].astype(F32), 0.0).astype(BF16)
+    kept[4].start()
     out_line = Line(
         links,
         depth,
@@ -936,35 +1001,47 @@
         lambda shard: [wo.at[lax.rem(shard, half)]],
         lambda shard: lax.div(shard, half) == core,
     )
-    x_line = Line(links, depth, row, place, lambda shard: [wx.at[shard], wb.at[core, shard]])
+    x_line = Line(links, depth, row, place, lambda shard: [wx.at[shard]])
     gate_line = Line(links, depth, row, place, lambda shard: [wg.at[shard]])
 
     pl.when(out_home)(out_kept.wait)
     pl.when(out_home)(out_pair.wait_recv)
     out_line.send(0)
     kept[0].wait()
-    kept[1].wait()
     for copy in plane_x:
         copy.wait_recv()
     x_line.send(0)
+    for copy in plane_g:
+        copy.start()
     kept[5].wait()
     for copy in pack_line:
         copy.wait_recv()
+    targets = jnp.concatenate(
+        [head_choice(target, plane, half, run // head_size, heads)[:, :16] for target in range(width)],
+        axis=1,
+    ).astype(BF16)
+    dt_rows = dot(targets, dt_pack[...].reshape(depth * in_rows, 128), ((0,), (1,)))
+    dt_send[...] = jnp.zeros_like(dt_send)
+    dt_send[:, :, 0 : depth * in_rows] = dt_rows.astype(BF16).reshape(width, 16, depth * in_rows)
+    kept[1].start()
     mine = packs.at[:, place]
     pack_plane = [links.copy(mine, mine, peer[mask]) for mask in order]
+    pack_plane += [
+        links.copy(dt_send.at[peer[mask][1]], dt_got.at[place], peer[mask]) for mask in order
+    ]
     for copy in pack_plane:
         copy.start()
-    for copy in plane_g:
-        copy.start()
     x_pass.relay()
+    cot_pass.first()
     x_line.wait(0)
     if depth > 2:
         x_line.send(1)
+    kept[1].wait()
     for copy in pack_plane:
         copy.wait_recv()
 
     small = [
-        packs[z, s, model // (depth * width) : model // (depth * width) + 16, :].astype(F32)[:8]
+        packs[z, s].astype(F32)[:8]
         for z in range(depth)
         for s in range(width)
     ]
@@ -984,9 +1061,19 @@
     lane = lax.broadcasted_iota(jnp.int32, (1, 128), 1)
     rates = jnp.where(lane < heads, -jnp.exp(chosen[1:2]), 0.0)
     skip = widen(chosen[2:3], heads, head_size)
-    dt_rows = packs[:, :, 0 : model // (depth * width), :].reshape(model, 128)
-    w_dt_all_out[...] = dt_rows
-    w_dt_out[...] = mm(dt_rows, choice.astype(BF16)).astype(BF16)
+    dt_tiles = lay_out(
+        [
+            pltpu.roll(dt_got[s].astype(F32), 256 - z * in_rows, 1)[:, :128]
+            if z
+            else dt_got[s].astype(F32)[:, :128]
+            for z in range(depth)
+            for s in range(width)
+        ],
+        0,
+        in_rows,
+    )
+    w_dt_out[...] = jnp.zeros_like(w_dt_out)
+    w_dt_out[0:16, :] = jnp.concatenate(dt_tiles, axis=1).astype(BF16)
     rows_out[...] = jnp.zeros_like(rows_out)
     rows_out[0:1, :] = norm_gain
     rows_out[1:2, :inner] = gate_gain
@@ -995,7 +1082,6 @@
     rows_out[4:5, :128] = rates
 
     x_pass.last()
-    cot_pass.first()
 
     def normalise(index, carry):
         for part in range(2):
@@ -1018,15 +1104,15 @@
     if depth > 3:
         x_line.wait(2)
     gate_line.send(0)
-    mine_bc = wb.at[core]
-    pair_bc = links.copy(mine_bc, mine_bc, peer[1])
+    near_bc = wx.at[:, :, :, pl.ds(inner, size)]
+    pair_bc = links.copy(near_bc, wb_far, peer[1])
     pair_bc.start()
     saves = [pltpu.make_async_copy(normed_all, normed_out, locals_.at[7])]
     saves[0].start()
     pair_bc.wait_recv()
 
     causal = triangles()
-    ones = causal.astype(F32)
+    ones_three = jnp.concatenate([causal.astype(BF16)] * 3, axis=1)
 
     def stored(index):
         at = pl.ds(pl.multiple_of(index * rows, rows), rows)
@@ -1059,10 +1145,13 @@
         tokens = normed_all[
             pl.ds(2 * block, 2), pl.ds(pl.multiple_of(slot * piece, piece), piece), :
         ].reshape(rows, model)
-        ext[8:, :inner] = mm(tokens, wx[...].reshape(model, inner))
-        ext[8:, inner : inner + size] = mm(tokens, wb[0].reshape(model, size))
-        ext[8:, inner + size :] = mm(tokens, wb[1].reshape(model, size))
-        dt_arg = mm(tokens, w_dt_out[...]) + rows_out[3:4, :128]
+        mine = mm(tokens, wx[...].reshape(model, inner + size))
+        ext[8:, :inner] = mine[:, :inner]
+        ext[8:, pl.ds(pl.multiple_of(inner + core * size, 128), size)] = mine[:, inner:]
+        ext[8:, pl.ds(pl.multiple_of(inner + (1 - core) * size, 128), size)] = mm(
+            tokens, wb_far[...].reshape(model, size)
+        )
+        dt_arg = mm_t(tokens, w_dt_out[...]) + rows_out[3:4, :128]
         dt_all[pl.ds(at, rows), :] = dt_arg
         pre = taps_out[kernel : kernel + 1, :] + sum(
             taps_out[k : k + 1, :] * ext[9 - kernel + k : 9 - kernel + k + rows, :]
@@ -1074,40 +1163,59 @@
         act = pre * sigmoid(pre)
         dt_block = softplus(dt_arg)
         steps_block = dt_block * rows_out[4:5, :128]
-        for sub in range(rows // CHUNK):
-            part = slice(sub * CHUNK, (sub + 1) * CHUNK)
-            x = act[part, :inner]
-            b = act[part, inner : inner + size].astype(BF16)
-            c = act[part, inner + size :].astype(BF16)
-            cum = dot(ones, steps_block[part], ((1,), (0,)), lax.Precision.HIGHEST)
-            cum_t = cum.T
-            total = cum[CHUNK - 1 : CHUNK, :]
-            x_dt = x * widen(dt_block[part], heads, head_size)
-            x_dt16 = x_dt.astype(BF16)
-            held = state[...]
-            held16 = held.astype(BF16)
-            states[index * (rows // CHUNK) + sub] = held16
-            y = mm(c, held16) * widen(jnp.exp(cum), heads, head_size)
-            y = y + rows_out[2:3, :inner] * x
-            cb = mm_t(c, b)
+        subs = rows // CHUNK
+        parts = [slice(sub * CHUNK, (sub + 1) * CHUNK) for sub in range(subs)]
+        x = act[:, :inner]
+        b = act[:, inner : inner + size].astype(BF16)
+        c = act[:, inner + size :].astype(BF16)
+        cums = [
+            mm(ones_three, jnp.concatenate(in_parts(steps_block[part], 3), axis=0))
+            for part in parts
+        ]
+        lasts = [cum[CHUNK - 1 : CHUNK, :] for cum in cums]
+        x_dt = x * widen(dt_block, heads, head_size)
+        x_dt16 = x_dt.astype(BF16)
+        cum_wide = widen(jnp.exp(jnp.concatenate(cums, axis=0)), heads, head_size)
+        out_wide = widen(
+            jnp.exp(jnp.concatenate([last - cum for last, cum in zip(lasts, cums)], axis=0)),
+            heads,
+            head_size,
+        )
+        weighted = (x_dt * out_wide).astype(BF16)
+        near, read = [], []
+        for sub, part in enumerate(parts):
+            cum_t = cums[sub].T
+            cb = mm_t(c[part], b[part])
             pieces = []
             for pair in range(heads // 2):
                 lanes = slice(2 * pair * head_size, 2 * (pair + 1) * head_size)
                 mixing = jnp.concatenate(
                     [
-                        (head_decays(cum, cum_t, 2 * pair + k, causal) * cb).astype(BF16)
+                        (head_decays(cums[sub], cum_t, 2 * pair + k, causal) * cb).astype(BF16)
                         for k in range(2)
                     ],
                     axis=1,
                 )
                 pieces.append(
-                    mm(mixing, jnp.concatenate(split_pair(x_dt16[:, lanes], head_size), axis=0))
+                    mm(
+                        mixing,
+                        jnp.concatenate(split_pair(x_dt16[part, lanes], head_size), axis=0),
+                    )
                 )
-            y_all[pl.ds(pl.multiple_of(at + sub * CHUNK, CHUNK), CHUNK), :] = y + jnp.concatenate(
-                pieces, axis=1
+            near.append(jnp.concatenate(pieces, axis=1))
+        for sub, part in enumerate(parts):
+            held = state[...]
+            held16 = held.astype(BF16)
+            states[index * subs + sub] = held16
+            read.append(mm(c[part], held16))
+            state[...] = held * widen(jnp.exp(lasts[sub]), heads, head_size) + t_mm(
+                b[part], weighted[part]
             )
-            weighted = (x_dt * widen(jnp.exp(total - cum), heads, head_size)).astype(BF16)
-            state[...] = held * widen(jnp.exp(total), heads, head_size) + t_mm(b, weighted)
+        y_all[pl.ds(at, rows), :] = (
+            jnp.concatenate(near, axis=0)
+            + jnp.concatenate(read, axis=0) * cum_wide
+            + rows_out[2:3, :inner] * x
+        )
         for copy in stored(index):
             copy.start()
 
@@ -1174,24 +1282,33 @@
         return carry
 
     lax.fori_loop(0, blocks, gate_block, 0)
+    squares = plane_total(links, sums, sums_in, peer, 2 * blocks)
     save_gate = pltpu.make_async_copy(gate_all, gate_out, locals_.at[8])
     save_gate.start()
+    wg_flat, wx_flat = wg[...].reshape(model, inner), wx[...].reshape(model, inner + size)
+    for at in range(0, model, 128):
+        turned[:inner, at : at + 128] = wg_flat[at : at + 128, :].T
+        turned[inner:, at : at + 128] = wx_flat[at : at + 128, :inner].T
+    save_weights = [
+        pltpu.make_async_copy(source, target, locals_.at[10 + k])
+        for k, (source, target) in enumerate(
+            (
+                (turned, turned_out),
+                (near_bc, wb_out.at[core]),
+                (wb_far, wb_out.at[1 - core]),
+                (wo, wo_out),
+            )
+        )
+    ]
+    for copy in save_weights[:3]:
+        copy.start()
     cot_pass.end()
     kept[4].wait()
     save_cot = pltpu.make_async_copy(cot_all, cot_out, locals_.at[9])
     save_cot.start()
     if depth > 3:
         out_line.wait(2)
-    save_weights = [
-        pltpu.make_async_copy(source, target, locals_.at[10 + k])
-        for k, (source, target) in enumerate(
-            ((wg, wg_out), (wx, wx_out), (wb, wb_out), (wo, wo_out))
-        )
-    ]
-    for copy in save_weights:
-        copy.start()
-
-    squares = plane_total(links, sums, sums_in, peer, 2 * blocks)
+    save_weights[3].start()
     inv_gate = lax.rsqrt(squares() / inner_all + EPS)
     norms_out[...] = by_column(inv_gate)
 
@@ -1214,18 +1331,25 @@
     lax.fori_loop(0, blocks, stores_end, 0)
 
 
-def forward(dims, x_own, cot_own, wg_send, wx_send, wb_send, wo_own, pack, head_params, collective):
+def forward(dims, arrays, collective):
     depth, width, heads, head_size, size, kernel, own_ch, inner_all = dims
     inner = heads * head_size
+    x_own, _, _, in_weight, wo_own = arrays[:5]
     rows, model = x_own.shape
+    in_rows = in_weight.shape[0]
     tokens = rows * width
     wide = inner + 2 * size
     shape = jax.ShapeDtypeStruct
     chunks = tokens // CHUNK
     weights = [
-        ((depth,) + wg_send.shape, BF16),
-        ((depth,) + wx_send.shape, BF16),
-        ((2, depth, width) + wb_send.shape[1:], BF16),
+        ((depth, width, in_rows, inner), BF16),
+        ((depth, width, in_rows, inner + size), BF16),
+        ((depth, width, in_rows, size), BF16),
+        ((depth // 2, 2) + wo_own.shape, BF16),
+    ]
+    passed = [
+        ((2 * inner, model), BF16),
+        ((2, depth, width, in_rows, size), BF16),
         ((depth // 2, 2) + wo_own.shape, BF16),
     ]
     kept = [
@@ -1236,16 +1360,20 @@
         ((tokens, inner), F32),
         ((chunks, size, inner), BF16),
     ]
-    in_hbm = [((width, rows, model), BF16)] * 2 + weights + kept
-    in_vmem = [((CHUNK, 128), F32), ((8, wide), F32), ((8, model), F32)] + [((model, 128), BF16)] * 2
+    in_hbm = [((width, rows, model), BF16)] * 2 + passed + kept
+    in_vmem = [((CHUNK, 128), F32), ((8, wide), F32), ((8, model), F32), ((128, model), BF16)]
     return pl.pallas_call(
         functools.partial(forward_kernel, dims),
         out_shape=tuple(shape(*s) for s in in_hbm + in_vmem),
-        in_specs=[INVMEM] * 8,
+        in_specs=[INVMEM] * len(arrays),
         out_specs=(ANY,) * len(in_hbm) + (INVMEM,) * len(in_vmem),
         scratch_shapes=[pltpu.VMEM((width, rows, model), BF16)] * 3
         + [pltpu.VMEM(*s) for s in weights]
-        + [pltpu.VMEM((depth, width) + pack.shape, BF16)]
+        + [
+            pltpu.VMEM((depth, width, 16, 128), BF16),
+            pltpu.VMEM((width, 16, 256), BF16),
+            pltpu.VMEM((2 * inner, model), BF16),
+        ]
         + [pltpu.VMEM(*s) for s in kept]
         + [
             pltpu.VMEM((rows + 8, wide), F32),
@@ -1253,6 +1381,14 @@
             pltpu.VMEM((8, -(-own_ch * depth * width // 128) * 128), F32),
             pltpu.VMEM((CHUNK, 128), F32),
             pltpu.VMEM((width, chunks, 128), F32),
+            pltpu.VMEM((rows, model), BF16),
+            pltpu.VMEM((width, in_rows, inner), BF16),
+            pltpu.VMEM((width, in_rows, inner + size), BF16),
+            pltpu.VMEM((16, 128), BF16),
+            pltpu.VMEM((in_rows, 128), BF16),
+            pltpu.VMEM((depth, in_rows, 128), BF16),
+            pltpu.VMEM((width, 16, 256), BF16),
+            pltpu.VMEM((8, 128), F32),
             pltpu.SemaphoreType.DMA((112,)),
             pltpu.SemaphoreType.DMA((112,)),
             pltpu.SemaphoreType.DMA((16,)),
@@ -1262,29 +1398,25 @@
             collective_id=collective, has_side_effects=True, vmem_limit_bytes=VMEM_LIMIT
         ),
         name="forward_fused",
-    )(x_own, cot_own, wg_send, wx_send, wb_send, wo_own, pack, head_params)
+    )(*arrays)
 
 
 class PlaneRows:
-    def __init__(self, links, row, place, parts, landed, local):
-        mine = landed.at[place]
+    def __init__(self, links, row, place, parts, landed, at, local):
+        mine = landed.at[place, :, at]
         peers = [(row, flip_all(place, mask)) for mask in (6, 7, 2, 3, 4, 5, 1)]
-        self.copies = [links.copy(parts.at[peer[1]], mine, peer) for peer in peers]
-        self.kept = pltpu.make_async_copy(parts.at[place], mine, local)
+        self.copies = [links.copy(parts.at[peer[1], :, at], mine, peer) for peer in peers]
+        self.kept = pltpu.make_async_copy(parts.at[place, :, at], mine, local)
 
     def begin(self):
         for copy in self.copies:
             copy.start()
         self.kept.start()
 
-    def arrived(self):
+    def end(self):
         self.kept.wait()
         for copy in self.copies:
-            copy.wait_recv()
-
-    def drain(self):
-        for copy in self.copies:
-            copy.wait_send()
+            copy.wait()
 
 
 class SendBack:
@@ -1331,17 +1463,16 @@
     norms,
     taps,
     rows_in,
-    head_sum,
     x_own,
     d_gate_hbm,
     d_x_hbm,
-    d_bc_hbm,
     d_arg_hbm,
     output,
     gate_back,
     out_grad,
     channel_sums,
     head_sums,
+    bc_landed,
     cot_all,
     normed_all,
     gate_all,
@@ -1350,8 +1481,8 @@
     wo,
     d_gate,
     d_x_all,
+    d_arg_all,
     d_bc,
-    d_arg_all,
     g_out,
     g_gate,
     pre_two,
@@ -1539,6 +1670,8 @@
 
     lax.fori_loop(0, width, out_block, 0)
     o_plane.begin()
+    if depth > 2:
+        out_line.phase(1)
     means[...] = norms[...] * by_column(crosses() / inner_all)
 
     def gate_block(index, carry):
@@ -1574,20 +1707,20 @@
     channel_sums[...] = jnp.zeros_like(channel_sums)
     head_sums[...] = jnp.zeros_like(head_sums)
     causal = triangles()
-    ones = causal.astype(F32)
-    before = 1.0 - ones.T
+    ones = causal.astype(BF16)
+    ones_three = jnp.concatenate([ones] * 3, axis=1)
+    after = jnp.where(triangles_up(), 1.0, 0.0).astype(BF16)
+    before = jnp.where(triangles_up(), 0.0, 1.0).astype(BF16)
+    both_ways = jnp.concatenate([after, before] * 2, axis=1)
+    of_head = head_of_channel(inner, head_size).astype(BF16)
 
     def head_totals(values):
-        return dot(values, head_sum[...], ((1,), (0,)), lax.Precision.HIGHEST)
-
-    def pump_first():
-        if depth > 2:
-            out_line.phase(1)
-
-    def pump_second():
-        o_plane.second()
-        if depth > 3:
-            out_line.phase(2)
+        high, low = in_parts(values, 2)
+        return mm(high, of_head) + mm(low, of_head)
+
+    home = lax.div(row, half) == core
+    rows_out = out_grad.shape[0]
+    far = links.copy(out_far, out_grad, peer[1])
 
     def pump_gate():
         if depth > 2:
@@ -1597,12 +1730,47 @@
         if depth > 3:
             gate_line.phase(2)
 
+    def pump_out():
+        out_line.finish(out_sum)
+        for this in range(2):
+
+            @pl.when(home & (core == this))
+            def _():
+                cast_rows(out_far, out_sum.at[pl.ds((1 - this) * rows_out, rows_out)])
+                far.start()
+                cast_rows(out_grad, out_sum.at[pl.ds(this * rows_out, rows_out)])
+
+    def pump_back():
+        gate_line.finish(gate_sum)
+        turn(gate_sent, gate_sum)
+        send_gate.begin()
+
+    quarter = everything // 4
+    bc_rows = [
+        PlaneRows(
+            links,
+            row,
+            place,
+            d_bc,
+            bc_landed,
+            pl.ds((2 * (k // 2) + 1 - k % 2) * quarter, quarter),
+            locals_.at[10 + k],
+        )
+        for k in range(4)
+    ]
+
+    def pump_out_last():
+        if depth > 3:
+            out_line.phase(2)
+
     pumps = {
-        0: pump_first,
-        2: pump_second,
-        4: pump_gate,
-        5: lambda: o_plane.finish(store_output),
-        6: pump_gate_last,
+        0: [pump_out_last],
+        1: [bc_rows[0].begin],
+        2: [pump_gate, o_plane.second],
+        3: [bc_rows[1].begin],
+        4: [pump_gate_last],
+        5: [bc_rows[2].begin, pump_out],
+        6: [lambda: o_plane.finish(store_output)],
     }
 
     def store_output(at, total):
@@ -1633,78 +1801,97 @@
         dt_block = softplus(dt_arg)
         rates = rows_in[4:5, :128]
         steps_block = dt_block * rates
-        for sub in reversed(range(subs)):
-            part = slice(sub * CHUNK, (sub + 1) * CHUNK)
-            at = pl.ds(pl.multiple_of(index * rows + sub * CHUNK, CHUNK), CHUNK)
-            x = act[part, :inner]
-            b = act[part, inner : inner + size].astype(BF16)
-            c = act[part, inner + size :].astype(BF16)
-            dt = dt_block[part]
-            cum = dot(ones, steps_block[part], ((1,), (0,)), lax.Precision.HIGHEST)
-            cum_t = cum.T
-            total = cum[CHUNK - 1 : CHUNK, :]
-            dt_wide = widen(dt, heads, head_size)
-            x_dt = x * dt_wide
-            x_dt16 = x_dt.astype(BF16)
-            d_y = d_y_all[at, :]
-            d_y16 = d_y.astype(BF16)
-            cum_wide = widen(jnp.exp(cum), heads, head_size)
-            d_read = (d_y * cum_wide).astype(BF16)
-            out_wide = widen(jnp.exp(total - cum), heads, head_size)
-            held16 = states_two[buffer, sub]
-            read = mm(c, held16) * cum_wide
-            grown = later[...]
-            grown16 = grown.astype(BF16)
-            d_x_later = out_wide * mm(b, grown16)
-            d_b = mm_t(grown16, (x_dt * out_wide).astype(BF16))
-            d_c = mm_t(held16, d_read)
-            later[...] = grown * widen(jnp.exp(total), heads, head_size) + t_mm(c, d_read)
-            cb = mm_t(c, b)
+        parts = [slice(sub * CHUNK, (sub + 1) * CHUNK) for sub in range(subs)]
+        at = pl.ds(pl.multiple_of(index * rows, rows), rows)
+        x = act[:, :inner]
+        b = act[:, inner : inner + size].astype(BF16)
+        c = act[:, inner + size :].astype(BF16)
+        cums = [
+            mm(ones_three, jnp.concatenate(in_parts(steps_block[part], 3), axis=0))
+            for part in parts
+        ]
+        lasts = [cum[CHUNK - 1 : CHUNK, :] for cum in cums]
+        dt_wide = widen(dt_block, heads, head_size)
+        cum_wide = widen(jnp.exp(jnp.concatenate(cums, axis=0)), heads, head_size)
+        out_wide = widen(
+            jnp.exp(jnp.concatenate([last - cum for last, cum in zip(lasts, cums)], axis=0)),
+            heads,
+            head_size,
+        )
+        x_dt = x * dt_wide
+        x_dt16 = x_dt.astype(BF16)
+        d_y = d_y_all[at, :]
+        d_y16 = d_y.astype(BF16)
+        d_read = (d_y * cum_wide).astype(BF16)
+        sent = (x_dt * out_wide).astype(BF16)
+        near, d_cbs = [], []
+        for sub, part in enumerate(parts):
+            cum_t = cums[sub].T
+            cb = mm_t(c[part], b[part])
             d_cb = jnp.zeros((CHUNK, CHUNK), F32)
             pieces = []
             for pair in range(heads // 2):
                 lanes = slice(2 * pair * head_size, 2 * (pair + 1) * head_size)
-                d_y_split = split_pair(d_y16[:, lanes], head_size)
+                d_y_split = split_pair(d_y16[part, lanes], head_size)
                 mixing = []
                 for k in range(2):
-                    decay = head_decays(cum, cum_t, 2 * pair + k, causal)
+                    decay = head_decays(cums[sub], cum_t, 2 * pair + k, causal)
                     mixing.append((decay * cb).astype(BF16))
-                    d_cb = d_cb + decay * mm_t(d_y_split[k], x_dt16[:, lanes])
+                    d_cb = d_cb + decay * mm_t(d_y_split[k], x_dt16[part, lanes])
                 pieces.append(
                     t_mm(jnp.concatenate(mixing, axis=0), jnp.concatenate(d_y_split, axis=0))
                 )
-            d_x_near = jnp.concatenate(pieces, axis=1)
-            d_x_dt = d_x_later + d_x_near
-            d_cb16 = d_cb.astype(BF16)
-            d_b = d_b + t_mm(c, d_cb16)
-            d_c = d_c + dot(b, d_cb16, ((0,), (1,)))
-            d_bc[:size, at] = d_b.astype(BF16)
-            d_bc[size:, at] = d_c.astype(BF16)
-            d_x = d_x_dt * dt_wide + skip * d_y
-            near = y_all[at, :] - skip * x - read
-            cross_wide = d_y * read + d_y16.astype(F32) * near - x_dt16.astype(F32) * d_x_near
-            d_dt_direct = head_totals(x * d_x_dt)
-            d_cum = head_totals(cross_wide)
-            through = head_totals(x_dt * d_x_later)
-            over = head_totals(
-                jnp.broadcast_to(
-                    jnp.sum(grown * held16.astype(F32), axis=0, keepdims=True), (8, inner)
+            near.append(jnp.concatenate(pieces, axis=1))
+            d_cbs.append(d_cb.astype(BF16))
+        later_rows, overs = [None] * subs, [None] * subs
+        for sub in reversed(range(subs)):
+            part = parts[sub]
+            held16 = states_two[buffer, sub]
+            grown = later[...]
+            grown16 = grown.astype(BF16)
+            later_rows[sub] = mm(b[part], grown16)
+            column_at = pl.ds(pl.multiple_of(index * rows + sub * CHUNK, CHUNK), CHUNK)
+            d_b = mm_t(grown16, sent[part]) + t_mm(c[part], d_cbs[sub])
+            d_c = mm_t(held16, d_read[part]) + dot(b[part], d_cbs[sub], ((0,), (1,)))
+            for first, value in ((0, d_b), (width // 2, d_c)):
+                d_bc[first : first + width // 2, :, column_at] = value.astype(BF16).reshape(
+                    width // 2, 2 * size // width, CHUNK
                 )
+            overs[sub] = jnp.sum(grown * held16.astype(F32), axis=0, keepdims=True)
+            later[...] = grown * widen(jnp.exp(lasts[sub]), heads, head_size) + t_mm(
+                c[part], d_read[part]
             )
-            d_log = (
-                dot(ones, d_cum, ((0,), (0,)), lax.Precision.HIGHEST)
-                + dot(before, through, ((1,), (0,)), lax.Precision.HIGHEST)
-                + over[0:1, :] * jnp.exp(total)
-            )
-            d_dt = d_dt_direct + rates * d_log
-            d_arg = d_dt * sigmoid(dt_arg[part])
-            d_arg_all[2 * block + sub, pl.ds(pl.multiple_of(slot * piece, piece), piece), :] = (
-                d_arg.astype(BF16)
-            )
-            head_sums[0:1, :] += jnp.sum(d_arg, axis=0, keepdims=True)
-            head_sums[1:2, :] += jnp.sum(d_log * dt, axis=0, keepdims=True) * rates
-            channel_sums[5:6, :] += jnp.sum(d_y * x, axis=0, keepdims=True)
-            d_ext[part, :] = d_x * slope[part]
+        d_x_near = jnp.concatenate(near, axis=0)
+        d_x_later = out_wide * jnp.concatenate(later_rows, axis=0)
+        d_x_dt = d_x_later + d_x_near
+        d_x = d_x_dt * dt_wide + skip * d_y
+        d_ext[0:rows, :] = d_x * slope
+        channel_sums[5:6, :] += jnp.sum(d_y * x, axis=0, keepdims=True)
+        cross_wide = d_y16.astype(F32) * (y_all[at, :] - skip * x) - x_dt16.astype(F32) * d_x_near
+        over_wide = jnp.concatenate(overs + [jnp.zeros((8 - subs, inner), F32)], axis=0)
+        d_dt_direct = mm((x * d_x_dt).astype(BF16), of_head)
+        d_cum = head_totals(cross_wide)
+        through = mm((x_dt * d_x_later).astype(BF16), of_head)
+        over = head_totals(over_wide)
+        d_log = jnp.concatenate(
+            [
+                mm(
+                    both_ways,
+                    jnp.concatenate(
+                        in_parts(jnp.concatenate([d_cum[part], through[part]], axis=0), 2), axis=0
+                    ),
+                )
+                + over[sub : sub + 1] * jnp.exp(lasts[sub])
+                for sub, part in enumerate(parts)
+            ],
+            axis=0,
+        )
+        d_arg = (d_dt_direct + rates * d_log) * sigmoid(dt_arg)
+        d_arg_all[
+            pl.ds(2 * block, 2), pl.ds(pl.multiple_of(slot * piece, piece), piece), :
+        ] = d_arg.astype(BF16).reshape(2, piece, 128)
+        head_sums[0:1, :] += jnp.sum(d_arg, axis=0, keepdims=True)
+        head_sums[1:2, :] += jnp.sum(d_log * dt_block, axis=0, keepdims=True) * rates
 
         d_conv = jnp.zeros((rows, inner), F32)
         x_in = conv_two[buffer]
@@ -1718,36 +1905,27 @@
         ] = d_conv.astype(BF16).reshape(2, piece, inner)
         d_ext[rows:, :] = d_ext[0:8, :]
 
-        for at_step, action in pumps.items():
-            pl.when(number == at_step)(action)
+        for at_step, actions in pumps.items():
+
+            @pl.when(number == at_step)
+            def _():
+                for action in actions:
+                    action()
 
         return carry
 
     lax.fori_loop(0, blocks, scan_block, 0)
+    bc_rows[3].begin()
+    pump_back()
     saves = [
         pltpu.make_async_copy(source, target, locals_.at[8 + k])
         for k, (source, target) in enumerate(
-            ((d_x_all, d_x_hbm), (d_bc, d_bc_hbm), (d_arg_all, d_arg_hbm))
+            ((d_x_all, d_x_hbm), (d_arg_all, d_arg_hbm))
         )
     ]
     for copy in saves:
         copy.start()
 
-    out_line.finish(out_sum)
-    home = lax.div(row, half) == core
-    rows_out = out_grad.shape[0]
-    far = links.copy(out_far, out_grad, peer[1])
-    for this in range(2):
-
-        @pl.when(home & (core == this))
-        def _():
-            cast_rows(out_far, out_sum.at[pl.ds((1 - this) * rows_out, rows_out)])
-            far.start()
-            cast_rows(out_grad, out_sum.at[pl.ds(this * rows_out, rows_out)])
-
-    gate_line.finish(gate_sum)
-    turn(gate_sent, gate_sum)
-    send_gate.begin()
     pl.when(jnp.logical_not(home))(far.wait_recv)
     pl.when(home)(far.wait_send)
     o_plane.drain()
@@ -1757,6 +1935,8 @@
     save_gate.wait()
     for copy in saves:
         copy.wait()
+    for rows_ in bc_rows:
+        rows_.end()
 
 
 def line_buffers(count, extent):
@@ -1785,15 +1965,16 @@
     saved = [
         ((width, rows, inner), BF16),
         ((width, rows, inner), BF16),
-        ((2 * size, tokens), BF16),
         ((width, rows, 128), BF16),
     ]
+    bc = ((width, 2 * size // width, tokens), BF16)
     kept = [
         ((rows, model), BF16),
         ((width, model // depth // width, inner), BF16),
         ((out_piece[0] // 2, model), F32),
         ((8, inner), F32),
         ((8, 128), F32),
+        bc,
     ]
     return pl.pallas_call(
         functools.partial(reverse_kernel, dims),
@@ -1805,6 +1986,7 @@
         + [pltpu.VMEM(hbm[-1].shape, BF16)]
         + [pltpu.VMEM(*s) for s in saved]
         + [
+            pltpu.VMEM(*bc),
             pltpu.VMEM((inner, model), F32),
             pltpu.VMEM((inner, model), F32),
             pltpu.VMEM((2, rows, wide), F32),
@@ -1824,9 +2006,9 @@
             pltpu.VMEM((in_piece[1], in_piece[0]), BF16),
             pltpu.VMEM((CHUNK, 128), F32),
             pltpu.VMEM((width, tokens // CHUNK, 128), F32),
-            pltpu.SemaphoreType.DMA((48,)),
-            pltpu.SemaphoreType.DMA((48,)),
-            pltpu.SemaphoreType.DMA((12,)),
+            pltpu.SemaphoreType.DMA((80,)),
+            pltpu.SemaphoreType.DMA((80,)),
+            pltpu.SemaphoreType.DMA((14,)),
             pltpu.SemaphoreType.DMA((2, 4)),
         ],
         compiler_params=pltpu.CompilerParams(
@@ -1855,30 +2037,26 @@
     dims,
     d_x_hbm,
     normed_hbm,
-    wg_hbm,
-    wx_hbm,
+    turned_hbm,
     d_gate_hbm,
     pre_hbm,
     conv_hbm,
     d_arg_hbm,
     wb_hbm,
     cot_hbm,
-    d_bc,
+    bc_landed,
     taps,
     channel_sums,
     head_sums,
-    head_sum,
     rows_in,
     x_own,
-    w_dt_all,
+    w_dt,
     gate_back,
     input_grad,
     in_grad,
     smalls,
     d_x,
     normed_all,
-    wg,
-    wx,
     d_gate,
     pre_own,
     conv_own,
@@ -1887,13 +2065,10 @@
     cot_own,
     w_turned,
     d_small,
-    small_in,
     g_x,
     g_small,
     d_parts,
-    d_extra,
     d_ext,
-    bc_landed,
     bc_sums,
     d_pair,
     d_sums,
@@ -1948,8 +2123,7 @@
             (
                 (d_x_hbm, d_x),
                 (normed_hbm, normed_all),
-                (wg_hbm, wg),
-                (wx_hbm, wx),
+                (turned_hbm, w_turned.at[pl.ds(0, 2 * inner)]),
                 (d_gate_hbm, d_gate),
                 (pre_hbm.at[:, window], pre_own),
                 (conv_hbm.at[:, window], conv_own),
@@ -1964,9 +2138,6 @@
     line_peers = [(lax.rem(row + up, depth), place) for up in range(1, depth)]
     greet([peer[mask] for mask in range(1, width)] + line_peers)
 
-    bc_rows = PlaneRows(links, row, place, d_bc, bc_landed, locals_.at[10])
-    bc_rows.begin()
-    small_rows = PlaneRows(links, row, place, d_small, small_in, locals_.at[11])
     cols = model // depth
 
     def line(own_ref, buffers):
@@ -1997,35 +2168,6 @@
     lax.fori_loop(0, inner // 128, x_grad_tile, 0)
     x_line.phase(0)
 
-    for copy in loads[2:5]:
-        copy.wait()
-
-    def turn_weights(number, carry):
-        at = pl.ds(pl.multiple_of(number * 128, 128), 128)
-        w_turned[:inner, at] = wg[at, :].T
-        w_turned[inner:, at] = wx[at, :].T
-        return carry
-
-    lax.fori_loop(0, model // 128, turn_weights, 0)
-
-    def token_grads(index):
-        both = jnp.concatenate([d_gate[index], d_x[index]], axis=1)
-        d_parts[index] = mm(both, w_turned[...]).astype(BF16)
-
-    for mask in (6, 2, 4, 0):
-        token_grads(peer[mask ^ 1][1])
-        d_plane.pair[mask].start()
-    token_grads(peer[6][1])
-    d_plane.far()
-    token_grads(peer[2][1])
-    d_plane.near(2)
-    token_grads(peer[4][1])
-    d_plane.near(4)
-    if depth > 2:
-        x_line.phase(1)
-    token_grads(place)
-    d_plane.near(0)
-
     lane = lax.broadcasted_iota(jnp.int32, (1, 128), 1)
     mine = lane < own
 
@@ -2033,9 +2175,8 @@
         return pltpu.roll(values, bc_turn, 1)
 
     own_taps = to_front(taps[:, window])
-    for copy in loads[5:8]:
+    for copy in loads[4:8]:
         copy.wait()
-    bc_rows.arrived()
     bc_sums[...] = jnp.zeros_like(bc_sums)
 
     def small_block(number, carry):
@@ -2069,16 +2210,48 @@
         return carry
 
     lax.fori_loop(0, blocks, small_block, 0)
-    small_rows.begin()
     g_small[...] = t_mm(
         d_small[...].reshape(everything, 128), normed_all[...].reshape(everything, model)
     )
     small_line.phase(0)
+    for copy in loads[2:4]:
+        copy.wait()
+
+    def turn_weights(number, carry):
+        at = pl.ds(pl.multiple_of(number * 128, 128), 128)
+        bc = to_front(wb[lax.div(place, per_block), at, :].astype(F32))
+        w_turned[2 * inner :, at] = jnp.where(mine, bc, 0.0).T.astype(BF16)
+        return carry
+
+    lax.fori_loop(0, model // 128, turn_weights, 0)
+    w_turned[2 * inner + own : 2 * inner + own + 16, :] = w_dt[0:16, :]
+
+    def token_grads(index):
+        both = jnp.concatenate([d_gate[index], d_x[index], d_small[index]], axis=1)
+        d_parts[index] = mm(both, w_turned[...]).astype(BF16)
+
+    for mask in (6, 2, 4, 0):
+        token_grads(peer[mask ^ 1][1])
+        d_plane.pair[mask].start()
+    token_grads(peer[6][1])
+    d_plane.far()
+    token_grads(peer[2][1])
+    d_plane.near(2)
+    token_grads(peer[4][1])
+    d_plane.near(4)
+    if depth > 2:
+        x_line.phase(1)
+    token_grads(place)
+    d_plane.near(0)
+
     sums_own[:, :inner] = channel_sums[...]
     sums_own[:, inner : inner + 128] = bc_sums[...]
     sums_own[:, inner + 128 :] = head_sums[...]
     sums_own[2:3, inner + 128 :] = dot(
-        channel_sums[...], head_sum[...], ((1,), (0,)), lax.Precision.HIGHEST
+        channel_sums[...],
+        head_of_channel(inner, head_size),
+        ((1,), (0,)),
+        lax.Precision.HIGHEST,
     )[5:6]
     sums_copies = [
         links.copy(sums_own, sums_line.at[k], device) for k, device in enumerate(line_peers)
@@ -2104,24 +2277,6 @@
     for copy in spread_sums:
         copy.start()
 
-    small_rows.arrived()
-    for copy in loads[8:]:
-        copy.wait()
-    bc_tiles = [jnp.zeros((rows, 128), F32)] * (2 * size // 128)
-    d_dt_all = jnp.zeros((rows, 128), F32)
-    for source in range(width):
-        got = small_in[source]
-        moved = jnp.where(mine, got.astype(F32), 0.0)
-        turn_by = own * (source % per_block)
-        if turn_by:
-            moved = pltpu.roll(moved, turn_by, 1)
-        bc_tiles[source // per_block] = bc_tiles[source // per_block] + moved
-        places = head_places(source, half, plane, group, heads, own).astype(BF16)
-        d_dt_all = d_dt_all + mm(got, places)
-    extra = mm_t(d_dt_all.astype(BF16), w_dt_all[...])
-    for k, tile in enumerate(bc_tiles):
-        extra = extra + mm_t(tile.astype(BF16), wb[k])
-    d_extra[...] = extra
     x_line.finish(x_sum)
     turn(x_sent, x_sum)
     send_x.begin()
@@ -2174,16 +2329,15 @@
         held = x_own[at].astype(F32)
         inv = lax.rsqrt(jnp.mean(held * held, axis=1, keepdims=True) + EPS)
         hat = held * inv
-        d_h = (total + d_extra[at]) * norm_gain
+        d_h = total * norm_gain
         grad = inv * (d_h - hat * jnp.mean(d_h * hat, axis=1, keepdims=True))
         input_grad[at] = (grad + cot_own[at].astype(F32)).astype(BF16)
 
+    loads[8].wait()
     d_plane.finish(store_grad)
     d_plane.drain()
     x_line.drain()
     small_line.drain()
-    bc_rows.drain()
-    small_rows.drain()
 
 
 def weights(dims, hbm, vmem, collective):
@@ -2205,22 +2359,19 @@
         out_shape=tuple(shape(*s) for s in kept),
         in_specs=[ANY] * len(hbm) + [INVMEM] * len(vmem),
         out_specs=(INVMEM,) * len(kept),
-        scratch_shapes=[pltpu.VMEM(v.shape, v.dtype) for v in hbm[:5]]
+        scratch_shapes=[pltpu.VMEM(v.shape, v.dtype) for v in (hbm[0], hbm[1], hbm[3])]
         + [
             pltpu.VMEM((tokens, 128), F32),
             pltpu.VMEM((tokens, 128), F32),
+            pltpu.VMEM(hbm[6].shape, BF16),
             pltpu.VMEM(hbm[7].shape, BF16),
-            pltpu.VMEM(hbm[8].shape, BF16),
             pltpu.VMEM((rows, model), BF16),
-            pltpu.VMEM((2 * inner, model), BF16),
-            pltpu.VMEM((width, rows, 128), BF16),
+            pltpu.VMEM((2 * inner + 128, model), BF16),
             pltpu.VMEM((width, rows, 128), BF16),
             pltpu.VMEM((inner, model), F32),
             pltpu.VMEM((128, model), F32),
             pltpu.VMEM((width, rows, model), BF16),
-            pltpu.VMEM((rows, model), F32),
             pltpu.VMEM((rows + 8, 128), F32),
-            pltpu.VMEM((width, own, tokens), BF16),
             pltpu.VMEM((8, 128), F32),
         ]
         + plane_buffers(rows, model)
@@ -2283,49 +2434,13 @@
     slot_len = piece * width
     tokens = slots * slot_len
 
-    def by_owner(values, axis):
-        shape = values.shape
-        return values.reshape(shape[:axis] + (2, half, plane, pair_rows) + shape[axis + 1 :])
-
-    gate_cols = inner_all
-    conv_cols = gate_cols + inner_all
-    bc_cols = conv_cols + 2 * size
     own_ch = conv_bias.shape[0]
-
-    def padded(values, lanes=128):
-        return jnp.pad(values, ((0, 0), (0, lanes - values.shape[1])))
-
-    def placed(values, top):
-        return jnp.pad(
-            values, ((top, 16 + in_rows - top - values.shape[0]), (0, 128 - values.shape[1]))
-        )
-
-    pack = (
-        placed(in_weight[:, bc_cols:], 0)
-        + placed(conv_weight, in_rows)
-        + placed(conv_bias[None], in_rows + taps_count)
-        + placed(gate_gain[None], in_rows + 5)
-        + placed(norm_gain[None], in_rows + 6)
-    )
-    head_params = jnp.pad(
-        jnp.stack([dt_bias, a_log, d_skip]), ((0, 5), (0, 128 - heads_all))
-    )
-    positions = place * piece + jnp.arange(piece, dtype=jnp.int32)
-    live = (positions[None, :] < lengths[:, None]).astype(BF16)
-    masked = cotangent * live[..., None]
-
-    def cols_for_all(values):
-        split = by_owner(values, 1)
-        return jnp.transpose(split, (3, 1, 0, 2, 4)).reshape(width, in_rows, inner)
-
-    w_bc_send = jnp.swapaxes(in_weight[:, conv_cols:bc_cols].reshape(in_rows, 2, size), 0, 1)
     tokens_dev = slots * piece
     dims = (depth, width, heads, head_size, size, taps_count, own_ch, inner_all)
     (
         normed_all,
         cot_all,
-        w_gate,
-        w_x,
+        w_turned,
         w_bc,
         w_out,
         conv_in,
@@ -2338,45 +2453,47 @@
         taps,
         param_rows,
         w_dt,
-        w_dt_all,
     ) = forward(
         dims,
-        block_input.reshape(tokens_dev, model),
-        masked.reshape(tokens_dev, model),
-        cols_for_all(in_weight[:, :gate_cols]),
-        cols_for_all(in_weight[:, gate_cols:conv_cols]),
-        w_bc_send,
-        out_weight,
-        pack,
-        head_params,
+        (
+            block_input.reshape(tokens_dev, model),
+            cotangent.reshape(tokens_dev, model),
+            lengths[None],
+            in_weight,
+            out_weight,
+            norm_gain[None],
+            gate_gain[None],
+            conv_weight,
+            conv_bias[None],
+            dt_bias[None],
+            a_log[None],
+            d_skip[None],
+        ),
         2,
     )
     x_own = block_input.reshape(tokens_dev, model)
-    head_sum = padded((jnp.arange(inner)[:, None] // head_size == jnp.arange(heads)).astype(F32))
     (
         d_gate,
         d_x,
-        d_bc,
         d_arg,
         output,
         gate_back,
         out_grad,
         channel_sums,
         head_sums,
+        d_bc,
     ) = reverse(
         dims,
         (cot_all, normed_all, gate, y, pre, conv_in, dt_arg, states, w_out),
-        (norms, taps, param_rows, head_sum, x_own),
+        (norms, taps, param_rows, x_own),
         3,
     )
-    bc_own = 2 * size // width
     input_grad, in_grad, smalls = weights(
         dims,
         (
             d_x,
             normed_all,
-            w_gate.reshape(model, inner),
-            w_x.reshape(model, inner),
+            w_turned,
             d_gate,
             pre,
             conv_in,
@@ -2385,14 +2502,13 @@
             cot_all,
         ),
         (
-            d_bc.reshape(width, bc_own, tokens),
+            d_bc,
             taps,
             channel_sums,
             head_sums,
-            head_sum,
             param_rows,
             x_own,
-            w_dt_all,
+            w_dt,
             gate_back,
         ),
         4,

time: 258 us -> 232 us (0.90)
  Pallas kernels: 234 us -> 220 us
  local copies, waits for them, and re-layouts: 11.9 us -> 5.27 us
  other arithmetic: 8.03 us -> 2.85 us
    pallas_call x1, Pallas kernels: 80.2 us -> 72.5 us  [reverse(): pl.pallas_call(functools.partial(reverse_kernel, dims), out_shape=tuple((...]
    pallas_call x1, Pallas kernels: 94.3 us -> 88.5 us  [forward(): pl.pallas_call(functools.partial(forward_kernel, dims), out_shape=tuple((...]
    reshape x6 -> x0, local copies, waits for them, and re-layouts: 3.45 us -> none  [the longest x2 1.88 us: cols_for_all(): return jnp.transpose(split, (3, 1, 0, 2, 4)).reshape(width, in_rows, inner)]
where the time goes in v4:
time: 232 us; the launch traced here: 229 us
  Pallas kernels  220 us (95%)
  local copies, waits for them, and re-layouts  5.27 us (2%)
  other arithmetic  2.85 us (1%)
    pallas_call x1, Pallas kernels, forward(): pl.pallas_call(functools.partial(forward_kernel, dims), out_shape=tuple((...  88.5 us
    pallas_call x1, Pallas kernels, reverse(): pl.pallas_call(functools.partial(reverse_kernel, dims), out_shape=tuple((...  72.5 us
    pallas_call x1, Pallas kernels, weights(): pl.pallas_call(functools.partial(weights_kernel, dims), out_shape=tuple((...  59.4 us

profile of v4, /device:TPU:9, one launch (start us, length us, event | category | flops | bytes accessed | tf_op | source)
XLA Modules:
  0.0 229.3 jit_solution(9295858249464492364)
XLA Ops:
  0.6 88.5 %forward_fused.1 = (bf16[8,256,1536]{2,1,0:T(8,128)(2,1)}, bf16[8,256,1536]{2,1,0:T(8,128)(2,1)}, bf16[768,1536]{1,0:T(8,128)(2,1)}, bf16[2,4,8,48,128]{4,3,2,1,...) custom-call(bf16[256,1536]{1,0:T(8,128)(2,1)} %bitcast.20, ...), custom_call_target="tpu_custom_call" | custom-call | tf_op jit(solution)/shard_map/forward_fused/pallas_call | solution.py:1365
  89.2 72.5 %reverse_fused.1 = (bf16[8,256,384]{2,1,0:T(8,128)(2,1)}, bf16[8,256,384]{2,1,0:T(8,128)(2,1)}, bf16[8,256,128]{2,1,0:T(8,128)(2,1)}, bf16[256,1536]{1,0:T(8,128...) custom-call(bf16[8,256,1536]{2,1,0:T(8,128)(2,1)} %get-tuple-element, ...), custom_call_target="tpu_custom_call" | custom-call | tf_op jit(solution)/shard_map/reverse_fused/pallas_call | solution.py:1979
  161.7 0.0 copy-start.1
  161.7 59.4 %weights_fused.1 = (bf16[256,1536]{1,0:T(8,128)(2,1)}, f32[48,6448]{1,0:T(8,128)}, f32[16,128]{1,0:T(8,128)}) custom-call(bf16[8,256,384]{2,1,0:T(8,128)(2,1)} %get-tuple-element.51.d_x_hbm, bf16[8,256,1536]{2,1,0:T(8,128)(2,1)} %get-tuple-element.39.normed_hbm, bf16[768,1536]{1,0:T(8,128)(2,1)} %get-tuple-element.52.turned_hbm, ...), custom_call_target="tpu_custom_call" | custom-call | tf_op jit(solution)/shard_map/weights_fused/pallas_call | solution.py:2357
  221.1 0.0 copy-start.7
  221.1 0.0 copy-start.6
  221.1 0.0 copy-start.2
  221.2 0.0 copy-start.3
  221.2 0.0 copy-start.8
  221.2 0.0 copy-start.4
  221.2 0.0 copy-done.1
  221.2 1.6 multiply_reduce_fusion
  222.8 0.0 copy-done.7
  222.8 0.0 copy-start.5
  222.9 0.5 convert_divide_fusion.1
  223.4 0.0 copy-done.6
  223.4 0.5 slice_bitcast_fusion.3
  223.9 0.0 copy-done.2
  223.9 0.0 copy-done.3
  223.9 0.2 multiply_reduce_fusion.1
  224.1 0.0 copy-done.8
  224.1 0.5 convert_divide_fusion
  224.6 0.5 slice_bitcast_fusion
  225.1 0.6 slice.15
  225.7 0.0 copy-done.4
  225.7 0.0 copy-start
  225.7 0.9 copy.27
  226.6 0.0 copy-done.5
  226.6 0.9 copy.28
  227.5 0.0 copy-done
  227.5 1.0 copy.29
  228.5 0.8 copy.30
Async XLA Ops:
  161.7 59.5 %copy-start.1 = (bf16[48,6448]{1,0:T(8,128)(2,1)S(1)}, bf16[48,6448]{1,0:T(8,128)(2,1)}, u32[]{:S(2)}) copy-start(bf16[48,6448]{1,0:T(8,128)(2,1)} %in_weight.1) | copy-start | bytes 1857028
  221.1 1.7 copy-start.7
  221.1 2.2 copy-start.6
  221.1 2.8 %copy-start.2 = (f32[96,1536]{1,0:T(8,128)S(1)}, f32[96,1536]{1,0:T(8,128)}, u32[]{:S(2)}) copy-start(f32[96,1536]{1,0:T(8,128)} %get-tuple-element.82) | copy-start | bytes 1769476
  221.2 2.7 %copy-start.3 = (bf16[96,1536]{1,0:T(8,128)(2,1)S(1)}, bf16[96,1536]{1,0:T(8,128)(2,1)}, u32[]{:S(2)}) copy-start(bf16[96,1536]{1,0:T(8,128)(2,1)} %wo_own.1) | copy-start | bytes 884740
  221.2 2.9 %copy-start.8 = (bf16[96]{0:T(256)(128)(2,1)S(1)}, bf16[96]{0:T(256)(128)(2,1)}, u32[]{:S(2)}) copy-start(bf16[96]{0:T(256)(128)(2,1)} %param.18) | copy-start | bytes 580
  221.2 4.5 %copy-start.4 = (bf16[256,1536]{1,0:T(8,128)(2,1)S(1)}, bf16[256,1536]{1,0:T(8,128)(2,1)}, u32[]{:S(2)}) copy-start(bf16[256,1536]{1,0:T(8,128)(2,1)} %get-tuple-element.50) | copy-start | bytes 2359300
  222.8 3.7 %copy-start.5 = (bf16[256,1536]{1,0:T(8,128)(2,1)S(1)}, bf16[256,1536]{1,0:T(8,128)(2,1)}, u32[]{:S(2)}) copy-start(bf16[256,1536]{1,0:T(8,128)(2,1)} %get-tuple-element.61) | copy-start | bytes 2359300
  225.7 1.8 copy-start

commit v5 on v4

--- a/solution.py
+++ b/solution.py
@@ -757,10 +757,11 @@
 
 
 class Pass:
-    def __init__(self, links, peer, place, own, everyone):
+    def __init__(self, links, peer, place, own, everyone, at):
+        own = own.at[at]
         rows = own.shape[0] // 2
-        mine = everyone.at[place]
-        from2, from4, far = (everyone.at[peer[mask][1]] for mask in (2, 4, 6))
+        mine = everyone.at[place, at]
+        from2, from4, far = (everyone.at[peer[mask][1], at] for mask in (2, 4, 6))
         top, low = pl.ds(0, rows), pl.ds(rows, rows)
         self.kept = None
         self.to2 = links.copy(own, mine, peer[2])
@@ -959,9 +960,10 @@
         copy.start()
     pl.when(out_home)(out_kept.start)
     pl.when(jnp.logical_not(out_home))(out_pair.start)
-    x_pass = Pass(links, peer, place, x_own, x_all)
-    cot_pass = Pass(links, peer, place, cot_own, cot_all)
-    x_pass.first()
+    slot_rows = [pl.ds(slot * piece, piece) for slot in range(slots)]
+    x_passes = [Pass(links, peer, place, x_own, x_all, at) for at in slot_rows]
+    cot_passes = [Pass(links, peer, place, cot_own, cot_all, at) for at in slot_rows]
+    x_passes[0].first()
 
     dt_own[...] = jnp.zeros_like(dt_own)
     last = in_weight.shape[1]
@@ -1001,7 +1003,10 @@
         lambda shard: [wo.at[lax.rem(shard, half)]],
         lambda shard: lax.div(shard, half) == core,
     )
-    x_line = Line(links, depth, row, place, lambda shard: [wx.at[shard]])
+    x_lines = [
+        Line(links, depth, row, place, lambda shard, k=k: [wx.at[shard, pl.ds(k, width // 2)]])
+        for k in (0, width // 2)
+    ]
     gate_line = Line(links, depth, row, place, lambda shard: [wg.at[shard]])
 
     pl.when(out_home)(out_kept.wait)
@@ -1010,9 +1015,9 @@
     kept[0].wait()
     for copy in plane_x:
         copy.wait_recv()
-    x_line.send(0)
-    for copy in plane_g:
-        copy.start()
+    for line in x_lines:
+        line.send(0)
+    x_passes[1].first()
     kept[5].wait()
     for copy in pack_line:
         copy.wait_recv()
@@ -1031,11 +1036,33 @@
     ]
     for copy in pack_plane:
         copy.start()
-    x_pass.relay()
-    cot_pass.first()
-    x_line.wait(0)
-    if depth > 2:
-        x_line.send(1)
+    x_passes[0].relay()
+    for copy in plane_g:
+        copy.start()
+    for line in x_lines:
+        line.wait(0)
+        if depth > 2:
+            line.send(1)
+    x_passes[0].last()
+    x_passes[1].relay()
+    cot_passes[0].first()
+
+    def normalise(index, carry):
+        for part in range(2):
+            held = x_all[index, part * piece : (part + 1) * piece, :].astype(F32)
+            inv = lax.rsqrt(jnp.mean(held * held, axis=1, keepdims=True) + EPS)
+            normed_all[index, part * piece : (part + 1) * piece, :] = (
+                held * inv * rows_out[0:1, :]
+            ).astype(BF16)
+        return carry
+
+    for line in x_lines:
+        if depth > 2:
+            line.wait(1)
+        if depth > 3:
+            line.send(2)
+    x_passes[1].last()
+    cot_passes[1].first()
     kept[1].wait()
     for copy in pack_plane:
         copy.wait_recv()
@@ -1081,32 +1108,21 @@
     rows_out[3:4, :128] = chosen[0:1]
     rows_out[4:5, :128] = rates
 
-    x_pass.last()
-
-    def normalise(index, carry):
-        for part in range(2):
-            held = x_all[index, part * piece : (part + 1) * piece, :].astype(F32)
-            inv = lax.rsqrt(jnp.mean(held * held, axis=1, keepdims=True) + EPS)
-            normed_all[index, part * piece : (part + 1) * piece, :] = (
-                held * inv * rows_out[0:1, :]
-            ).astype(BF16)
-        return carry
-
-    x_line.wait(1) if depth > 2 else None
-    if depth > 3:
-        x_line.send(2)
     for copy in plane_g:
         copy.wait_recv()
     kept[2].wait()
-    x_pass.end()
-    kept[3].wait()
-    lax.fori_loop(0, width, normalise, 0)
     if depth > 3:
-        x_line.wait(2)
+        x_lines[0].wait(2)
     gate_line.send(0)
+    if depth > 3:
+        x_lines[1].wait(2)
     near_bc = wx.at[:, :, :, pl.ds(inner, size)]
     pair_bc = links.copy(near_bc, wb_far, peer[1])
     pair_bc.start()
+    for each in x_passes:
+        each.end()
+    kept[3].wait()
+    lax.fori_loop(0, width, normalise, 0)
     saves = [pltpu.make_async_copy(normed_all, normed_out, locals_.at[7])]
     saves[0].start()
     pair_bc.wait_recv()
@@ -1222,34 +1238,30 @@
         @pl.when(index == 1)
         def _():
             gate_line.wait(0)
-            if depth > 2:
-                gate_line.send(1)
+            gate_line.send(1) if depth > 2 else None
+            out_line.wait(0)
+            out_line.send(1) if depth > 2 else None
 
         @pl.when(index == 2)
         def _():
-            cot_pass.relay()
-
-        if depth > 2:
-
-            @pl.when(index == 4)
-            def _():
-                gate_line.wait(1)
-                if depth > 3:
-                    gate_line.send(2)
+            cot_passes[0].relay()
+            cot_passes[1].relay()
+
+        @pl.when(index == 4)
+        def _():
+            gate_line.wait(1) if depth > 2 else None
+            gate_line.send(2) if depth > 3 else None
+            out_line.wait(1) if depth > 2 else None
+            out_line.send(2) if depth > 3 else None
 
         @pl.when(index == 5)
         def _():
-            cot_pass.last()
-            out_line.wait(0)
-            if depth <= 3 and depth > 2:
-                out_line.send(1)
-
-        if depth > 3:
-
-            @pl.when(index == 6)
-            def _():
-                gate_line.wait(2)
-                out_line.send(1)
+            cot_passes[0].last()
+            cot_passes[1].last()
+
+        @pl.when(index == 6)
+        def _():
+            gate_line.wait(2) if depth > 3 else None
 
         return carry
 
@@ -1271,14 +1283,6 @@
             part = gated[sub * CHUNK : (sub + 1) * CHUNK]
             total = jnp.sum(part * part, axis=1, keepdims=True)
             sums[...] = jnp.where(chunk_lane == index * (rows // CHUNK) + sub, total, sums[...])
-        if depth > 2:
-
-            @pl.when(index == blocks // 2)
-            def _():
-                out_line.wait(1)
-                if depth > 3:
-                    out_line.send(2)
-
         return carry
 
     lax.fori_loop(0, blocks, gate_block, 0)
@@ -1302,10 +1306,14 @@
     ]
     for copy in save_weights[:3]:
         copy.start()
-    cot_pass.end()
     kept[4].wait()
-    save_cot = pltpu.make_async_copy(cot_all, cot_out, locals_.at[9])
-    save_cot.start()
+    save_cot = [
+        pltpu.make_async_copy(cot_all.at[:, at], cot_out.at[:, at], locals_.at[9 + 5 * k])
+        for k, at in enumerate(slot_rows)
+    ]
+    for each, copy in zip(cot_passes, save_cot):
+        each.end()
+        copy.start()
     if depth > 3:
         out_line.wait(2)
     save_weights[3].start()
@@ -1316,11 +1324,11 @@
         for copy in copies:
             copy.wait_send()
     pl.when(jnp.logical_not(out_home))(out_pair.wait_send)
-    for line in (out_line, x_line, gate_line):
+    for line in [out_line, gate_line] + x_lines:
         line.drain()
-    x_pass.drain()
-    cot_pass.drain()
-    for copy in saves + [save_gate, save_cot] + save_weights:
+    for each in x_passes + cot_passes:
+        each.drain()
+    for copy in saves + [save_gate] + save_cot + save_weights:
         copy.wait()
 
     def stores_end(index, carry):
@@ -1389,8 +1397,8 @@
             pltpu.VMEM((depth, in_rows, 128), BF16),
             pltpu.VMEM((width, 16, 256), BF16),
             pltpu.VMEM((8, 128), F32),
-            pltpu.SemaphoreType.DMA((112,)),
-            pltpu.SemaphoreType.DMA((112,)),
+            pltpu.SemaphoreType.DMA((160,)),
+            pltpu.SemaphoreType.DMA((160,)),
             pltpu.SemaphoreType.DMA((16,)),
             pltpu.SemaphoreType.DMA((5, tokens // rows)),
         ],
@@ -1664,12 +1672,24 @@
     lax.fori_loop(0, blocks, cot_block, 0)
     crosses = plane_total(links, means, sums_in, peer, 2 * blocks)
 
-    def out_block(index, carry):
+    def out_block(index):
         cot_all[index] = mm(d_gate[index], wo[...].reshape(inner, model)).astype(BF16)
-        return carry
-
-    lax.fori_loop(0, width, out_block, 0)
-    o_plane.begin()
+
+    def for_pair(mask):
+        out_block(peer[mask ^ 1][1])
+        o_plane.pair[mask].start()
+
+    for_pair(6)
+    out_block(peer[6][1])
+    for_pair(2)
+    out_block(peer[2][1])
+    o_plane.far()
+    for_pair(4)
+    out_block(peer[4][1])
+    o_plane.near(2)
+    for_pair(0)
+    out_block(place)
+    o_plane.near(4)
     if depth > 2:
         out_line.phase(1)
     means[...] = norms[...] * by_column(crosses() / inner_all)
@@ -1702,7 +1722,7 @@
     loads[4].wait()
     lax.fori_loop(0, inner // 128, gate_grad_tile, 0)
     gate_line.phase(0)
-    o_plane.first()
+    o_plane.near(0)
 
     channel_sums[...] = jnp.zeros_like(channel_sums)
     head_sums[...] = jnp.zeros_like(head_sums)
@@ -1764,13 +1784,13 @@
             out_line.phase(2)
 
     pumps = {
-        0: [pump_out_last],
+        0: [o_plane.second, pump_out_last],
         1: [bc_rows[0].begin],
-        2: [pump_gate, o_plane.second],
-        3: [bc_rows[1].begin],
+        2: [pump_gate],
+        3: [bc_rows[1].begin, pump_out],
         4: [pump_gate_last],
-        5: [bc_rows[2].begin, pump_out],
-        6: [lambda: o_plane.finish(store_output)],
+        5: [bc_rows[2].begin, lambda: o_plane.finish(store_output)],
+        7: [pump_back],
     }
 
     def store_output(at, total):
@@ -1916,7 +1936,6 @@
 
     lax.fori_loop(0, blocks, scan_block, 0)
     bc_rows[3].begin()
-    pump_back()
     saves = [
         pltpu.make_async_copy(source, target, locals_.at[8 + k])
         for k, (source, target) in enumerate(
@@ -2230,17 +2249,22 @@
         both = jnp.concatenate([d_gate[index], d_x[index], d_small[index]], axis=1)
         d_parts[index] = mm(both, w_turned[...]).astype(BF16)
 
-    for mask in (6, 2, 4, 0):
+    def for_pair(mask):
         token_grads(peer[mask ^ 1][1])
         d_plane.pair[mask].start()
+
+    for_pair(6)
     token_grads(peer[6][1])
+    for_pair(2)
     d_plane.far()
     token_grads(peer[2][1])
+    for_pair(4)
     d_plane.near(2)
-    token_grads(peer[4][1])
-    d_plane.near(4)
     if depth > 2:
         x_line.phase(1)
+    token_grads(peer[4][1])
+    for_pair(0)
+    d_plane.near(4)
     token_grads(place)
     d_plane.near(0)
 

time: 232 us -> 225 us (0.970); the launches traced: 229 us -> 225 us
  Pallas kernels: 220 us -> 216 us
    pallas_call x1, Pallas kernels: 59.4 us -> 55.1 us  [weights(): pl.pallas_call(functools.partial(weights_kernel, dims), out_shape=tuple((...]
where the time goes in v5:
time: 225 us
  Pallas kernels  216 us (96%)
  local copies, waits for them, and re-layouts  5.27 us (2%)
  other arithmetic  2.85 us (1%)
    pallas_call x1, Pallas kernels, forward(): pl.pallas_call(functools.partial(forward_kernel, dims), out_shape=tuple((...  88.8 us
    pallas_call x1, Pallas kernels, reverse(): pl.pallas_call(functools.partial(reverse_kernel, dims), out_shape=tuple((...  72.4 us
    pallas_call x1, Pallas kernels, weights(): pl.pallas_call(functools.partial(weights_kernel, dims), out_shape=tuple((...  55.1 us

profile of v5, /device:TPU:9, one launch (start us, length us, event | category | flops | bytes accessed | tf_op | source)
XLA Modules:
  0.0 225.2 jit_solution(12381904469753915625)
XLA Ops:
  0.6 88.8 %forward_fused.1 = (bf16[8,256,1536]{2,1,0:T(8,128)(2,1)}, bf16[8,256,1536]{2,1,0:T(8,128)(2,1)}, bf16[768,1536]{1,0:T(8,128)(2,1)}, bf16[2,4,8,48,128]{4,3,2,1,...) custom-call(bf16[256,1536]{1,0:T(8,128)(2,1)} %bitcast.20, ...), custom_call_target="tpu_custom_call" | custom-call | tf_op jit(solution)/shard_map/forward_fused/pallas_call | solution.py:1373
  89.4 72.4 %reverse_fused.1 = (bf16[8,256,384]{2,1,0:T(8,128)(2,1)}, bf16[8,256,384]{2,1,0:T(8,128)(2,1)}, bf16[8,256,128]{2,1,0:T(8,128)(2,1)}, bf16[256,1536]{1,0:T(8,128...) custom-call(bf16[8,256,1536]{2,1,0:T(8,128)(2,1)} %get-tuple-element, ...), custom_call_target="tpu_custom_call" | custom-call | tf_op jit(solution)/shard_map/reverse_fused/pallas_call | solution.py:1998
  161.8 0.0 copy-start.1
  161.8 55.1 %weights_fused.1 = (bf16[256,1536]{1,0:T(8,128)(2,1)}, f32[48,6448]{1,0:T(8,128)}, f32[16,128]{1,0:T(8,128)}) custom-call(bf16[8,256,384]{2,1,0:T(8,128)(2,1)} %get-tuple-element.51.d_x_hbm, bf16[8,256,1536]{2,1,0:T(8,128)(2,1)} %get-tuple-element.39.normed_hbm, bf16[768,1536]{1,0:T(8,128)(2,1)} %get-tuple-element.52.turned_hbm, ...), custom_call_target="tpu_custom_call" | custom-call | tf_op jit(solution)/shard_map/weights_fused/pallas_call | solution.py:2381
  217.0 0.0 copy-start.7
  217.0 0.0 copy-start.6
  217.0 0.0 copy-start.2
  217.0 0.0 copy-start.3
  217.0 0.0 copy-start.8
  217.0 0.0 copy-start.4
  217.0 0.0 copy-done.1
  217.0 1.6 multiply_reduce_fusion
  218.7 0.0 copy-done.7
  218.7 0.0 copy-start.5
  218.7 0.5 convert_divide_fusion.1
  219.2 0.0 copy-done.6
  219.2 0.5 slice_bitcast_fusion.3
  219.7 0.0 copy-done.2
  219.7 0.0 copy-done.3
  219.7 0.2 multiply_reduce_fusion.1
  219.9 0.0 copy-done.8
  219.9 0.5 convert_divide_fusion
  220.4 0.5 slice_bitcast_fusion
  220.9 0.6 slice.15
  221.5 0.0 copy-done.4
  221.5 0.0 copy-start
  221.5 0.9 copy.27
  222.4 0.0 copy-done.5
  222.4 0.9 copy.28
  223.3 0.0 copy-done
  223.3 1.0 copy.29
  224.3 0.8 copy.30
Async XLA Ops:
  161.8 55.2 %copy-start.1 = (bf16[48,6448]{1,0:T(8,128)(2,1)S(1)}, bf16[48,6448]{1,0:T(8,128)(2,1)}, u32[]{:S(2)}) copy-start(bf16[48,6448]{1,0:T(8,128)(2,1)} %in_weight.1) | copy-start | bytes 1857028
  217.0 1.7 copy-start.7
  217.0 2.2 copy-start.6
  217.0 2.8 %copy-start.2 = (f32[96,1536]{1,0:T(8,128)S(1)}, f32[96,1536]{1,0:T(8,128)}, u32[]{:S(2)}) copy-start(f32[96,1536]{1,0:T(8,128)} %get-tuple-element.82) | copy-start | bytes 1769476
  217.0 2.7 %copy-start.3 = (bf16[96,1536]{1,0:T(8,128)(2,1)S(1)}, bf16[96,1536]{1,0:T(8,128)(2,1)}, u32[]{:S(2)}) copy-start(bf16[96,1536]{1,0:T(8,128)(2,1)} %wo_own.1) | copy-start | bytes 884740
  217.0 2.9 %copy-start.8 = (bf16[96]{0:T(256)(128)(2,1)S(1)}, bf16[96]{0:T(256)(128)(2,1)}, u32[]{:S(2)}) copy-start(bf16[96]{0:T(256)(128)(2,1)} %param.18) | copy-start | bytes 580
  217.0 4.5 %copy-start.4 = (bf16[256,1536]{1,0:T(8,128)(2,1)S(1)}, bf16[256,1536]{1,0:T(8,128)(2,1)}, u32[]{:S(2)}) copy-start(bf16[256,1536]{1,0:T(8,128)(2,1)} %get-tuple-element.50) | copy-start | bytes 2359300
  218.7 3.7 %copy-start.5 = (bf16[256,1536]{1,0:T(8,128)(2,1)S(1)}, bf16[256,1536]{1,0:T(8,128)(2,1)}, u32[]{:S(2)}) copy-start(bf16[256,1536]{1,0:T(8,128)(2,1)} %get-tuple-element.61) | copy-start | bytes 2359300
  221.5 1.8 copy-start

commit v6 on v5

--- a/solution.py
+++ b/solution.py
@@ -1773,10 +1773,18 @@
             place,
             d_bc,
             bc_landed,
-            pl.ds((2 * (k // 2) + 1 - k % 2) * quarter, quarter),
+            pl.ds(first, count),
             locals_.at[10 + k],
         )
-        for k in range(4)
+        for k, (first, count) in enumerate(
+            (
+                (quarter, quarter),
+                (0, quarter),
+                (3 * quarter, quarter),
+                (2 * quarter + quarter // 2, quarter // 2),
+                (2 * quarter, quarter // 2),
+            )
+        )
     ]
 
     def pump_out_last():
@@ -1790,6 +1798,7 @@
         3: [bc_rows[1].begin, pump_out],
         4: [pump_gate_last],
         5: [bc_rows[2].begin, lambda: o_plane.finish(store_output)],
+        6: [bc_rows[3].begin],
         7: [pump_back],
     }
 
@@ -1935,7 +1944,7 @@
         return carry
 
     lax.fori_loop(0, blocks, scan_block, 0)
-    bc_rows[3].begin()
+    bc_rows[4].begin()
     saves = [
         pltpu.make_async_copy(source, target, locals_.at[8 + k])
         for k, (source, target) in enumerate(
@@ -2027,7 +2036,7 @@
             pltpu.VMEM((width, tokens // CHUNK, 128), F32),
             pltpu.SemaphoreType.DMA((80,)),
             pltpu.SemaphoreType.DMA((80,)),
-            pltpu.SemaphoreType.DMA((14,)),
+            pltpu.SemaphoreType.DMA((15,)),
             pltpu.SemaphoreType.DMA((2, 4)),
         ],
         compiler_params=pltpu.CompilerParams(
@@ -2282,9 +2291,9 @@
     ]
     for copy in sums_copies:
         copy.start()
-    d_plane.second()
     if depth > 3:
         x_line.phase(2)
+    d_plane.second()
     if depth > 2:
         small_line.phase(1)
     for copy in sums_copies:

time: 225 us -> 225 us (level)
  no operation moved by 1% of the time
where the time goes in v6:
time: 225 us
  Pallas kernels  216 us (96%)
  local copies, waits for them, and re-layouts  5.27 us (2%)
  other arithmetic  2.85 us (1%)
    pallas_call x1, Pallas kernels, forward(): pl.pallas_call(functools.partial(forward_kernel, dims), out_shape=tuple((...  88.8 us
    pallas_call x1, Pallas kernels, reverse(): pl.pallas_call(functools.partial(reverse_kernel, dims), out_shape=tuple((...  71.9 us
    pallas_call x1, Pallas kernels, weights(): pl.pallas_call(functools.partial(weights_kernel, dims), out_shape=tuple((...  55.1 us

profile of v6, /device:TPU:9, one launch (start us, length us, event | category | flops | bytes accessed | tf_op | source)
XLA Modules:
  0.0 224.7 jit_solution(13858035555988273984)
XLA Ops:
  0.6 88.8 %forward_fused.1 = (bf16[8,256,1536]{2,1,0:T(8,128)(2,1)}, bf16[8,256,1536]{2,1,0:T(8,128)(2,1)}, bf16[768,1536]{1,0:T(8,128)(2,1)}, bf16[2,4,8,48,128]{4,3,2,1,...) custom-call(bf16[256,1536]{1,0:T(8,128)(2,1)} %bitcast.20, ...), custom_call_target="tpu_custom_call" | custom-call | tf_op jit(solution)/shard_map/forward_fused/pallas_call | solution.py:1373
  89.4 71.9 %reverse_fused.1 = (bf16[8,256,384]{2,1,0:T(8,128)(2,1)}, bf16[8,256,384]{2,1,0:T(8,128)(2,1)}, bf16[8,256,128]{2,1,0:T(8,128)(2,1)}, bf16[256,1536]{1,0:T(8,128...) custom-call(bf16[8,256,1536]{2,1,0:T(8,128)(2,1)} %get-tuple-element, ...), custom_call_target="tpu_custom_call" | custom-call | tf_op jit(solution)/shard_map/reverse_fused/pallas_call | solution.py:2007
  161.3 0.0 copy-start.1
  161.3 55.1 %weights_fused.1 = (bf16[256,1536]{1,0:T(8,128)(2,1)}, f32[48,6448]{1,0:T(8,128)}, f32[16,128]{1,0:T(8,128)}) custom-call(bf16[8,256,384]{2,1,0:T(8,128)(2,1)} %get-tuple-element.51.d_x_hbm, bf16[8,256,1536]{2,1,0:T(8,128)(2,1)} %get-tuple-element.39.normed_hbm, bf16[768,1536]{1,0:T(8,128)(2,1)} %get-tuple-element.52.turned_hbm, ...), custom_call_target="tpu_custom_call" | custom-call | tf_op jit(solution)/shard_map/weights_fused/pallas_call | solution.py:2390
  216.5 0.0 copy-start.7
  216.5 0.0 copy-start.6
  216.5 0.0 copy-start.2
  216.5 0.0 copy-start.3
  216.5 0.0 copy-start.8
  216.5 0.0 copy-start.4
  216.5 0.0 copy-done.1
  216.5 1.6 multiply_reduce_fusion
  218.2 0.0 copy-done.7
  218.2 0.0 copy-start.5
  218.2 0.5 convert_divide_fusion.1
  218.7 0.0 copy-done.6
  218.7 0.5 slice_bitcast_fusion.3
  219.2 0.0 copy-done.2
  219.2 0.0 copy-done.3
  219.2 0.2 multiply_reduce_fusion.1
  219.4 0.0 copy-done.8
  219.4 0.5 convert_divide_fusion
  219.9 0.5 slice_bitcast_fusion
  220.5 0.6 slice.15
  221.0 0.0 copy-done.4
  221.0 0.0 copy-start
  221.0 0.9 copy.27
  221.9 0.0 copy-done.5
  221.9 0.9 copy.28
  222.8 0.0 copy-done
  222.8 1.0 copy.29
  223.9 0.8 copy.30
Async XLA Ops:
  161.3 55.2 %copy-start.1 = (bf16[48,6448]{1,0:T(8,128)(2,1)S(1)}, bf16[48,6448]{1,0:T(8,128)(2,1)}, u32[]{:S(2)}) copy-start(bf16[48,6448]{1,0:T(8,128)(2,1)} %in_weight.1) | copy-start | bytes 1857028
  216.5 1.7 copy-start.7
  216.5 2.2 %copy-start.6 = (f32[16,128]{1,0:T(8,128)S(1)}, f32[16,128]{1,0:T(8,128)}, u32[]{:S(2)}) copy-start(f32[16,128]{1,0:T(8,128)} %get-tuple-element.64) | copy-start | bytes 24580
  216.5 2.8 %copy-start.2 = (f32[96,1536]{1,0:T(8,128)S(1)}, f32[96,1536]{1,0:T(8,128)}, u32[]{:S(2)}) copy-start(f32[96,1536]{1,0:T(8,128)} %get-tuple-element.82) | copy-start | bytes 1769476
  216.5 2.7 %copy-start.3 = (bf16[96,1536]{1,0:T(8,128)(2,1)S(1)}, bf16[96,1536]{1,0:T(8,128)(2,1)}, u32[]{:S(2)}) copy-start(bf16[96,1536]{1,0:T(8,128)(2,1)} %wo_own.1) | copy-start | bytes 884740
  216.5 2.9 %copy-start.8 = (bf16[96]{0:T(256)(128)(2,1)S(1)}, bf16[96]{0:T(256)(128)(2,1)}, u32[]{:S(2)}) copy-start(bf16[96]{0:T(256)(128)(2,1)} %param.18) | copy-start | bytes 580
  216.5 4.5 %copy-start.4 = (bf16[256,1536]{1,0:T(8,128)(2,1)S(1)}, bf16[256,1536]{1,0:T(8,128)(2,1)}, u32[]{:S(2)}) copy-start(bf16[256,1536]{1,0:T(8,128)(2,1)} %get-tuple-element.50) | copy-start | bytes 2359300
  218.2 3.7 %copy-start.5 = (bf16[256,1536]{1,0:T(8,128)(2,1)S(1)}, bf16[256,1536]{1,0:T(8,128)(2,1)}, u32[]{:S(2)}) copy-start(bf16[256,1536]{1,0:T(8,128)(2,1)} %get-tuple-element.61) | copy-start | bytes 2359300
  221.0 1.8 copy-start
